TPU v7x, 128 devices: a whole 4x4x4 slice. The times are simulated.
128 devices in a mesh: img: 16 (over y_hi, x, core), phr: 8 (over y_lo, z).
Axes of the slice: x: 4, y: 4 (y_hi: 2, y_lo: 2; y = y_hi * 2 + y_lo), z: 4, core: 2. Of those that a mesh axis runs over, the one named last changes fastest.
Arguments:
- regions: bfloat16 [16384, 1024], P('img'), may hold values from -3 to 3
- phrases: bfloat16 [32768, 1024], P('phr'), may hold values from -6 to 6
- positive: int32 [16384], P('img'), may hold values from 0 to 32767
- valid: int32 [512, 32], P('img'), may hold values 0 or 1
Outputs:
- grad_regions: bfloat16 [16384, 1024], P('img', 'phr')
- grad_phrases: bfloat16 [32768, 1024], P(('phr', 'img'))
All inputs are finite; a program needn't handle non-finite values. No bound on the sum of `valid` on one device may be relied on, other than what follows from the above.
Results may differ from a plain program's by a relative error of at most 0.0034.
Values may be sent and summed in bfloat16 or wider, within the bound.
No kernel may reach another device: no remote copies, remote signals or barrier semaphores. Data moves between devices by JAX's collectives and lax.ppermute only.
A program may use at most 128 MiB of HBM per device.

v0:
```python
import jax
import jax.numpy as jnp
from jax import lax
from jax.sharding import PartitionSpec as P

logit_scale = 2.0


def joined(part, axis, combine):
    gathered = jax.tree.map(lambda a: lax.all_gather(a, axis), part)

    def take(source):
        return jax.tree.map(lambda a: lax.dynamic_index_in_dim(a, source, 0, False), gathered)

    return lax.fori_loop(
        1, lax.axis_size(axis), lambda source, state: combine(state, take(source)), take(0)
    )


def combine_totals(first, second):
    top = jnp.maximum(first[0], second[0])
    total = first[1] * jnp.exp(first[0] - top) + second[1] * jnp.exp(second[0] - top)
    return (top, total)


def per_device(regions, phrases, positive, valid):
    pdev = phrases.shape[0]
    offset = lax.axis_index("phr") * pdev
    weight = valid.reshape(-1).astype(jnp.float32)
    scores = logit_scale * lax.dot_general(
        regions, phrases, (((1,), (1,)), ((), ())), preferred_element_type=jnp.float32
    )
    columns = offset + jnp.arange(pdev, dtype=jnp.int32)
    hits = (positive[:, None] == columns[None, :]).astype(jnp.float32)
    top = jnp.max(scores, axis=1)
    total = jnp.sum(jnp.exp(scores - top[:, None]), axis=1)
    top, total = joined((top, total), "phr", combine_totals)
    lse = top + jnp.log(total)
    coeff = (weight[:, None] * (jnp.exp(scores - lse[:, None]) - hits)).astype(jnp.bfloat16)
    partial_rows = logit_scale * jnp.dot(coeff, phrases, preferred_element_type=jnp.float32)
    grad_regions = lax.psum_scatter(partial_rows, "phr", scatter_dimension=1, tiled=True).astype(
        jnp.bfloat16
    )
    grad_phrases = lax.psum_scatter(
        logit_scale
        * lax.dot_general(
            coeff, regions, (((0,), (0,)), ((), ())), preferred_element_type=jnp.float32
        ),
        "img",
        scatter_dimension=0,
        tiled=True,
    )
    return (grad_regions, grad_phrases.astype(jnp.bfloat16))


def solution(mesh):
    in_specs = (P("img", None), P("phr", None), P("img"), P("img", None))
    out_specs = (P("img", "phr"), P(("phr", "img"), None))
    return jax.shard_map(
        per_device, mesh=mesh, in_specs=in_specs, out_specs=out_specs, check_vma=False
    )
```

profile of v0, /device:TPU:0, one launch (start us, length us, event | category | flops | bytes accessed | tf_op | source)
XLA Modules:
  0.0 328.3 jit_solution(2003548850749267279)
XLA Ops:
  7.2 0.0 copy-start
  7.2 0.0 reduce-scatter.3.cloned.1.call-start
  7.2 1.5 copy-done
  8.8 14.6 %multiply_reduce_fusion = (f32[1024]{0:T(1024)S(1)}, f32[1024,4096]{1,0:T(8,128)}) fusion(bf16[1024,1024]{1,0:T(8,128)(2,1)S(1)} %copy-done, bf16[4096,1024]{1,0:T(8,128)(2,1)} %param.7), kind=kOutput, calls=%fused_computation.5 | convolution fusion | flops 8598322176 | bytes 27267072 | tf_op jit(solution)/shard_map/dot_general | solution.py:30
  23.4 29.5 %all-gather = f32[8192]{0:T(1024)S(1)} all-gather(f32[1024]{0:T(1024)S(1)} %get-tuple-element.151), channel_id=2, replica_groups=mesh['img'=16,'phr'=8] {'phr'}, dimensions={0}, use_global_device_ids=true | all-gather | bytes 36864 | tf_op jit(solution)/shard_map/all_gather | solution.py:10
  52.9 0.0 copy-start.2
  52.9 0.0 copy-start.3
  52.9 8.6 %exponential_reduce_fusion = f32[1024]{0:T(1024)S(1)} fusion(f32[1024,4096]{1,0:T(8,128)} %get-tuple-element.152, f32[1024]{0:T(1024)S(1)} %get-tuple-element.151), kind=kLoop, calls=%fused_computation.4 | loop fusion | flops 12581888 | bytes 16785408 | tf_op jit(solution)/shard_map/reduce_sum | solution.py:36
  61.5 28.1 %all-gather.1 = f32[8192]{0:T(1024)S(1)} all-gather(f32[1024]{0:T(1024)S(1)} %exponential_reduce_fusion), channel_id=3, replica_groups=mesh['img'=16,'phr'=8] {'phr'}, dimensions={0}, use_global_device_ids=true | all-gather | bytes 36864 | tf_op jit(solution)/shard_map/all_gather | solution.py:10
  89.6 0.0 copy-done.2
  89.6 0.1 convert_element_type.23
  89.7 0.4 while.17
  90.1 0.0 copy-done.3
  90.1 8.7 %multiply_convert_fusion = bf16[1024,4096]{1,0:T(8,128)(2,1)S(1)} fusion(f32[1024,4096]{1,0:T(8,128)} %get-tuple-element.152, s32[4096]{0:T(1024)S(1)} %iota_add_fusion, f32[1024]{0:T(1024)S(1)} %log_add_fusion, f32[1024]{0:T(1024)S(1)} %convert_element_type.23, s32[1024]{0:T(1024)S(1)} %copy-done.3), kind=kLoop, calls=%fused_computation.3 | loop fusion | flops 29360128 | bytes 25194496 | tf_op jit(solution)/shard_map/convert_element_type | solution.py:39
  98.9 0.0 copy-start.1
  98.9 3.2 copy-done.1
  102.1 12.6 %convolution_multiply_fusion.1 = f32[1024,1024]{1,0:T(8,128)} fusion(bf16[1024,4096]{1,0:T(8,128)(2,1)S(1)} %multiply_convert_fusion, bf16[4096,1024]{1,0:T(8,128)(2,1)} %param.7), kind=kOutput, calls=%fused_computation.7 | convolution fusion | flops 8590983168 | bytes 20971520 | tf_op jit(solution)/shard_map/dot_general | solution.py:40
  114.7 0.0 reduce-scatter.3.cloned.1.call-update
  114.7 0.2 reduce-scatter.5.cloned.1.call-start
  114.9 14.6 %convolution_multiply_fusion = f32[4096,1024]{1,0:T(8,128)} fusion(bf16[1024,4096]{1,0:T(8,128)(2,1)} %copy-done.1, bf16[1024,1024]{1,0:T(8,128)(2,1)S(1)} %copy-done), kind=kOutput, calls=%fused_computation.6 | convolution fusion | flops 8594128896 | bytes 27262976 | tf_op jit(solution)/shard_map/dot_general | solution.py:46
  129.5 0.0 reduce-scatter.5.cloned.1.call-update
  129.5 39.7 %reduce-scatter.3.cloned.1.call-done = f32[1024,128]{1,0:T(8,128)} async-done(((f32[1024,1024]{1,0:T(8,128)}), f32[1024,128]{1,0:T(8,128)}) %reduce-scatter.3.cloned.1.call-update) | async-done | bytes 524304 | tf_op jit(solution)/shard_map/reduce_scatter | solution.py:41
  169.2 1.8 convert_element_type.26
  171.0 148.4 %reduce-scatter.5.cloned.1.call-done = f32[256,1024]{1,0:T(8,128)} async-done(((f32[4096,1024]{1,0:T(8,128)}), f32[256,1024]{1,0:T(8,128)}) %reduce-scatter.5.cloned.1.call-update) | async-done | bytes 1048592 | tf_op jit(solution)/shard_map/reduce_scatter | solution.py:44
  319.4 2.1 convert_element_type.27
  (21 shorter events, 0.2 us)
Async XLA Ops:
  7.2 1.6 copy-start
  7.2 162.0 %reduce-scatter.3.cloned.1.call-start = ((), (), s32[]{:S(2)}) async-start(), calls=%async_computation.2 | async-start | bytes 4718592 | tf_op jit(solution)/shard_map/reduce_scatter | solution.py:41
  52.9 36.8 %copy-start.2 = (s32[32,32]{1,0:T(8,128)S(1)}, s32[32,32]{1,0:T(8,128)}, u32[]{:S(2)}) copy-start(s32[32,32]{1,0:T(8,128)} %param.9) | copy-start | bytes 12292
  52.9 37.2 %copy-start.3 = (s32[1024]{0:T(1024)S(1)}, s32[1024]{0:T(1024)}, u32[]{:S(2)}) copy-start(s32[1024]{0:T(1024)} %param.8) | copy-start | bytes 12292
  98.9 3.2 copy-start.1
  114.7 204.7 %reduce-scatter.5.cloned.1.call-start = ((), (), s32[]{:S(2)}) async-start(), calls=%async_computation.3 | async-start | bytes 17825792 | tf_op jit(solution)/shard_map/reduce_scatter | solution.py:44
Sparse Core Ops, SparseCore 0:
  114.8 54.3 reduce-scatter.2
  173.6 145.7 reduce-scatter.4
where the time goes:
time: 329 us; the launch traced here: 328 us
  waiting for transfers between devices  188 us (57%)
  blocking collectives  57.5 us (17%)
  matrix products  41.8 us (13%)
  other arithmetic  21.3 us (6%)
  between operations  14.1 us (4%)
  local copies, waits for them, and re-layouts  4.95 us (2%)
    reduce_scatter x1, waiting for transfers between devices, per_device(): lax.psum_scatter(logit_scale * lax.dot_general(coeff, regions, (((0,), (0...  148 us
    all_gather x2, blocking collectives, joined(): gathered = jax.tree.map(lambda a: lax.all_gather(a, axis), part)  57.5 us
    reduce_scatter x1, waiting for transfers between devices, per_device(): lax.psum_scatter(partial_rows, 'phr', scatter_dimension=1, tiled=True)  39.7 us
    dot_general x1, matrix products, per_device(): lax.dot_general(regions, phrases, (((1,), (1,)), ((), ())), preferred_ele...  14.6 us
    dot_general x1, matrix products, per_device(): lax.dot_general(coeff, regions, (((0,), (0,)), ((), ())), preferred_eleme...  14.6 us
    dot_general x1, matrix products, per_device(): jnp.dot(coeff, phrases, preferred_element_type=jnp.float32)  12.6 us
    convert_element_type x1, other arithmetic, per_device(): (weight[:, None] * (jnp.exp(scores - lse[:, None]) - hits)).astype(jnp.bf...  8.75 us
    reduce_sum x1, other arithmetic, per_device(): total = jnp.sum(jnp.exp(scores - top[:, None]), axis=1)  8.63 us
  transfers between devices with their start and end apart: 2, of which 2 were waited for; matrix products, arithmetic and copies ran while one was open for 5% of the time, Pallas kernels for 0%

commit v1 on v0

v1 whole, which is shorter than its diff:
```python
import math

import jax
import jax.numpy as jnp
from jax import lax
from jax.experimental import pallas as pl
from jax.experimental.pallas import tpu as pltpu
from jax.sharding import PartitionSpec as P

logit_scale = 2.0
log2e = math.log2(math.e)
BLK = 256
ORDER = (2, 1, 3, 0)
VMEM = 48 * 1024 * 1024


def img_perm(f):
    pairs = []
    for y in range(2):
        for x in range(4):
            for c in range(2):
                y2, x2, c2 = f(y, x, c)
                pairs.append(((y * 4 + x) * 2 + c, (y2 * 4 + x2) * 2 + c2))
    return pairs


def phr_perm(f):
    pairs = []
    for y in range(2):
        for z in range(4):
            y2, z2 = f(y, z)
            pairs.append((y * 4 + z, y2 * 4 + z2))
    return pairs


CORE = img_perm(lambda y, x, c: (y, x, 1 - c))
X1 = img_perm(lambda y, x, c: (y, x ^ 1, c))
X3 = img_perm(lambda y, x, c: (y, x ^ 3, c))
YH = img_perm(lambda y, x, c: (1 - y, x, c))


def over_img(a, perm):
    return lax.ppermute(a, "img", perm)


def over_phr(a, dy, dz):
    return lax.ppermute(a, "phr", phr_perm(lambda y, z: (y ^ dy, z ^ dz)))


def scores_kernel(blk, p_ref, r_ref, e_ref, m_ref, l_ref):
    s = lax.dot_general(
        p_ref[...], r_ref[...], (((1,), (1,)), ((), ())), preferred_element_type=jnp.float32
    )
    s = s * (logit_scale * log2e)
    m = jnp.max(s, axis=0, keepdims=True)
    e = jnp.exp2(s - m)
    e_ref[...] = e
    m_ref[0] = m
    l_ref[0] = jnp.sum(e, axis=0, keepdims=True)


def scores_call(blk, phrases, regions):
    rows, dim = regions.shape
    tiles = phrases.shape[0] // BLK // 2
    return pl.pallas_call(
        scores_kernel,
        grid_spec=pltpu.PrefetchScalarGridSpec(
            num_scalar_prefetch=1,
            grid=(tiles,),
            in_specs=[
                pl.BlockSpec((BLK, dim), lambda j, blk: (blk[j], 0)),
                pl.BlockSpec((rows, dim), lambda j, blk: (0, 0)),
            ],
            out_specs=[
                pl.BlockSpec((BLK, rows), lambda j, blk: (j, 0)),
                pl.BlockSpec((1, 1, rows), lambda j, blk: (j, 0, 0)),
                pl.BlockSpec((1, 1, rows), lambda j, blk: (j, 0, 0)),
            ],
        ),
        out_shape=[
            jax.ShapeDtypeStruct((tiles * BLK, rows), jnp.float32),
            jax.ShapeDtypeStruct((tiles, 1, rows), jnp.float32),
            jax.ShapeDtypeStruct((tiles, 1, rows), jnp.float32),
        ],
        compiler_params=pltpu.CompilerParams(vmem_limit_bytes=VMEM),
        cost_estimate=pl.CostEstimate(
            flops=2 * tiles * BLK * rows * dim,
            bytes_accessed=tiles * BLK * rows * 4 + rows * dim * 2 + tiles * BLK * dim * 2,
            transcendentals=tiles * BLK * rows,
        ),
        name="scores",
    )(blk, phrases, regions)


def coefficients(e, scale, pos, first):
    column = first + lax.broadcasted_iota(jnp.int32, e.shape, 0)
    return (e * scale - (column == pos).astype(jnp.float32)).astype(jnp.bfloat16)


def phrase_kernel(
    base, off, eo, ep, so, sp, po, pp, ro, rp, send_a, send_b, keep_a, keep_b
):
    i = pl.program_id(0)
    first = off[base + i]
    half = ro.shape[1] // 2
    co = coefficients(eo[...], so[0], po[...], first)
    cp = coefficients(ep[...], sp[0], pp[...], first)
    acc = jnp.dot(co, ro[...], preferred_element_type=jnp.float32)
    acc += jnp.dot(cp, rp[...], preferred_element_type=jnp.float32)
    acc = logit_scale * acc
    left, right = acc[:, :half], acc[:, half:]
    places = (
        (send_a, 1, send_b, 1),
        (send_a, 0, keep_b, 1),
        (keep_a, 1, send_b, 0),
        (keep_a, 0, keep_b, 0),
    )
    for step, (a, ia, b, ib) in enumerate(places):

        @pl.when(i == step)
        def _():
            a[ia] = left.astype(a.dtype)
            b[ib] = right.astype(b.dtype)


def phrase_call(base, off, eo, ep, so, sp, po, pp, ro, rp):
    rows, dim = ro.shape
    half = dim // 2
    e_spec = pl.BlockSpec((BLK, rows), lambda i, off: (base + i, 0))
    s_spec = pl.BlockSpec((1, 1, rows), lambda i, off: (base + i, 0, 0))
    p_spec = pl.BlockSpec((1, rows), lambda i, off: (0, 0))
    r_spec = pl.BlockSpec((rows, dim), lambda i, off: (0, 0))
    out_spec = pl.BlockSpec((2, BLK, half), lambda i, off: (0, 0, 0))
    return pl.pallas_call(
        lambda *refs: phrase_kernel(base, *refs),
        grid_spec=pltpu.PrefetchScalarGridSpec(
            num_scalar_prefetch=1,
            grid=(4,),
            in_specs=[e_spec, e_spec, s_spec, s_spec, p_spec, p_spec, r_spec, r_spec],
            out_specs=[out_spec] * 4,
        ),
        out_shape=[jax.ShapeDtypeStruct((2, BLK, half), jnp.bfloat16)] * 2
        + [jax.ShapeDtypeStruct((2, BLK, half), jnp.float32)] * 2,
        compiler_params=pltpu.CompilerParams(vmem_limit_bytes=VMEM),
        cost_estimate=pl.CostEstimate(
            flops=2 * 4 * BLK * 2 * rows * dim,
            bytes_accessed=4 * BLK * 2 * rows * 4 + 2 * rows * dim * 2 + 4 * BLK * dim * 3,
            transcendentals=0,
        ),
        name="phrase_part",
    )(off, eo, ep, so, sp, po, pp, ro, rp)


def region_kernel(blk, off, dst, p_hbm, e, s, pos, out, p_buf, coeff, acc, sem):
    tiles = s.shape[0]

    @pl.when(pl.program_id(0) == 0)
    def _():
        copies = [
            pltpu.make_async_copy(
                p_hbm.at[pl.ds(pl.multiple_of(blk[j] * BLK, BLK), BLK)],
                p_buf.at[pl.ds(j * BLK, BLK)],
                sem.at[j],
            )
            for j in range(tiles)
        ]
        for copy in copies:
            copy.start()
        for copy in copies:
            copy.wait()

    for j in range(tiles):
        part = pl.ds(j * BLK, BLK)
        coeff[part] = coefficients(e[part], s[j], pos[...], off[j])
    acc[...] = logit_scale * lax.dot_general(
        coeff[...], p_buf[...], (((0,), (0,)), ((), ())), preferred_element_type=jnp.float32
    )
    for k in range(8):
        cols = pl.ds(pl.multiple_of(dst[k] * 128, 128), 128)
        out[k] = acc[:, cols].astype(out.dtype)


def region_call(blk, off, dst, phrases, e, s, pos, dtype):
    tiles, _, rows = s.shape
    dim = phrases.shape[1]
    return pl.pallas_call(
        region_kernel,
        grid_spec=pltpu.PrefetchScalarGridSpec(
            num_scalar_prefetch=3,
            grid=(rows // BLK,),
            in_specs=[
                pl.BlockSpec(memory_space=pl.ANY),
                pl.BlockSpec((tiles * BLK, BLK), lambda i, *_: (0, i)),
                pl.BlockSpec((tiles, 1, BLK), lambda i, *_: (0, 0, i)),
                pl.BlockSpec((1, BLK), lambda i, *_: (0, i)),
            ],
            out_specs=pl.BlockSpec((8, BLK, 128), lambda i, *_: (0, i, 0)),
            scratch_shapes=[
                pltpu.VMEM((tiles * BLK, dim), jnp.bfloat16),
                pltpu.VMEM((tiles * BLK, BLK), jnp.bfloat16),
                pltpu.VMEM((BLK, dim), jnp.float32),
                pltpu.SemaphoreType.DMA((tiles,)),
            ],
        ),
        out_shape=jax.ShapeDtypeStruct((8, rows, 128), dtype),
        compiler_params=pltpu.CompilerParams(vmem_limit_bytes=VMEM),
        cost_estimate=pl.CostEstimate(
            flops=2 * tiles * BLK * rows * dim,
            bytes_accessed=tiles * BLK * rows * 4 + rows * dim * 4 + tiles * BLK * dim * 2,
            transcendentals=0,
        ),
        name="region_part",
    )(blk, off, dst, phrases, e, s, pos)


def combine(first, *others):
    top = first[0]
    for other in others:
        top = jnp.maximum(top, other[0])
    total = first[1] * jnp.exp2(first[0] - top)
    for other in others:
        total += other[1] * jnp.exp2(other[0] - top)
    return jnp.stack([top, total])


def per_device(regions, phrases, positive, valid):
    img, phr = lax.axis_index("img"), lax.axis_index("phr")
    core, x, yh = img % 2, (img // 2) % 4, img // 8
    yl, z = phr // 4, phr % 4
    blk = jnp.stack([((yh ^ e) * 4 + (x ^ d)) * 2 + core for e in (1, 0) for d in ORDER])
    off = phr * phrases.shape[0] + blk * BLK
    dst = jnp.stack([(yl ^ dy) * 4 + (z ^ dz) for dy in (0, 1) for dz in range(4)])
    blk, off, dst = (a.astype(jnp.int32) for a in (blk, off, dst))

    pos_own = jnp.where(valid.reshape(-1) != 0, positive, -1)
    regions_pair = over_img(regions, CORE)
    pos_pair = over_img(pos_own, CORE)
    e_own, m_own, l_own = scores_call(blk, phrases, regions)
    e_pair, m_pair, l_pair = scores_call(blk, phrases, regions_pair)

    m = jnp.stack([m_own[:, 0], m_pair[:, 0]])
    l = jnp.stack([l_own[:, 0], l_pair[:, 0]])
    top = jnp.max(m, axis=1)
    state = jnp.stack([top, jnp.sum(l * jnp.exp2(m - top[:, None]), axis=1)])
    state = combine(state, over_img(state, CORE)[:, ::-1])
    state = combine(state, over_phr(state, 1, 0))
    state = combine(state, *[over_phr(state, 0, dz) for dz in (1, 2, 3)])
    lse = state[0] + jnp.log2(state[1])
    s_own = jnp.where(pos_own >= 0, jnp.exp2(m_own - lse[0]), 0.0)
    s_pair = jnp.where(pos_pair >= 0, jnp.exp2(m_pair - lse[1]), 0.0)
    po, pp = pos_own[None], pos_pair[None]

    totals = []
    for base in (0, 4):
        send_a, send_b, keep_a, keep_b = phrase_call(
            base, off, e_own, e_pair, s_own, s_pair, po, pp, regions, regions_pair
        )
        got_a = over_img(send_a, X1)
        got_b = over_img(send_b, X3)
        sum_a = keep_a + got_a.astype(jnp.float32)
        sum_b = keep_b + got_b.astype(jnp.float32)
        last_a = over_img(sum_a[1].astype(jnp.bfloat16), X3)
        last_b = over_img(sum_b[1].astype(jnp.bfloat16), X1)
        totals.append(
            jnp.concatenate(
                [sum_a[0] + last_a.astype(jnp.float32), sum_b[0] + last_b.astype(jnp.float32)],
                axis=1,
            )
        )
    far, near = totals
    grad_phrases = near + over_img(far.astype(jnp.bfloat16), YH).astype(jnp.float32)

    for_pair = region_call(blk, off, dst, phrases, e_pair, s_pair, pp, jnp.bfloat16)
    from_pair = over_img(for_pair, CORE)
    kept = region_call(blk, off, dst, phrases, e_own, s_own, po, jnp.float32)
    kept = kept + from_pair.astype(jnp.float32)
    sends = kept[1:].astype(jnp.bfloat16)
    grad_regions = kept[0]
    for k in range(1, 8):
        grad_regions += over_phr(sends[k - 1], k // 4, k % 4).astype(jnp.float32)
    return grad_regions.astype(jnp.bfloat16), grad_phrases.astype(jnp.bfloat16)


def solution(mesh):
    in_specs = (P("img", None), P("phr", None), P("img"), P("img", None))
    out_specs = (P("img", "phr"), P(("phr", "img"), None))
    return jax.shard_map(
        per_device, mesh=mesh, in_specs=in_specs, out_specs=out_specs, check_vma=False
    )
```

time: 329 us -> 145 us (0.44)
  waiting for transfers between devices: 188 us -> 43.1 us
  Pallas kernels: 0 us -> 62.3 us
  blocking collectives: 57.5 us -> 0 us
  matrix products: 41.8 us -> 0 us
  starting transfers between devices: 0.26 us -> 29.7 us
  other arithmetic: 21.3 us -> 5.93 us
  between operations: 14.1 us -> 0.99 us
    reduce_scatter x2 -> x0, waiting for transfers between devices: 188 us -> none  [the longest x1 148 us: per_device(): lax.psum_scatter(logit_scale * lax.dot_general(coeff, regions, (((0,), (0...]
    pallas_call x0 -> x6, Pallas kernels: none -> 62.3 us  [the longest x2 24.1 us: scores_call(): pl.pallas_call(scores_kernel, grid_spec=pltpu.PrefetchScalarGridSpec(num_...]
    all_gather x2 -> x0, blocking collectives: 57.5 us -> none  [joined(): gathered = jax.tree.map(lambda a: lax.all_gather(a, axis), part)]
    ppermute x0 -> x24, waiting for transfers between devices: none -> 43.1 us  [the longest x11 30.2 us: over_phr(): return lax.ppermute(a, 'phr', phr_perm(lambda y, z: (y ^ dy, z ^ dz)))]
    dot_general x3 -> x0, matrix products: 41.8 us -> none  [the longest x1 14.6 us: per_device(): lax.dot_general(regions, phrases, (((1,), (1,)), ((), ())), preferred_ele...]
    ppermute x0 -> x24, starting transfers between devices: none -> 29.7 us  [the longest x11 15.4 us: over_phr(): return lax.ppermute(a, 'phr', phr_perm(lambda y, z: (y ^ dy, z ^ dz)))]
    convert_element_type x4 -> x2, other arithmetic: 12.6 us -> 1.91 us  [the longest x1 0.97 us: per_device(): grad_regions.astype(jnp.bfloat16)]
    reduce_sum x1, other arithmetic: 8.63 us -> 0.16 us  [per_device(): state = jnp.stack([top, jnp.sum(l * jnp.exp2(m - top[:, None]), axis=1)])]
  transfers between devices with their start and end apart: 2 -> 24, of which waited for: 2 -> 12; matrix products, arithmetic and copies ran while one was open for 5% -> 4% of each run, Pallas kernels for 0% -> 29%
where the time goes in v1:
time: 145 us
  Pallas kernels  62.3 us (43%)
  waiting for transfers between devices  43.1 us (30%)
  starting transfers between devices  29.7 us (20%)
  other arithmetic  5.93 us (4%)
  local copies, waits for them, and re-layouts  2.54 us (2%)
    ppermute x11, waiting for transfers between devices, over_phr(): return lax.ppermute(a, 'phr', phr_perm(lambda y, z: (y ^ dy, z ^ dz)))  30.2 us
    pallas_call x2, Pallas kernels, scores_call(): pl.pallas_call(scores_kernel, grid_spec=pltpu.PrefetchScalarGridSpec(num_...  24.1 us
    pallas_call x2, Pallas kernels, region_call(): pl.pallas_call(region_kernel, grid_spec=pltpu.PrefetchScalarGridSpec(num_...  21.3 us
    pallas_call x2, Pallas kernels, phrase_call(): pl.pallas_call(lambda *refs: phrase_kernel(base, *refs), grid_spec=pltpu....  16.9 us
    ppermute x11, starting transfers between devices, over_phr(): return lax.ppermute(a, 'phr', phr_perm(lambda y, z: (y ^ dy, z ^ dz)))  15.4 us
    ppermute x13, starting transfers between devices, over_img(): return lax.ppermute(a, 'img', perm)  14.2 us
    ppermute x13, waiting for transfers between devices, over_img(): return lax.ppermute(a, 'img', perm)  12.9 us
  transfers between devices with their start and end apart: 24, of which 12 were waited for; matrix products, arithmetic and copies ran while one was open for 4% of the time, Pallas kernels for 29%

profile of v1, /device:TPU:0, one launch (start us, length us, event | category | flops | bytes accessed | tf_op | source)
XLA Modules:
  0.0 144.6 jit_solution(3564683528883518250)
XLA Ops:
  0.8 0.7 broadcast_compare_fusion
  1.7 1.6 %copy-done = bf16[1024,1024]{1,0:T(8,128)(2,1)S(1)} copy-done((bf16[1024,1024]{1,0:T(8,128)(2,1)S(1)}, bf16[1024,1024]{1,0:T(8,128)(2,1)}, u32[]{:S(2)}) %copy-start) | copy-done | bytes 2097176
  3.3 11.7 %scores.2 = (f32[2048,1024]{1,0:T(8,128)}, f32[8,1,1024]{2,1,0:T(1,128)S(1)}, f32[8,1,1024]{2,1,0:T(1,128)S(1)}) custom-call(s32[8]{0:T(128)S(1)} %stack.87.blk, bf16[4096,1024]{1,0:T(8,128)(2,1)} %p_hbm.3, bf16[1024,1024]{1,0:T(8,128)(2,1)S(1)} %copy-done), custom_call_target="tpu_custom_call" | custom-call | flops 4294967296 | bytes 14680064 | tf_op jit(solution)/shard_map/scores/pallas_call | solution.py:65
  15.0 12.4 %scores.3 = (f32[2048,1024]{1,0:T(8,128)}, f32[8,1,1024]{2,1,0:T(1,128)S(1)}, f32[8,1,1024]{2,1,0:T(1,128)S(1)}) custom-call(s32[8]{0:T(128)S(1)} %stack.87.blk, bf16[4096,1024]{1,0:T(8,128)(2,1)} %p_hbm.3, bf16[1024,1024]{1,0:T(8,128)(2,1)} %collective-permute-done.r_ref.refs_8_), custom_call_target="tpu_custom_call" | custom-call | flops 4294967296 | bytes 14680064 | tf_op jit(solution)/shard_map/scores/pallas_call | solution.py:65
  27.4 0.2 fusion.19
  27.6 0.5 collective-permute-start.1
  28.3 0.7 collective-permute-done.1
  29.0 0.2 slice.109
  29.1 0.2 slice.111
  29.4 1.7 %collective-permute-start.2 = (f32[2,2,1024]{2,1,0:T(2,128)S(1)}, f32[2,2,1024]{2,1,0:T(2,128)S(1)}, u32[]{:S(2)}, u32[]{:S(2)}) collective-permute-start(f32[2,2,1024]{2,1,0:T(2,128)S(1)} %pad_maximum_fusion.3), channel_id=1, source_target_pairs={{0,4},{1,5},{2,6},{3,7},{4,0},{5,1},{6,2},{7,3},{8,12},{9,13},{10,... | collective-permute-start | bytes 49160 | tf_op jit(solution)/shard_map/ppermute | solution.py:47
  31.3 2.0 %collective-permute-done.2 = f32[2,2,1024]{2,1,0:T(2,128)S(1)} collective-permute-done((f32[2,2,1024]{2,1,0:T(2,128)S(1)}, f32[2,2,1024]{2,1,0:T(2,128)S(1)}, u32[]{:S(2)}, u32[]{:S(2)}) %collective-permute-start.2) | collective-permute-done | bytes 16416 | tf_op jit(solution)/shard_map/ppermute | solution.py:47
  33.3 2.1 %collective-permute-start.3 = (f32[2,2,1024]{2,1,0:T(2,128)S(1)}, f32[2,2,1024]{2,1,0:T(2,128)S(1)}, u32[]{:S(2)}, u32[]{:S(2)}) collective-permute-start(f32[2,2,1024]{2,1,0:T(2,128)S(1)} %pad_maximum_fusion.4), channel_id=1, source_target_pairs={{0,1},{1,0},{2,3},{3,2},{4,5},{5,4},{6,7},{7,6},{8,9},{9,8},{10,11... | collective-permute-start | bytes 49160 | tf_op jit(solution)/shard_map/ppermute | solution.py:47
  35.4 3.6 %collective-permute-start.4 = (f32[2,2,1024]{2,1,0:T(2,128)S(1)}, f32[2,2,1024]{2,1,0:T(2,128)S(1)}, u32[]{:S(2)}, u32[]{:S(2)}) collective-permute-start(f32[2,2,1024]{2,1,0:T(2,128)S(1)} %pad_maximum_fusion.4), channel_id=1, source_target_pairs={{0,2},{1,3},{2,0},{3,1},{4,6},{5,7},{6,4},{7,5},{8,10},{9,11},{10,... | collective-permute-start | bytes 49160 | tf_op jit(solution)/shard_map/ppermute | solution.py:47
  39.0 1.9 %collective-permute-done.4 = f32[2,2,1024]{2,1,0:T(2,128)S(1)} collective-permute-done((f32[2,2,1024]{2,1,0:T(2,128)S(1)}, f32[2,2,1024]{2,1,0:T(2,128)S(1)}, u32[]{:S(2)}, u32[]{:S(2)}) %collective-permute-start.4) | collective-permute-done | bytes 16416 | tf_op jit(solution)/shard_map/ppermute | solution.py:47
  40.8 3.1 %collective-permute-done.5 = f32[2,2,1024]{2,1,0:T(2,128)S(1)} collective-permute-done((f32[2,2,1024]{2,1,0:T(2,128)S(1)}, f32[2,2,1024]{2,1,0:T(2,128)S(1)}, u32[]{:S(2)}, u32[]{:S(2)}) %collective-permute-start.5) | collective-permute-done | bytes 16416 | tf_op jit(solution)/shard_map/ppermute | solution.py:47
  44.1 8.5 %phrase_part.3 = (bf16[2,256,512]{2,1,0:T(8,128)(2,1)S(1)}, bf16[2,256,512]{2,1,0:T(8,128)(2,1)S(1)}, f32[2,256,512]{2,1,0:T(8,128)S(1)}, f32[2,256,512]{2,1,0:T(8,128)S(1)}) custom-call(s32[8]{0:T(128)S(1)} %multiply_add_fusion.2.off.refs_0_, f32[2048,1024]{1,0:T(8,128)} %get-tuple-element.16.e.refs_1_, f32[2048,1024]{1,0:T(8,128)} %get-tuple-element.21.e.refs_2_, ...), custom_call_target="tpu_custom_call" | custom-call | flops 4294967296 | bytes 15728640 | tf_op jit(solution)/shard_map/phrase_part/pallas_call | solution.py:134
  52.6 1.6 %collective-permute-start.19 = (bf16[2,256,512]{2,1,0:T(8,128)(2,1)S(1)}, bf16[2,256,512]{2,1,0:T(8,128)(2,1)}, u32[]{:S(2)}, u32[]{:S(2)}) collective-permute-start(bf16[2,256,512]{2,1,0:T(8,128)(2,1)S(1)} %get-tuple-element.27), channel_id=1, source_target_pairs={{0,16},{8,24},{16,0},{24,8},{32,48},{40,56},{48,32},{56,40},{64,80... | collective-permute-start | bytes 1572872 | tf_op jit(solution)/shard_map/ppermute | solution.py:43
  54.2 2.1 %collective-permute-start.21 = (bf16[2,256,512]{2,1,0:T(8,128)(2,1)S(1)}, bf16[2,256,512]{2,1,0:T(8,128)(2,1)S(1)}, u32[]{:S(2)}, u32[]{:S(2)}) collective-permute-start(bf16[2,256,512]{2,1,0:T(8,128)(2,1)S(1)} %get-tuple-element.29), channel_id=1, source_target_pairs={{0,48},{8,56},{16,32},{24,40},{32,16},{40,24},{48,0},{56,8},{64,11... | collective-permute-start | bytes 1572872 | tf_op jit(solution)/shard_map/ppermute | solution.py:43
  56.3 8.5 %phrase_part.2 = (bf16[2,256,512]{2,1,0:T(8,128)(2,1)S(1)}, bf16[2,256,512]{2,1,0:T(8,128)(2,1)S(1)}, f32[2,256,512]{2,1,0:T(8,128)S(1)}, f32[2,256,512]{2,1,0:T(8,128)S(1)}) custom-call(s32[8]{0:T(128)S(1)} %multiply_add_fusion.2.off.refs_0_, f32[2048,1024]{1,0:T(8,128)} %get-tuple-element.16.e.refs_1_, f32[2048,1024]{1,0:T(8,128)} %get-tuple-element.21.e.refs_2_, ...), custom_call_target="tpu_custom_call" | custom-call | flops 4294967296 | bytes 15728640 | tf_op jit(solution)/shard_map/phrase_part/pallas_call | solution.py:134
  64.8 0.7 collective-permute-start.15
  65.4 0.6 collective-permute-start.17
  66.1 10.6 %region_part.3 = bf16[8,1024,128]{2,1,0:T(8,128)(2,1)S(1)} custom-call(s32[8]{0:T(128)S(1)} %stack.87.blk, s32[8]{0:T(128)S(1)} %multiply_add_fusion.2.off.refs_0_, s32[8]{0:T(128)S(1)} %stack.96.dst, bf16[4096,1024]{1,0:T(8,128)(2,1)} %p_hbm.3, f32[2048,1024]{1,0:T(8,128)} %get-tuple-element.21.e.refs_2_, f32[8,1,1024]{2,1,0:T(1,128)S(1)} %broadcast_select_fusion.s.refs_4_, ...), custom_call_target="tpu_custom_call" | custom-call | flops 4294967296 | bytes 16777216 | tf_op jit(solution)/shard_map/region_part/pallas_call | solution.py:186
  76.8 10.7 %region_part.2 = f32[8,1024,128]{2,1,0:T(8,128)S(1)} custom-call(s32[8]{0:T(128)S(1)} %stack.87.blk, s32[8]{0:T(128)S(1)} %multiply_add_fusion.2.off.refs_0_, s32[8]{0:T(128)S(1)} %stack.96.dst, bf16[4096,1024]{1,0:T(8,128)(2,1)} %p_hbm.3, f32[2048,1024]{1,0:T(8,128)} %get-tuple-element.16.e.refs_1_, f32[8,1,1024]{2,1,0:T(1,128)S(1)} %broadcast_select_fusion.1.s.refs_3_, ...), custom_call_target="tpu_custom_call" | custom-call | flops 4294967296 | bytes 16777216 | tf_op jit(solution)/shard_map/region_part/pallas_call | solution.py:186
  87.5 1.2 convert_add_fusion.2
  88.8 2.7 %collective-permute-start.20 = (bf16[256,512]{1,0:T(8,128)(2,1)S(1)}, bf16[256,512]{1,0:T(8,128)(2,1)S(1)}, u32[]{:S(2)}, u32[]{:S(2)}) collective-permute-start(bf16[256,512]{1,0:T(8,128)(2,1)S(1)} %fusion.17), channel_id=1, source_target_pairs={{0,48},{8,56},{16,32},{24,40},{32,16},{40,24},{48,0},{56,8},{64,11... | collective-permute-start | bytes 786440 | tf_op jit(solution)/shard_map/ppermute | solution.py:43
  91.4 0.2 convert_add_fusion.1
  91.7 0.5 collective-permute-start.22
  92.2 0.2 convert_add_fusion.4
  92.4 1.2 collective-permute-start.16
  93.9 0.8 collective-permute-start.18
  94.6 4.5 %collective-permute-done.20 = bf16[256,512]{1,0:T(8,128)(2,1)S(1)} collective-permute-done((bf16[256,512]{1,0:T(8,128)(2,1)S(1)}, bf16[256,512]{1,0:T(8,128)(2,1)S(1)}, u32[]{:S(2)}, u32[]{:S(2)}) %collective-permute-start.20) | collective-permute-done | bytes 262176 | tf_op jit(solution)/shard_map/ppermute | solution.py:43
  99.3 1.8 %collective-permute-done.22 = bf16[256,512]{1,0:T(8,128)(2,1)S(1)} collective-permute-done((bf16[256,512]{1,0:T(8,128)(2,1)S(1)}, bf16[256,512]{1,0:T(8,128)(2,1)S(1)}, u32[]{:S(2)}, u32[]{:S(2)}) %collective-permute-start.22) | collective-permute-done | bytes 262176 | tf_op jit(solution)/shard_map/ppermute | solution.py:43
  101.2 3.3 %collective-permute-start.23 = (bf16[256,1024]{1,0:T(8,128)(2,1)S(1)}, bf16[256,1024]{1,0:T(8,128)(2,1)S(1)}, u32[]{:S(2)}, u32[]{:S(2)}) collective-permute-start(bf16[256,1024]{1,0:T(8,128)(2,1)S(1)} %pad_maximum_fusion), channel_id=1, source_target_pairs={{0,64},{8,72},{16,80},{24,88},{32,96},{40,104},{48,112},{56,120},{... | collective-permute-start | bytes 1572872 | tf_op jit(solution)/shard_map/ppermute | solution.py:43
  104.5 0.7 fusion.47
  105.4 0.8 collective-permute-start.11
  106.3 1.0 collective-permute-start.12
  107.3 4.6 %collective-permute-start.13 = (bf16[1024,128]{1,0:T(8,128)(2,1)S(1)}, bf16[1024,128]{1,0:T(8,128)(2,1)S(1)}, u32[]{:S(2)}, u32[]{:S(2)}) collective-permute-start(bf16[1024,128]{1,0:T(8,128)(2,1)S(1)} %get-tuple-element.38), channel_id=1, source_target_pairs={{0,6},{1,7},{2,4},{3,5},{4,2},{5,3},{6,0},{7,1},{8,14},{9,15},{10,... | collective-permute-start | bytes 786440 | tf_op jit(solution)/shard_map/ppermute | solution.py:47
  111.9 5.8 %collective-permute-done.23 = bf16[256,1024]{1,0:T(8,128)(2,1)S(1)} collective-permute-done((bf16[256,1024]{1,0:T(8,128)(2,1)S(1)}, bf16[256,1024]{1,0:T(8,128)(2,1)S(1)}, u32[]{:S(2)}, u32[]{:S(2)}) %collective-permute-start.23) | collective-permute-done | bytes 524320 | tf_op jit(solution)/shard_map/ppermute | solution.py:43
  117.7 1.0 collective-permute-start.14
  118.7 0.3 collective-permute-start.8
  119.0 4.7 %collective-permute-done.11 = bf16[1024,128]{1,0:T(8,128)(2,1)S(1)} collective-permute-done((bf16[1024,128]{1,0:T(8,128)(2,1)S(1)}, bf16[1024,128]{1,0:T(8,128)(2,1)S(1)}, u32[]{:S(2)}, u32[]{:S(2)}) %collective-permute-start.11) | collective-permute-done | bytes 262176 | tf_op jit(solution)/shard_map/ppermute | solution.py:47
  123.7 0.3 collective-permute-start.9
  124.0 0.9 fusion
  125.0 3.2 %collective-permute-done.12 = bf16[1024,128]{1,0:T(8,128)(2,1)S(1)} collective-permute-done((bf16[1024,128]{1,0:T(8,128)(2,1)S(1)}, bf16[1024,128]{1,0:T(8,128)(2,1)S(1)}, u32[]{:S(2)}, u32[]{:S(2)}) %collective-permute-start.12) | collective-permute-done | bytes 262176 | tf_op jit(solution)/shard_map/ppermute | solution.py:47
  128.2 7.4 %collective-permute-done.13 = bf16[1024,128]{1,0:T(8,128)(2,1)S(1)} collective-permute-done((bf16[1024,128]{1,0:T(8,128)(2,1)S(1)}, bf16[1024,128]{1,0:T(8,128)(2,1)S(1)}, u32[]{:S(2)}, u32[]{:S(2)}) %collective-permute-start.13) | collective-permute-done | bytes 262176 | tf_op jit(solution)/shard_map/ppermute | solution.py:47
  135.6 5.8 %collective-permute-done.14 = bf16[1024,128]{1,0:T(8,128)(2,1)S(1)} collective-permute-done((bf16[1024,128]{1,0:T(8,128)(2,1)S(1)}, bf16[1024,128]{1,0:T(8,128)(2,1)S(1)}, u32[]{:S(2)}, u32[]{:S(2)}) %collective-permute-start.14) | collective-permute-done | bytes 262176 | tf_op jit(solution)/shard_map/ppermute | solution.py:47
  141.4 2.2 %collective-permute-done.9 = bf16[1024,128]{1,0:T(8,128)(2,1)S(1)} collective-permute-done((bf16[1024,128]{1,0:T(8,128)(2,1)S(1)}, bf16[1024,128]{1,0:T(8,128)(2,1)S(1)}, u32[]{:S(2)}, u32[]{:S(2)}) %collective-permute-start.9) | collective-permute-done | bytes 262176 | tf_op jit(solution)/shard_map/ppermute | solution.py:47
  143.6 1.0 fusion.14
  (50 shorter events, 1.9 us)
Async XLA Ops:
  0.6 14.3 %collective-permute-start = (bf16[1024,1024]{1,0:T(8,128)(2,1)}, bf16[1024,1024]{1,0:T(8,128)(2,1)}, u32[]{:S(2)}, u32[]{:S(2)}) collective-permute-start(bf16[1024,1024]{1,0:T(8,128)(2,1)} %refs_7_.3), channel_id=1, source_target_pairs={{0,8},{8,0},{16,24},{24,16},{32,40},{40,32},{48,56},{56,48},{64,72... | collective-permute-start | bytes 6291464 | tf_op jit(solution)/shard_map/ppermute | solution.py:43
  1.7 1.6 %copy-start = (bf16[1024,1024]{1,0:T(8,128)(2,1)S(1)}, bf16[1024,1024]{1,0:T(8,128)(2,1)}, u32[]{:S(2)}) copy-start(bf16[1024,1024]{1,0:T(8,128)(2,1)} %refs_7_.3) | copy-start | bytes 6291460
  14.9 13.2 %copy-start.2 = (s32[1024]{0:T(1024)S(1)}, s32[1024]{0:T(1024)}, u32[]{:S(2)}) copy-start(s32[1024]{0:T(1024)} %param.6) | copy-start | bytes 12292
  14.9 29.2 %copy-start.1 = (bf16[1024,1024]{1,0:T(8,128)(2,1)S(1)}, bf16[1024,1024]{1,0:T(8,128)(2,1)}, u32[]{:S(2)}) copy-start(bf16[1024,1024]{1,0:T(8,128)(2,1)} %refs_7_.3) | copy-start | bytes 6291460
  27.6 1.3 collective-permute-start.1
  28.1 10.8 %collective-permute-start.6 = (s32[1024]{0:T(1024)S(1)}, s32[1024]{0:T(1024)S(1)}, u32[]{:S(2)}, u32[]{:S(2)}) collective-permute-start(s32[1024]{0:T(1024)S(1)} %get-tuple-element.35), channel_id=1, source_target_pairs={{0,8},{8,0},{16,24},{24,16},{32,40},{40,32},{48,56},{56,48},{64,72... | collective-permute-start | bytes 12296 | tf_op jit(solution)/shard_map/ppermute | solution.py:43
  29.4 3.8 %collective-permute-start.2 = (f32[2,2,1024]{2,1,0:T(2,128)S(1)}, f32[2,2,1024]{2,1,0:T(2,128)S(1)}, u32[]{:S(2)}, u32[]{:S(2)}) collective-permute-start(f32[2,2,1024]{2,1,0:T(2,128)S(1)} %pad_maximum_fusion.3), channel_id=1, source_target_pairs={{0,4},{1,5},{2,6},{3,7},{4,0},{5,1},{6,2},{7,3},{8,12},{9,13},{10,... | collective-permute-start | bytes 49160 | tf_op jit(solution)/shard_map/ppermute | solution.py:47
  33.3 5.7 %collective-permute-start.3 = (f32[2,2,1024]{2,1,0:T(2,128)S(1)}, f32[2,2,1024]{2,1,0:T(2,128)S(1)}, u32[]{:S(2)}, u32[]{:S(2)}) collective-permute-start(f32[2,2,1024]{2,1,0:T(2,128)S(1)} %pad_maximum_fusion.4), channel_id=1, source_target_pairs={{0,1},{1,0},{2,3},{3,2},{4,5},{5,4},{6,7},{7,6},{8,9},{9,8},{10,11... | collective-permute-start | bytes 49160 | tf_op jit(solution)/shard_map/ppermute | solution.py:47
  35.4 5.5 %collective-permute-start.4 = (f32[2,2,1024]{2,1,0:T(2,128)S(1)}, f32[2,2,1024]{2,1,0:T(2,128)S(1)}, u32[]{:S(2)}, u32[]{:S(2)}) collective-permute-start(f32[2,2,1024]{2,1,0:T(2,128)S(1)} %pad_maximum_fusion.4), channel_id=1, source_target_pairs={{0,2},{1,3},{2,0},{3,1},{4,6},{5,7},{6,4},{7,5},{8,10},{9,11},{10,... | collective-permute-start | bytes 49160 | tf_op jit(solution)/shard_map/ppermute | solution.py:47
  39.0 4.9 %collective-permute-start.5 = (f32[2,2,1024]{2,1,0:T(2,128)S(1)}, f32[2,2,1024]{2,1,0:T(2,128)S(1)}, u32[]{:S(2)}, u32[]{:S(2)}) collective-permute-start(f32[2,2,1024]{2,1,0:T(2,128)S(1)} %pad_maximum_fusion.4), channel_id=1, source_target_pairs={{0,3},{1,2},{2,1},{3,0},{4,7},{5,6},{6,5},{7,4},{8,11},{9,10},{10,... | collective-permute-start | bytes 49160 | tf_op jit(solution)/shard_map/ppermute | solution.py:47
  52.6 34.9 %collective-permute-start.19 = (bf16[2,256,512]{2,1,0:T(8,128)(2,1)S(1)}, bf16[2,256,512]{2,1,0:T(8,128)(2,1)}, u32[]{:S(2)}, u32[]{:S(2)}) collective-permute-start(bf16[2,256,512]{2,1,0:T(8,128)(2,1)S(1)} %get-tuple-element.27), channel_id=1, source_target_pairs={{0,16},{8,24},{16,0},{24,8},{32,48},{40,56},{48,32},{56,40},{64,80... | collective-permute-start | bytes 1572872 | tf_op jit(solution)/shard_map/ppermute | solution.py:43
  54.2 37.3 %collective-permute-start.21 = (bf16[2,256,512]{2,1,0:T(8,128)(2,1)S(1)}, bf16[2,256,512]{2,1,0:T(8,128)(2,1)S(1)}, u32[]{:S(2)}, u32[]{:S(2)}) collective-permute-start(bf16[2,256,512]{2,1,0:T(8,128)(2,1)S(1)} %get-tuple-element.29), channel_id=1, source_target_pairs={{0,48},{8,56},{16,32},{24,40},{32,16},{40,24},{48,0},{56,8},{64,11... | collective-permute-start | bytes 1572872 | tf_op jit(solution)/shard_map/ppermute | solution.py:43
  64.8 27.4 %collective-permute-start.15 = (bf16[2,256,512]{2,1,0:T(8,128)(2,1)S(1)}, bf16[2,256,512]{2,1,0:T(8,128)(2,1)S(1)}, u32[]{:S(2)}, u32[]{:S(2)}) collective-permute-start(bf16[2,256,512]{2,1,0:T(8,128)(2,1)S(1)} %get-tuple-element.23), channel_id=1, source_target_pairs={{0,16},{8,24},{16,0},{24,8},{32,48},{40,56},{48,32},{56,40},{64,80... | collective-permute-start | bytes 1572872 | tf_op jit(solution)/shard_map/ppermute | solution.py:43
  65.4 28.2 %collective-permute-start.17 = (bf16[2,256,512]{2,1,0:T(8,128)(2,1)S(1)}, bf16[2,256,512]{2,1,0:T(8,128)(2,1)S(1)}, u32[]{:S(2)}, u32[]{:S(2)}) collective-permute-start(bf16[2,256,512]{2,1,0:T(8,128)(2,1)S(1)} %get-tuple-element.25), channel_id=1, source_target_pairs={{0,48},{8,56},{16,32},{24,40},{32,16},{40,24},{48,0},{56,8},{64,11... | collective-permute-start | bytes 1572872 | tf_op jit(solution)/shard_map/ppermute | solution.py:43
  76.7 27.8 %collective-permute-start.7 = (bf16[8,1024,128]{2,1,0:T(8,128)(2,1)S(1)}, bf16[8,1024,128]{2,1,0:T(8,128)(2,1)S(1)}, u32[]{:S(2)}, u32[]{:S(2)}) collective-permute-start(bf16[8,1024,128]{2,1,0:T(8,128)(2,1)S(1)} %region_part.3), channel_id=1, source_target_pairs={{0,8},{8,0},{16,24},{24,16},{32,40},{40,32},{48,56},{56,48},{64,72... | collective-permute-start | bytes 6291464 | tf_op jit(solution)/shard_map/ppermute | solution.py:43
  88.8 10.4 %collective-permute-start.20 = (bf16[256,512]{1,0:T(8,128)(2,1)S(1)}, bf16[256,512]{1,0:T(8,128)(2,1)S(1)}, u32[]{:S(2)}, u32[]{:S(2)}) collective-permute-start(bf16[256,512]{1,0:T(8,128)(2,1)S(1)} %fusion.17), channel_id=1, source_target_pairs={{0,48},{8,56},{16,32},{24,40},{32,16},{40,24},{48,0},{56,8},{64,11... | collective-permute-start | bytes 786440 | tf_op jit(solution)/shard_map/ppermute | solution.py:43
  91.7 9.4 %collective-permute-start.22 = (bf16[256,512]{1,0:T(8,128)(2,1)S(1)}, bf16[256,512]{1,0:T(8,128)(2,1)S(1)}, u32[]{:S(2)}, u32[]{:S(2)}) collective-permute-start(bf16[256,512]{1,0:T(8,128)(2,1)S(1)} %fusion.18), channel_id=1, source_target_pairs={{0,16},{8,24},{16,0},{24,8},{32,48},{40,56},{48,32},{56,40},{64,80... | collective-permute-start | bytes 786440 | tf_op jit(solution)/shard_map/ppermute | solution.py:43
  92.4 13.8 %collective-permute-start.16 = (bf16[256,512]{1,0:T(8,128)(2,1)S(1)}, bf16[256,512]{1,0:T(8,128)(2,1)S(1)}, u32[]{:S(2)}, u32[]{:S(2)}) collective-permute-start(bf16[256,512]{1,0:T(8,128)(2,1)S(1)} %fusion.15), channel_id=1, source_target_pairs={{0,48},{8,56},{16,32},{24,40},{32,16},{40,24},{48,0},{56,8},{64,11... | collective-permute-start | bytes 786440 | tf_op jit(solution)/shard_map/ppermute | solution.py:43
  93.9 13.4 %collective-permute-start.18 = (bf16[256,512]{1,0:T(8,128)(2,1)S(1)}, bf16[256,512]{1,0:T(8,128)(2,1)S(1)}, u32[]{:S(2)}, u32[]{:S(2)}) collective-permute-start(bf16[256,512]{1,0:T(8,128)(2,1)S(1)} %fusion.16), channel_id=1, source_target_pairs={{0,16},{8,24},{16,0},{24,8},{32,48},{40,56},{48,32},{56,40},{64,80... | collective-permute-start | bytes 786440 | tf_op jit(solution)/shard_map/ppermute | solution.py:43
  101.2 16.4 %collective-permute-start.23 = (bf16[256,1024]{1,0:T(8,128)(2,1)S(1)}, bf16[256,1024]{1,0:T(8,128)(2,1)S(1)}, u32[]{:S(2)}, u32[]{:S(2)}) collective-permute-start(bf16[256,1024]{1,0:T(8,128)(2,1)S(1)} %pad_maximum_fusion), channel_id=1, source_target_pairs={{0,64},{8,72},{16,80},{24,88},{32,96},{40,104},{48,112},{56,120},{... | collective-permute-start | bytes 1572872 | tf_op jit(solution)/shard_map/ppermute | solution.py:43
  105.3 13.3 %collective-permute-start.10 = (bf16[1024,128]{1,0:T(8,128)(2,1)S(1)}, bf16[1024,128]{1,0:T(8,128)(2,1)S(1)}, u32[]{:S(2)}, u32[]{:S(2)}) collective-permute-start(bf16[1024,128]{1,0:T(8,128)(2,1)S(1)} %get-tuple-element.41), channel_id=1, source_target_pairs={{0,3},{1,2},{2,1},{3,0},{4,7},{5,6},{6,5},{7,4},{8,11},{9,10},{10,... | collective-permute-start | bytes 786440 | tf_op jit(solution)/shard_map/ppermute | solution.py:47
  105.4 18.2 %collective-permute-start.11 = (bf16[1024,128]{1,0:T(8,128)(2,1)S(1)}, bf16[1024,128]{1,0:T(8,128)(2,1)S(1)}, u32[]{:S(2)}, u32[]{:S(2)}) collective-permute-start(bf16[1024,128]{1,0:T(8,128)(2,1)S(1)} %get-tuple-element.40), channel_id=1, source_target_pairs={{0,4},{1,5},{2,6},{3,7},{4,0},{5,1},{6,2},{7,3},{8,12},{9,13},{10,... | collective-permute-start | bytes 786440 | tf_op jit(solution)/shard_map/ppermute | solution.py:47
  106.3 21.9 %collective-permute-start.12 = (bf16[1024,128]{1,0:T(8,128)(2,1)S(1)}, bf16[1024,128]{1,0:T(8,128)(2,1)S(1)}, u32[]{:S(2)}, u32[]{:S(2)}) collective-permute-start(bf16[1024,128]{1,0:T(8,128)(2,1)S(1)} %get-tuple-element.39), channel_id=1, source_target_pairs={{0,5},{1,4},{2,7},{3,6},{4,1},{5,0},{6,3},{7,2},{8,13},{9,12},{10,... | collective-permute-start | bytes 786440 | tf_op jit(solution)/shard_map/ppermute | solution.py:47
  107.3 28.3 %collective-permute-start.13 = (bf16[1024,128]{1,0:T(8,128)(2,1)S(1)}, bf16[1024,128]{1,0:T(8,128)(2,1)S(1)}, u32[]{:S(2)}, u32[]{:S(2)}) collective-permute-start(bf16[1024,128]{1,0:T(8,128)(2,1)S(1)} %get-tuple-element.38), channel_id=1, source_target_pairs={{0,6},{1,7},{2,4},{3,5},{4,2},{5,3},{6,0},{7,1},{8,14},{9,15},{10,... | collective-permute-start | bytes 786440 | tf_op jit(solution)/shard_map/ppermute | solution.py:47
  117.7 23.7 %collective-permute-start.14 = (bf16[1024,128]{1,0:T(8,128)(2,1)S(1)}, bf16[1024,128]{1,0:T(8,128)(2,1)S(1)}, u32[]{:S(2)}, u32[]{:S(2)}) collective-permute-start(bf16[1024,128]{1,0:T(8,128)(2,1)S(1)} %get-tuple-element.37), channel_id=1, source_target_pairs={{0,7},{1,6},{2,5},{3,4},{4,3},{5,2},{6,1},{7,0},{8,15},{9,14},{10,... | collective-permute-start | bytes 786440 | tf_op jit(solution)/shard_map/ppermute | solution.py:47
  118.7 22.7 %collective-permute-start.8 = (bf16[1024,128]{1,0:T(8,128)(2,1)S(1)}, bf16[1024,128]{1,0:T(8,128)(2,1)S(1)}, u32[]{:S(2)}, u32[]{:S(2)}) collective-permute-start(bf16[1024,128]{1,0:T(8,128)(2,1)S(1)} %get-tuple-element.36), channel_id=1, source_target_pairs={{0,1},{1,0},{2,3},{3,2},{4,5},{5,4},{6,7},{7,6},{8,9},{9,8},{10,11... | collective-permute-start | bytes 786440 | tf_op jit(solution)/shard_map/ppermute | solution.py:47
  123.7 19.9 %collective-permute-start.9 = (bf16[1024,128]{1,0:T(8,128)(2,1)S(1)}, bf16[1024,128]{1,0:T(8,128)(2,1)S(1)}, u32[]{:S(2)}, u32[]{:S(2)}) collective-permute-start(bf16[1024,128]{1,0:T(8,128)(2,1)S(1)} %get-tuple-element.42), channel_id=1, source_target_pairs={{0,2},{1,3},{2,0},{3,1},{4,6},{5,7},{6,4},{7,5},{8,10},{9,11},{10,... | collective-permute-start | bytes 786440 | tf_op jit(solution)/shard_map/ppermute | solution.py:47

commit v2 on v0

v2 whole, which is shorter than its diff:
```python
import math

import jax
import jax.numpy as jnp
from jax import lax
from jax.experimental import pallas as pl
from jax.experimental.pallas import tpu as pltpu
from jax.sharding import PartitionSpec as P

logit_scale = 2.0
log2e = math.log2(math.e)
BLK = 256
ORDER = (2, 1, 3, 0)
VMEM = 8 * 1024 * 1024


def img_perm(f):
    pairs = []
    for y in range(2):
        for x in range(4):
            for c in range(2):
                y2, x2, c2 = f(y, x, c)
                pairs.append(((y * 4 + x) * 2 + c, (y2 * 4 + x2) * 2 + c2))
    return pairs


def phr_perm(f):
    pairs = []
    for y in range(2):
        for z in range(4):
            y2, z2 = f(y, z)
            pairs.append((y * 4 + z, y2 * 4 + z2))
    return pairs


CORE = img_perm(lambda y, x, c: (y, x, 1 - c))
X1 = img_perm(lambda y, x, c: (y, x ^ 1, c))
X3 = img_perm(lambda y, x, c: (y, x ^ 3, c))
YH = img_perm(lambda y, x, c: (1 - y, x, c))


def over_img(a, perm):
    return lax.ppermute(a, "img", perm)


def over_phr(a, dy, dz):
    return lax.ppermute(a, "phr", phr_perm(lambda y, z: (y ^ dy, z ^ dz)))


def vmem(a):
    return pltpu.with_memory_space_constraint(a, pltpu.VMEM)


WHOLE = pl.BlockSpec(memory_space=pltpu.VMEM)
SCALAR = pl.BlockSpec(memory_space=pltpu.SMEM)
HBM = pl.BlockSpec(memory_space=pltpu.HBM)


def call(body, in_specs, outs, name, flops, **kwargs):
    return pl.pallas_call(
        body,
        in_specs=in_specs,
        out_specs=[WHOLE] * len(outs),
        out_shape=[pltpu.VMEM(*out) for out in outs],
        compiler_params=pltpu.CompilerParams(vmem_limit_bytes=VMEM),
        cost_estimate=pl.CostEstimate(flops=flops, bytes_accessed=1 << 20, transcendentals=0),
        name=name,
        **kwargs,
    )


def score_block(j, phrases, regions, e, m, l):
    part = pl.ds(j * BLK, BLK)
    s = lax.dot_general(
        phrases[part], regions[...], (((1,), (1,)), ((), ())), preferred_element_type=jnp.float32
    )
    s = s * (logit_scale * log2e)
    top = jnp.max(s, axis=0, keepdims=True)
    value = jnp.exp2(s - top)
    e[part] = value
    m[j] = top
    l[j] = jnp.sum(value, axis=0, keepdims=True)


def first_scores_kernel(blk, p_hbm, r_hbm, e, m, l, phrases, regions, sem):
    tiles = m.shape[0]
    copies = [pltpu.make_async_copy(r_hbm, regions, sem.at[tiles])]
    for j in range(tiles):
        rows = pl.ds(pl.multiple_of(blk[j] * BLK, BLK), BLK)
        copies.append(
            pltpu.make_async_copy(p_hbm.at[rows], phrases.at[pl.ds(j * BLK, BLK)], sem.at[j])
        )
    for copy in copies:
        copy.start()
    copies[0].wait()
    for j in range(tiles):
        copies[j + 1].wait()
        score_block(j, phrases, regions, e, m, l)


def first_scores_call(blk, phrases, regions):
    rows, dim = regions.shape
    half = phrases.shape[0] // 2
    tiles = half // BLK
    return call(
        first_scores_kernel,
        [SCALAR, HBM, HBM],
        [
            ((half, rows), jnp.float32),
            ((tiles, 1, rows), jnp.float32),
            ((tiles, 1, rows), jnp.float32),
            ((half, dim), phrases.dtype),
            ((rows, dim), regions.dtype),
        ],
        "first_scores",
        2 * half * rows * dim,
        scratch_shapes=[pltpu.SemaphoreType.DMA((tiles + 1,))],
    )(blk, *[pltpu.with_memory_space_constraint(a, pltpu.HBM) for a in (phrases, regions)])


def scores_kernel(phrases, regions, e, m, l):
    for j in range(m.shape[0]):
        score_block(j, phrases, regions, e, m, l)


def scores_call(phrases, regions):
    rows, dim = regions.shape
    half = phrases.shape[0]
    tiles = half // BLK
    return call(
        scores_kernel,
        [WHOLE] * 2,
        [
            ((half, rows), jnp.float32),
            ((tiles, 1, rows), jnp.float32),
            ((tiles, 1, rows), jnp.float32),
        ],
        "scores",
        2 * half * rows * dim,
    )(vmem(phrases), vmem(regions))


def coefficients(e, scale, pos, first):
    column = first + lax.broadcasted_iota(jnp.int32, e.shape, 0)
    return (e * scale - (column == pos).astype(jnp.float32)).astype(jnp.bfloat16)


def phrase_kernel(base, off, eo, ep, so, sp, po, pp, ro, rp, send_a, send_b, keep_a, keep_b):
    half = ro.shape[1] // 2
    places = (
        (send_a, 1, send_b, 1),
        (send_a, 0, keep_b, 1),
        (keep_a, 1, send_b, 0),
        (keep_a, 0, keep_b, 0),
    )
    for step, (a, ia, b, ib) in enumerate(places):
        j = base + step
        part = pl.ds(j * BLK, BLK)
        co = coefficients(eo[part], so[j], po[...], off[j])
        cp = coefficients(ep[part], sp[j], pp[...], off[j])
        acc = jnp.dot(co, ro[...], preferred_element_type=jnp.float32)
        acc += jnp.dot(cp, rp[...], preferred_element_type=jnp.float32)
        acc = logit_scale * acc
        a[ia] = acc[:, :half].astype(a.dtype)
        b[ib] = acc[:, half:].astype(b.dtype)


def phrase_call(base, off, *arrays):
    rows, dim = arrays[-1].shape
    shape = (2, BLK, dim // 2)
    return call(
        lambda *refs: phrase_kernel(base, *refs),
        [SCALAR] + [WHOLE] * len(arrays),
        [(shape, jnp.bfloat16)] * 2 + [(shape, jnp.float32)] * 2,
        "phrase_part",
        2 * 4 * BLK * 2 * rows * dim,
    )(off, *[vmem(a) for a in arrays])


def region_kernel(phr, off, e, s, pos, phrases, out):
    tiles, _, rows = s.shape
    for i in range(0, rows, BLK):
        lanes = pl.ds(i, BLK)
        coeff = jnp.concatenate(
            [
                coefficients(e[pl.ds(j * BLK, BLK), lanes], s[j, :, lanes], pos[:, lanes], off[j])
                for j in range(tiles)
            ],
            axis=0,
        )
        acc = logit_scale * lax.dot_general(
            coeff, phrases[...], (((0,), (0,)), ((), ())), preferred_element_type=jnp.float32
        )
        for q in range(8):
            out[phr[0] ^ q, lanes] = acc[:, q * 128 : (q + 1) * 128].astype(out.dtype)


def region_call(phr, off, e, s, pos, phrases, dtype):
    tiles, _, rows = s.shape
    dim = phrases.shape[1]
    arrays = (e, s, pos, phrases)
    return call(
        region_kernel,
        [SCALAR] * 2 + [WHOLE] * len(arrays),
        [((8, rows, 128), dtype)],
        "region_part",
        2 * tiles * BLK * rows * dim,
    )(phr, off, *[vmem(a) for a in arrays])[0]


GROUPS = [[(i * 2 + c) * 8 + p for c in range(2) for p in range(8)] for i in range(8)]


def per_device(regions, phrases, positive, valid):
    img, phr = lax.axis_index("img"), lax.axis_index("phr")
    core = img % 2
    blk = jnp.stack([img ^ (e * 8 + d * 2) for e in (1, 0) for d in ORDER]).astype(jnp.int32)
    off = (phr * phrases.shape[0] + blk * BLK).astype(jnp.int32)
    phr_id = phr.astype(jnp.int32)[None]

    pos_own = jnp.where(valid.reshape(-1) != 0, positive, -1)
    regions_pair = over_img(regions, CORE)
    pos_pair = over_img(pos_own, CORE)
    e_own, m_own, l_own, phrases, regions = first_scores_call(blk, phrases, regions)
    e_pair, m_pair, l_pair = scores_call(phrases, regions_pair)

    m = jnp.stack([m_own[:, 0], m_pair[:, 0]])
    l = jnp.stack([l_own[:, 0], l_pair[:, 0]])
    top = jnp.max(m, axis=1)
    state = jnp.stack([top, jnp.sum(l * jnp.exp2(m - top[:, None]), axis=1)])
    to_core = jnp.arange(2, dtype=jnp.int32)[:, None, None, None, None]
    sends = jnp.where(to_core == core, state, state[:, ::-1])
    sends = jnp.broadcast_to(sends, (2, 8) + state.shape).reshape((16,) + state.shape)
    got = lax.all_to_all(
        sends, ("img", "phr"), 0, 0, tiled=True, axis_index_groups=GROUPS
    )
    top = jnp.max(got[:, 0], axis=0)
    lse = top + jnp.log2(jnp.sum(got[:, 1] * jnp.exp2(got[:, 0] - top), axis=0))
    s_own = jnp.where(pos_own >= 0, jnp.exp2(m_own - lse[0]), 0.0)
    s_pair = jnp.where(pos_pair >= 0, jnp.exp2(m_pair - lse[1]), 0.0)
    po, pp = pos_own[None], pos_pair[None]

    totals = []
    for base in (0, 4):
        send_a, send_b, keep_a, keep_b = phrase_call(
            base, off, e_own, e_pair, s_own, s_pair, po, pp, regions, regions_pair
        )
        got_a = over_img(send_a, X1)
        got_b = over_img(send_b, X3)
        sum_a = keep_a + got_a.astype(jnp.float32)
        sum_b = keep_b + got_b.astype(jnp.float32)
        last_a = over_img(sum_a[1].astype(jnp.bfloat16), X3)
        last_b = over_img(sum_b[1].astype(jnp.bfloat16), X1)
        totals.append(
            jnp.concatenate(
                [sum_a[0] + last_a.astype(jnp.float32), sum_b[0] + last_b.astype(jnp.float32)],
                axis=1,
            )
        )
    far, near = totals
    grad_phrases = near + over_img(far.astype(jnp.bfloat16), YH).astype(jnp.float32)

    for_pair = region_call(phr_id, off, e_pair, s_pair, pp, phrases, jnp.bfloat16)
    from_pair = over_img(for_pair, CORE)
    kept = region_call(phr_id, off, e_own, s_own, po, phrases, jnp.float32)
    kept = kept + from_pair.astype(jnp.float32)
    sends = kept[1:].astype(jnp.bfloat16)
    grad_regions = kept[0]
    for k in range(1, 8):
        grad_regions += over_phr(sends[k - 1], k // 4, k % 4).astype(jnp.float32)
    return grad_regions.astype(jnp.bfloat16), grad_phrases.astype(jnp.bfloat16)


def solution(mesh):
    in_specs = (P("img", None), P("phr", None), P("img"), P("img", None))
    out_specs = (P("img", "phr"), P(("phr", "img"), None))
    return jax.shard_map(
        per_device, mesh=mesh, in_specs=in_specs, out_specs=out_specs, check_vma=False
    )
```

time: 329 us -> 128 us (0.39)
  waiting for transfers between devices: 188 us -> 35.7 us
  blocking collectives: 57.5 us -> 0 us
  matrix products: 41.8 us -> 0 us
  Pallas kernels: 0 us -> 36.6 us
  starting transfers between devices: 0.26 us -> 31.3 us
  other arithmetic: 21.3 us -> 5.71 us
  between operations: 14.1 us -> 0.96 us
  local copies, waits for them, and re-layouts: 4.95 us -> 17.7 us
    reduce_scatter x2 -> x0, waiting for transfers between devices: 188 us -> none  [the longest x1 148 us: per_device(): lax.psum_scatter(logit_scale * lax.dot_general(coeff, regions, (((0,), (0...]
    all_gather x2 -> x0, blocking collectives: 57.5 us -> none  [joined(): gathered = jax.tree.map(lambda a: lax.all_gather(a, axis), part)]
    dot_general x3 -> x0, matrix products: 41.8 us -> none  [the longest x1 14.6 us: per_device(): lax.dot_general(regions, phrases, (((1,), (1,)), ((), ())), preferred_ele...]
    pallas_call x0 -> x6, Pallas kernels: none -> 36.6 us  [the longest x2 11 us: region_call(): call(region_kernel, [SCALAR] * 2 + [WHOLE] * len(arrays), [((8, rows, 128...]
    ppermute x0 -> x19, waiting for transfers between devices: none -> 27.9 us  [the longest x12 14.1 us: over_img(): return lax.ppermute(a, 'img', perm)]
    ppermute x0 -> x19, starting transfers between devices: none -> 24.6 us  [the longest x12 14.7 us: over_img(): return lax.ppermute(a, 'img', perm)]
    unnamed x8 -> x24, local copies, waits for them, and re-layouts: 4.77 us -> 16.2 us
    convert_element_type x4 -> x2, other arithmetic: 12.6 us -> 1.91 us  [the longest x1 0.97 us: per_device(): grad_regions.astype(jnp.bfloat16)]
  transfers between devices with their start and end apart: 2 -> 20, of which waited for: 2 -> 8; matrix products, arithmetic and copies ran while one was open for 5% -> 5% of each run, Pallas kernels for 0% -> 25%
where the time goes in v2:
time: 128 us
  Pallas kernels  36.6 us (29%)
  waiting for transfers between devices  35.7 us (28%)
  starting transfers between devices  31.3 us (24%)
  local copies, waits for them, and re-layouts  17.7 us (14%)
  other arithmetic  5.71 us (4%)
    unnamed x24, local copies, waits for them, and re-layouts  16.2 us
    ppermute x12, starting transfers between devices, over_img(): return lax.ppermute(a, 'img', perm)  14.7 us
    ppermute x12, waiting for transfers between devices, over_img(): return lax.ppermute(a, 'img', perm)  14.1 us
    ppermute x7, waiting for transfers between devices, over_phr(): return lax.ppermute(a, 'phr', phr_perm(lambda y, z: (y ^ dy, z ^ dz)))  13.7 us
    pallas_call x2, Pallas kernels, region_call(): call(region_kernel, [SCALAR] * 2 + [WHOLE] * len(arrays), [((8, rows, 128...  11 us
    pallas_call x2, Pallas kernels, phrase_call(): call(lambda *refs: phrase_kernel(base, *refs), [SCALAR] + [WHOLE] * len(a...  10.1 us
    ppermute x7, starting transfers between devices, over_phr(): return lax.ppermute(a, 'phr', phr_perm(lambda y, z: (y ^ dy, z ^ dz)))  9.91 us
    pallas_call x1, Pallas kernels, first_scores_call(): call(first_scores_kernel, [SCALAR, HBM, HBM], [((half, rows), jnp.float32...  9.8 us
  transfers between devices with their start and end apart: 20, of which 8 were waited for; matrix products, arithmetic and copies ran while one was open for 5% of the time, Pallas kernels for 25%

profile of v2, /device:TPU:0, one launch (start us, length us, event | category | flops | bytes accessed | tf_op | source)
XLA Modules:
  0.0 128.0 jit_solution(5858175033388015816)
XLA Ops:
  0.7 0.7 broadcast_compare_fusion
  1.5 0.7 broadcast_compare_fusion.2
  2.2 0.5 collective-permute-start.1
  2.8 9.8 %first_scores.1 = (f32[2048,1024]{1,0:T(8,128)S(1)}, f32[8,1,1024]{2,1,0:T(1,128)S(1)}, f32[8,1,1024]{2,1,0:T(1,128)S(1)}, bf16[2048,1024]{1,0:T(8,128)(2,1)S(1)}, bf16[1024,1024]{1,0:T(8,128)(2,1)S(1)}) custom-call(s32[8]{0:T(128)S(1)} %stack.50.blk, bf16[4096,1024]{1,0:T(8,128)(2,1)} %p_hbm.1, bf16[1024,1024]{1,0:T(8,128)(2,1)} %r_hbm.1), custom_call_target="tpu_custom_call" | custom-call | flops 4294967296 | bytes 1048576 | tf_op jit(solution)/shard_map/first_scores/pallas_call | solution.py:105
  12.6 3.3 %copy-done = f32[2048,1024]{1,0:T(8,128)} copy-done((f32[2048,1024]{1,0:T(8,128)}, f32[2048,1024]{1,0:T(8,128)S(1)}, u32[]{:S(2)}) %copy-start) | copy-done | bytes 8388632
  15.9 1.4 %copy-done.4 = bf16[1024,1024]{1,0:T(8,128)(2,1)} copy-done((bf16[1024,1024]{1,0:T(8,128)(2,1)}, bf16[1024,1024]{1,0:T(8,128)(2,1)S(1)}, u32[]{:S(2)}) %copy-start.4) | copy-done | bytes 2097176
  17.3 5.7 %scores.1 = (f32[2048,1024]{1,0:T(8,128)S(1)}, f32[8,1,1024]{2,1,0:T(1,128)S(1)}, f32[8,1,1024]{2,1,0:T(1,128)S(1)}) custom-call(bf16[2048,1024]{1,0:T(8,128)(2,1)S(1)} %get-tuple-element.20.phrases, bf16[1024,1024]{1,0:T(8,128)(2,1)S(1)} %collective-permute-done.regions.refs_8_), custom_call_target="tpu_custom_call" | custom-call | flops 4294967296 | bytes 1048576 | tf_op jit(solution)/shard_map/scores/pallas_call | solution.py:130
  23.0 3.2 %copy-done.2 = f32[2048,1024]{1,0:T(8,128)} copy-done((f32[2048,1024]{1,0:T(8,128)}, f32[2048,1024]{1,0:T(8,128)S(1)}, u32[]{:S(2)}) %copy-start.2) | copy-done | bytes 8388632
  26.3 0.2 fusion.23
  26.5 0.2 rev.3
  26.8 0.8 broadcast_in_dim.55
  27.6 6.7 %all-to-all-start = ((f32[16,2,2,1024]{3,2,1,0:T(2,128)}), f32[16,2,2,1024]{3,2,1,0:T(2,128)S(1)}, u32[]{:S(2)}, u32[]{:S(2)}) async-start(f32[16,2,2,1024]{3,2,1,0:T(2,128)} %bitcast.15), calls=%async_computation | async-start | bytes 524288 | tf_op jit(solution)/shard_map/all_to_all | solution.py:234
  34.4 7.8 %all-to-all-done = f32[16,2,2,1024]{3,2,1,0:T(2,128)S(1)} async-done(((f32[16,2,2,1024]{3,2,1,0:T(2,128)}), f32[16,2,2,1024]{3,2,1,0:T(2,128)S(1)}, u32[]{:S(2)}, u32[]{:S(2)}) %all-to-all-start) | async-done | bytes 262176 | tf_op jit(solution)/shard_map/all_to_all | solution.py:234
  42.6 3.4 %copy-done.1 = f32[2048,1024]{1,0:T(8,128)S(1)} copy-done((f32[2048,1024]{1,0:T(8,128)S(1)}, f32[2048,1024]{1,0:T(8,128)}, u32[]{:S(2)}) %copy-start.1) | copy-done | bytes 8388632
  45.9 3.4 %copy-done.3 = f32[2048,1024]{1,0:T(8,128)S(1)} copy-done((f32[2048,1024]{1,0:T(8,128)S(1)}, f32[2048,1024]{1,0:T(8,128)}, u32[]{:S(2)}) %copy-start.3) | copy-done | bytes 8388632
  49.3 1.6 %copy-done.5 = bf16[1024,1024]{1,0:T(8,128)(2,1)S(1)} copy-done((bf16[1024,1024]{1,0:T(8,128)(2,1)S(1)}, bf16[1024,1024]{1,0:T(8,128)(2,1)}, u32[]{:S(2)}) %copy-start.5) | copy-done | bytes 2097176
  50.9 5.1 %phrase_part.3 = (bf16[2,256,512]{2,1,0:T(8,128)(2,1)S(1)}, bf16[2,256,512]{2,1,0:T(8,128)(2,1)S(1)}, f32[2,256,512]{2,1,0:T(8,128)S(1)}, f32[2,256,512]{2,1,0:T(8,128)S(1)}) custom-call(s32[8]{0:T(128)S(1)} %multiply_add_fusion.1.off.refs_0_, f32[2048,1024]{1,0:T(8,128)S(1)} %copy-done.1, f32[2048,1024]{1,0:T(8,128)S(1)} %copy-done.3, ...), custom_call_target="tpu_custom_call" | custom-call | flops 4294967296 | bytes 1048576 | tf_op jit(solution)/shard_map/phrase_part/pallas_call | solution.py:171
  56.0 1.6 %collective-permute-start.14 = (bf16[2,256,512]{2,1,0:T(8,128)(2,1)S(1)}, bf16[2,256,512]{2,1,0:T(8,128)(2,1)S(1)}, u32[]{:S(2)}, u32[]{:S(2)}) collective-permute-start(bf16[2,256,512]{2,1,0:T(8,128)(2,1)S(1)} %get-tuple-element.31), channel_id=1, source_target_pairs={{0,16},{8,24},{16,0},{24,8},{32,48},{40,56},{48,32},{56,40},{64,80... | collective-permute-start | bytes 1572872 | tf_op jit(solution)/shard_map/ppermute | solution.py:43
  57.6 2.2 %collective-permute-start.16 = (bf16[2,256,512]{2,1,0:T(8,128)(2,1)S(1)}, bf16[2,256,512]{2,1,0:T(8,128)(2,1)S(1)}, u32[]{:S(2)}, u32[]{:S(2)}) collective-permute-start(bf16[2,256,512]{2,1,0:T(8,128)(2,1)S(1)} %get-tuple-element.33), channel_id=1, source_target_pairs={{0,48},{8,56},{16,32},{24,40},{32,16},{40,24},{48,0},{56,8},{64,11... | collective-permute-start | bytes 1572872 | tf_op jit(solution)/shard_map/ppermute | solution.py:43
  59.8 5.1 %phrase_part.2 = (bf16[2,256,512]{2,1,0:T(8,128)(2,1)S(1)}, bf16[2,256,512]{2,1,0:T(8,128)(2,1)S(1)}, f32[2,256,512]{2,1,0:T(8,128)S(1)}, f32[2,256,512]{2,1,0:T(8,128)S(1)}) custom-call(s32[8]{0:T(128)S(1)} %multiply_add_fusion.1.off.refs_0_, f32[2048,1024]{1,0:T(8,128)S(1)} %copy-done.1, f32[2048,1024]{1,0:T(8,128)S(1)} %copy-done.3, ...), custom_call_target="tpu_custom_call" | custom-call | flops 4294967296 | bytes 1048576 | tf_op jit(solution)/shard_map/phrase_part/pallas_call | solution.py:171
  64.8 0.7 collective-permute-start.10
  65.5 0.9 collective-permute-start.12
  66.4 5.4 %region_part.3 = bf16[8,1024,128]{2,1,0:T(8,128)(2,1)S(1)} custom-call(s32[1]{0:T(128)} %bitcast.phr, s32[8]{0:T(128)S(1)} %multiply_add_fusion.1.off.refs_0_, f32[2048,1024]{1,0:T(8,128)S(1)} %bitcast.100, f32[8,1,1024]{2,1,0:T(1,128)S(1)} %broadcast_select_fusion.s.refs_4_, s32[1,1024]{1,0:T(1,128)S(1)} %bitcast.110, bf16[2048,1024]{1,0:T(8,128)(2,1)S(1)} %copy-done.7), custom_call_target="tpu_custom_call" | custom-call | flops 4294967296 | bytes 1048576 | tf_op jit(solution)/shard_map/region_part/pallas_call | solution.py:202
  71.9 5.5 %region_part.2 = f32[8,1024,128]{2,1,0:T(8,128)S(1)} custom-call(s32[1]{0:T(128)} %bitcast.phr, s32[8]{0:T(128)S(1)} %multiply_add_fusion.1.off.refs_0_, f32[2048,1024]{1,0:T(8,128)S(1)} %bitcast.98, f32[8,1,1024]{2,1,0:T(1,128)S(1)} %broadcast_select_fusion.1.s.refs_3_, s32[1,1024]{1,0:T(1,128)S(1)} %bitcast.107, bf16[2048,1024]{1,0:T(8,128)(2,1)S(1)} %copy-done.7), custom_call_target="tpu_custom_call" | custom-call | flops 4294967296 | bytes 1048576 | tf_op jit(solution)/shard_map/region_part/pallas_call | solution.py:202
  77.5 0.2 convert_add_fusion.2
  77.7 2.4 %collective-permute-start.15 = (bf16[256,512]{1,0:T(8,128)(2,1)S(1)}, bf16[256,512]{1,0:T(8,128)(2,1)S(1)}, u32[]{:S(2)}, u32[]{:S(2)}) collective-permute-start(bf16[256,512]{1,0:T(8,128)(2,1)S(1)} %fusion.17), channel_id=1, source_target_pairs={{0,48},{8,56},{16,32},{24,40},{32,16},{40,24},{48,0},{56,8},{64,11... | collective-permute-start | bytes 786440 | tf_op jit(solution)/shard_map/ppermute | solution.py:43
  80.1 0.2 convert_add_fusion.1
  80.4 0.3 collective-permute-start.17
  80.7 0.7 collective-permute-done.10
  81.4 0.2 convert_add_fusion.4
  81.6 2.8 %collective-permute-start.11 = (bf16[256,512]{1,0:T(8,128)(2,1)S(1)}, bf16[256,512]{1,0:T(8,128)(2,1)S(1)}, u32[]{:S(2)}, u32[]{:S(2)}) collective-permute-start(bf16[256,512]{1,0:T(8,128)(2,1)S(1)} %fusion.15), channel_id=1, source_target_pairs={{0,48},{8,56},{16,32},{24,40},{32,16},{40,24},{48,0},{56,8},{64,11... | collective-permute-start | bytes 786440 | tf_op jit(solution)/shard_map/ppermute | solution.py:43
  84.5 0.4 collective-permute-done.12
  84.9 0.2 convert_add_fusion.3
  85.1 0.2 collective-permute-start.13
  85.3 5.2 %collective-permute-done.15 = bf16[256,512]{1,0:T(8,128)(2,1)S(1)} collective-permute-done((bf16[256,512]{1,0:T(8,128)(2,1)S(1)}, bf16[256,512]{1,0:T(8,128)(2,1)S(1)}, u32[]{:S(2)}, u32[]{:S(2)}) %collective-permute-start.15) | collective-permute-done | bytes 262176 | tf_op jit(solution)/shard_map/ppermute | solution.py:43
  90.8 3.0 %collective-permute-start.18 = (bf16[256,1024]{1,0:T(8,128)(2,1)S(1)}, bf16[256,1024]{1,0:T(8,128)(2,1)S(1)}, u32[]{:S(2)}, u32[]{:S(2)}) collective-permute-start(bf16[256,1024]{1,0:T(8,128)(2,1)S(1)} %pad_maximum_fusion), channel_id=1, source_target_pairs={{0,64},{8,72},{16,80},{24,88},{32,96},{40,104},{48,112},{56,120},{... | collective-permute-start | bytes 1572872 | tf_op jit(solution)/shard_map/ppermute | solution.py:43
  93.7 0.7 fusion.25
  94.5 0.6 collective-permute-start.3
  95.1 1.5 %collective-permute-start.4 = (bf16[1024,128]{1,0:T(8,128)(2,1)S(1)}, bf16[1024,128]{1,0:T(8,128)(2,1)S(1)}, u32[]{:S(2)}, u32[]{:S(2)}) collective-permute-start(bf16[1024,128]{1,0:T(8,128)(2,1)S(1)} %get-tuple-element.44), channel_id=1, source_target_pairs={{0,2},{1,3},{2,0},{3,1},{4,6},{5,7},{6,4},{7,5},{8,10},{9,11},{10,... | collective-permute-start | bytes 786440 | tf_op jit(solution)/shard_map/ppermute | solution.py:47
  96.8 2.7 %collective-permute-start.5 = (bf16[1024,128]{1,0:T(8,128)(2,1)S(1)}, bf16[1024,128]{1,0:T(8,128)(2,1)S(1)}, u32[]{:S(2)}, u32[]{:S(2)}) collective-permute-start(bf16[1024,128]{1,0:T(8,128)(2,1)S(1)} %get-tuple-element.43), channel_id=1, source_target_pairs={{0,3},{1,2},{2,1},{3,0},{4,7},{5,6},{6,5},{7,4},{8,11},{9,10},{10,... | collective-permute-start | bytes 786440 | tf_op jit(solution)/shard_map/ppermute | solution.py:47
  99.5 7.7 %collective-permute-done.18 = bf16[256,1024]{1,0:T(8,128)(2,1)S(1)} collective-permute-done((bf16[256,1024]{1,0:T(8,128)(2,1)S(1)}, bf16[256,1024]{1,0:T(8,128)(2,1)S(1)}, u32[]{:S(2)}, u32[]{:S(2)}) %collective-permute-start.18) | collective-permute-done | bytes 524320 | tf_op jit(solution)/shard_map/ppermute | solution.py:43
  107.2 2.9 %collective-permute-start.8 = (bf16[1024,128]{1,0:T(8,128)(2,1)S(1)}, bf16[1024,128]{1,0:T(8,128)(2,1)S(1)}, u32[]{:S(2)}, u32[]{:S(2)}) collective-permute-start(bf16[1024,128]{1,0:T(8,128)(2,1)S(1)} %get-tuple-element.40), channel_id=1, source_target_pairs={{0,6},{1,7},{2,4},{3,5},{4,2},{5,3},{6,0},{7,1},{8,14},{9,15},{10,... | collective-permute-start | bytes 786440 | tf_op jit(solution)/shard_map/ppermute | solution.py:47
  110.2 2.1 %collective-permute-start.9 = (bf16[1024,128]{1,0:T(8,128)(2,1)S(1)}, bf16[1024,128]{1,0:T(8,128)(2,1)S(1)}, u32[]{:S(2)}, u32[]{:S(2)}) collective-permute-start(bf16[1024,128]{1,0:T(8,128)(2,1)S(1)} %get-tuple-element.39), channel_id=1, source_target_pairs={{0,7},{1,6},{2,5},{3,4},{4,3},{5,2},{6,1},{7,0},{8,15},{9,14},{10,... | collective-permute-start | bytes 786440 | tf_op jit(solution)/shard_map/ppermute | solution.py:47
  112.3 0.9 fusion
  113.3 4.1 %collective-permute-done.7 = bf16[1024,128]{1,0:T(8,128)(2,1)S(1)} collective-permute-done((bf16[1024,128]{1,0:T(8,128)(2,1)S(1)}, bf16[1024,128]{1,0:T(8,128)(2,1)S(1)}, u32[]{:S(2)}, u32[]{:S(2)}) %collective-permute-start.7) | collective-permute-done | bytes 262176 | tf_op jit(solution)/shard_map/ppermute | solution.py:47
  117.3 6.5 %collective-permute-done.8 = bf16[1024,128]{1,0:T(8,128)(2,1)S(1)} collective-permute-done((bf16[1024,128]{1,0:T(8,128)(2,1)S(1)}, bf16[1024,128]{1,0:T(8,128)(2,1)S(1)}, u32[]{:S(2)}, u32[]{:S(2)}) %collective-permute-start.8) | collective-permute-done | bytes 262176 | tf_op jit(solution)/shard_map/ppermute | solution.py:47
  123.9 3.1 %collective-permute-done.9 = bf16[1024,128]{1,0:T(8,128)(2,1)S(1)} collective-permute-done((bf16[1024,128]{1,0:T(8,128)(2,1)S(1)}, bf16[1024,128]{1,0:T(8,128)(2,1)S(1)}, u32[]{:S(2)}, u32[]{:S(2)}) %collective-permute-start.9) | collective-permute-done | bytes 262176 | tf_op jit(solution)/shard_map/ppermute | solution.py:47
  127.0 1.0 fusion.14
  (60 shorter events, 1.6 us)
Async XLA Ops:
  0.6 16.7 %collective-permute-start = (bf16[1024,1024]{1,0:T(8,128)(2,1)}, bf16[1024,1024]{1,0:T(8,128)(2,1)S(1)}, u32[]{:S(2)}, u32[]{:S(2)}) collective-permute-start(bf16[1024,1024]{1,0:T(8,128)(2,1)} %r_hbm.1), channel_id=1, source_target_pairs={{0,8},{8,0},{16,24},{24,16},{32,40},{40,32},{48,56},{56,48},{64,72... | collective-permute-start | bytes 6291464 | tf_op jit(solution)/shard_map/ppermute | solution.py:43
  2.2 32.1 %collective-permute-start.1 = (s32[1024]{0:T(1024)S(1)}, s32[1024]{0:T(1024)S(1)}, u32[]{:S(2)}, u32[]{:S(2)}) collective-permute-start(s32[1024]{0:T(1024)S(1)} %get-tuple-element.37), channel_id=1, source_target_pairs={{0,8},{8,0},{16,24},{24,16},{32,40},{40,32},{48,56},{56,48},{64,72... | collective-permute-start | bytes 12296 | tf_op jit(solution)/shard_map/ppermute | solution.py:43
  12.6 3.3 %copy-start = (f32[2048,1024]{1,0:T(8,128)}, f32[2048,1024]{1,0:T(8,128)S(1)}, u32[]{:S(2)}) copy-start(f32[2048,1024]{1,0:T(8,128)S(1)} %get-tuple-element.18.e.refs_1_) | copy-start | bytes 25165828
  15.9 1.4 %copy-start.4 = (bf16[1024,1024]{1,0:T(8,128)(2,1)}, bf16[1024,1024]{1,0:T(8,128)(2,1)S(1)}, u32[]{:S(2)}) copy-start(bf16[1024,1024]{1,0:T(8,128)(2,1)S(1)} %get-tuple-element.25.refs_7_) | copy-start | bytes 6291460
  17.3 5.7 %copy-start.6 = (bf16[2048,1024]{1,0:T(8,128)(2,1)}, bf16[2048,1024]{1,0:T(8,128)(2,1)S(1)}, u32[]{:S(2)}) copy-start(bf16[2048,1024]{1,0:T(8,128)(2,1)S(1)} %get-tuple-element.20.phrases) | copy-start | bytes 12582916
  23.0 3.2 %copy-start.2 = (f32[2048,1024]{1,0:T(8,128)}, f32[2048,1024]{1,0:T(8,128)S(1)}, u32[]{:S(2)}) copy-start(f32[2048,1024]{1,0:T(8,128)S(1)} %get-tuple-element.24.e.refs_2_) | copy-start | bytes 25165828
  27.6 14.6 %all-to-all-start = ((f32[16,2,2,1024]{3,2,1,0:T(2,128)}), f32[16,2,2,1024]{3,2,1,0:T(2,128)S(1)}, u32[]{:S(2)}, u32[]{:S(2)}) async-start(f32[16,2,2,1024]{3,2,1,0:T(2,128)} %bitcast.15), calls=%async_computation | async-start | bytes 524288 | tf_op jit(solution)/shard_map/all_to_all | solution.py:234
  42.6 3.4 %copy-start.1 = (f32[2048,1024]{1,0:T(8,128)S(1)}, f32[2048,1024]{1,0:T(8,128)}, u32[]{:S(2)}) copy-start(f32[2048,1024]{1,0:T(8,128)} %copy-done) | copy-start | bytes 25165828
  45.9 3.4 %copy-start.3 = (f32[2048,1024]{1,0:T(8,128)S(1)}, f32[2048,1024]{1,0:T(8,128)}, u32[]{:S(2)}) copy-start(f32[2048,1024]{1,0:T(8,128)} %copy-done.2) | copy-start | bytes 25165828
  49.3 1.6 %copy-start.5 = (bf16[1024,1024]{1,0:T(8,128)(2,1)S(1)}, bf16[1024,1024]{1,0:T(8,128)(2,1)}, u32[]{:S(2)}) copy-start(bf16[1024,1024]{1,0:T(8,128)(2,1)} %copy-done.4) | copy-start | bytes 6291460
  50.9 21.0 %slice-start = ((s8[8388608]{0:T(1024)(128)(4,1)}), s8[4194304]{0:T(1024)(128)(4,1)S(1)}, s32[]{:S(2)}) async-start(s8[8388608]{0:T(1024)(128)(4,1)} %bitcast.97), calls=%async_computation.1 | async-start | bytes 8388608
  56.0 21.5 %collective-permute-start.14 = (bf16[2,256,512]{2,1,0:T(8,128)(2,1)S(1)}, bf16[2,256,512]{2,1,0:T(8,128)(2,1)S(1)}, u32[]{:S(2)}, u32[]{:S(2)}) collective-permute-start(bf16[2,256,512]{2,1,0:T(8,128)(2,1)S(1)} %get-tuple-element.31), channel_id=1, source_target_pairs={{0,16},{8,24},{16,0},{24,8},{32,48},{40,56},{48,32},{56,40},{64,80... | collective-permute-start | bytes 1572872 | tf_op jit(solution)/shard_map/ppermute | solution.py:43
  57.6 8.8 %slice-start.2 = ((s8[8388608]{0:T(1024)(128)(4,1)}), s8[4194304]{0:T(1024)(128)(4,1)S(1)}, s32[]{:S(2)}) async-start(s8[8388608]{0:T(1024)(128)(4,1)} %bitcast.99), calls=%async_computation.3 | async-start | bytes 8388608
  57.6 8.8 %slice-start.3 = ((s8[8388608]{0:T(1024)(128)(4,1)}), s8[4194304]{0:T(1024)(128)(4,1)S(1)}, s32[]{:S(2)}) async-start(s8[8388608]{0:T(1024)(128)(4,1)} %bitcast.99), calls=%async_computation.4 | async-start | bytes 8388608
  57.6 8.8 %copy-start.7 = (bf16[2048,1024]{1,0:T(8,128)(2,1)S(1)}, bf16[2048,1024]{1,0:T(8,128)(2,1)}, u32[]{:S(2)}) copy-start(bf16[2048,1024]{1,0:T(8,128)(2,1)} %copy-done.6) | copy-start | bytes 12582916
  57.6 14.3 %slice-start.1 = ((s8[8388608]{0:T(1024)(128)(4,1)}), s8[4194304]{0:T(1024)(128)(4,1)S(1)}, s32[]{:S(2)}) async-start(s8[8388608]{0:T(1024)(128)(4,1)} %bitcast.97), calls=%async_computation.2 | async-start | bytes 8388608
  57.6 22.5 %collective-permute-start.16 = (bf16[2,256,512]{2,1,0:T(8,128)(2,1)S(1)}, bf16[2,256,512]{2,1,0:T(8,128)(2,1)S(1)}, u32[]{:S(2)}, u32[]{:S(2)}) collective-permute-start(bf16[2,256,512]{2,1,0:T(8,128)(2,1)S(1)} %get-tuple-element.33), channel_id=1, source_target_pairs={{0,48},{8,56},{16,32},{24,40},{32,16},{40,24},{48,0},{56,8},{64,11... | collective-permute-start | bytes 1572872 | tf_op jit(solution)/shard_map/ppermute | solution.py:43
  64.8 16.6 %collective-permute-start.10 = (bf16[2,256,512]{2,1,0:T(8,128)(2,1)S(1)}, bf16[2,256,512]{2,1,0:T(8,128)(2,1)S(1)}, u32[]{:S(2)}, u32[]{:S(2)}) collective-permute-start(bf16[2,256,512]{2,1,0:T(8,128)(2,1)S(1)} %get-tuple-element.27), channel_id=1, source_target_pairs={{0,16},{8,24},{16,0},{24,8},{32,48},{40,56},{48,32},{56,40},{64,80... | collective-permute-start | bytes 1572872 | tf_op jit(solution)/shard_map/ppermute | solution.py:43
  65.5 19.4 %collective-permute-start.12 = (bf16[2,256,512]{2,1,0:T(8,128)(2,1)S(1)}, bf16[2,256,512]{2,1,0:T(8,128)(2,1)S(1)}, u32[]{:S(2)}, u32[]{:S(2)}) collective-permute-start(bf16[2,256,512]{2,1,0:T(8,128)(2,1)S(1)} %get-tuple-element.29), channel_id=1, source_target_pairs={{0,48},{8,56},{16,32},{24,40},{32,16},{40,24},{48,0},{56,8},{64,11... | collective-permute-start | bytes 1572872 | tf_op jit(solution)/shard_map/ppermute | solution.py:43
  71.8 21.9 %collective-permute-start.2 = (bf16[8,1024,128]{2,1,0:T(8,128)(2,1)S(1)}, bf16[8,1024,128]{2,1,0:T(8,128)(2,1)S(1)}, u32[]{:S(2)}, u32[]{:S(2)}) collective-permute-start(bf16[8,1024,128]{2,1,0:T(8,128)(2,1)S(1)} %region_part.3), channel_id=1, source_target_pairs={{0,8},{8,0},{16,24},{24,16},{32,40},{40,32},{48,56},{56,48},{64,72... | collective-permute-start | bytes 6291464 | tf_op jit(solution)/shard_map/ppermute | solution.py:43
  77.7 12.8 %collective-permute-start.15 = (bf16[256,512]{1,0:T(8,128)(2,1)S(1)}, bf16[256,512]{1,0:T(8,128)(2,1)S(1)}, u32[]{:S(2)}, u32[]{:S(2)}) collective-permute-start(bf16[256,512]{1,0:T(8,128)(2,1)S(1)} %fusion.17), channel_id=1, source_target_pairs={{0,48},{8,56},{16,32},{24,40},{32,16},{40,24},{48,0},{56,8},{64,11... | collective-permute-start | bytes 786440 | tf_op jit(solution)/shard_map/ppermute | solution.py:43
  80.4 10.2 %collective-permute-start.17 = (bf16[256,512]{1,0:T(8,128)(2,1)S(1)}, bf16[256,512]{1,0:T(8,128)(2,1)S(1)}, u32[]{:S(2)}, u32[]{:S(2)}) collective-permute-start(bf16[256,512]{1,0:T(8,128)(2,1)S(1)} %fusion.18), channel_id=1, source_target_pairs={{0,16},{8,24},{16,0},{24,8},{32,48},{40,56},{48,32},{56,40},{64,80... | collective-permute-start | bytes 786440 | tf_op jit(solution)/shard_map/ppermute | solution.py:43
  81.6 15.1 %collective-permute-start.11 = (bf16[256,512]{1,0:T(8,128)(2,1)S(1)}, bf16[256,512]{1,0:T(8,128)(2,1)S(1)}, u32[]{:S(2)}, u32[]{:S(2)}) collective-permute-start(bf16[256,512]{1,0:T(8,128)(2,1)S(1)} %fusion.15), channel_id=1, source_target_pairs={{0,48},{8,56},{16,32},{24,40},{32,16},{40,24},{48,0},{56,8},{64,11... | collective-permute-start | bytes 786440 | tf_op jit(solution)/shard_map/ppermute | solution.py:43
  85.1 14.4 %collective-permute-start.13 = (bf16[256,512]{1,0:T(8,128)(2,1)S(1)}, bf16[256,512]{1,0:T(8,128)(2,1)S(1)}, u32[]{:S(2)}, u32[]{:S(2)}) collective-permute-start(bf16[256,512]{1,0:T(8,128)(2,1)S(1)} %fusion.16), channel_id=1, source_target_pairs={{0,16},{8,24},{16,0},{24,8},{32,48},{40,56},{48,32},{56,40},{64,80... | collective-permute-start | bytes 786440 | tf_op jit(solution)/shard_map/ppermute | solution.py:43
  90.8 16.4 %collective-permute-start.18 = (bf16[256,1024]{1,0:T(8,128)(2,1)S(1)}, bf16[256,1024]{1,0:T(8,128)(2,1)S(1)}, u32[]{:S(2)}, u32[]{:S(2)}) collective-permute-start(bf16[256,1024]{1,0:T(8,128)(2,1)S(1)} %pad_maximum_fusion), channel_id=1, source_target_pairs={{0,64},{8,72},{16,80},{24,88},{32,96},{40,104},{48,112},{56,120},{... | collective-permute-start | bytes 1572872 | tf_op jit(solution)/shard_map/ppermute | solution.py:43
  94.5 12.7 %collective-permute-start.3 = (bf16[1024,128]{1,0:T(8,128)(2,1)S(1)}, bf16[1024,128]{1,0:T(8,128)(2,1)S(1)}, u32[]{:S(2)}, u32[]{:S(2)}) collective-permute-start(bf16[1024,128]{1,0:T(8,128)(2,1)S(1)} %get-tuple-element.38), channel_id=1, source_target_pairs={{0,1},{1,0},{2,3},{3,2},{4,5},{5,4},{6,7},{7,6},{8,9},{9,8},{10,11... | collective-permute-start | bytes 786440 | tf_op jit(solution)/shard_map/ppermute | solution.py:47
  95.1 15.0 %collective-permute-start.4 = (bf16[1024,128]{1,0:T(8,128)(2,1)S(1)}, bf16[1024,128]{1,0:T(8,128)(2,1)S(1)}, u32[]{:S(2)}, u32[]{:S(2)}) collective-permute-start(bf16[1024,128]{1,0:T(8,128)(2,1)S(1)} %get-tuple-element.44), channel_id=1, source_target_pairs={{0,2},{1,3},{2,0},{3,1},{4,6},{5,7},{6,4},{7,5},{8,10},{9,11},{10,... | collective-permute-start | bytes 786440 | tf_op jit(solution)/shard_map/ppermute | solution.py:47
  96.8 16.5 %collective-permute-start.5 = (bf16[1024,128]{1,0:T(8,128)(2,1)S(1)}, bf16[1024,128]{1,0:T(8,128)(2,1)S(1)}, u32[]{:S(2)}, u32[]{:S(2)}) collective-permute-start(bf16[1024,128]{1,0:T(8,128)(2,1)S(1)} %get-tuple-element.43), channel_id=1, source_target_pairs={{0,3},{1,2},{2,1},{3,0},{4,7},{5,6},{6,5},{7,4},{8,11},{9,10},{10,... | collective-permute-start | bytes 786440 | tf_op jit(solution)/shard_map/ppermute | solution.py:47
  99.5 13.8 %collective-permute-start.6 = (bf16[1024,128]{1,0:T(8,128)(2,1)S(1)}, bf16[1024,128]{1,0:T(8,128)(2,1)S(1)}, u32[]{:S(2)}, u32[]{:S(2)}) collective-permute-start(bf16[1024,128]{1,0:T(8,128)(2,1)S(1)} %get-tuple-element.42), channel_id=1, source_target_pairs={{0,4},{1,5},{2,6},{3,7},{4,0},{5,1},{6,2},{7,3},{8,12},{9,13},{10,... | collective-permute-start | bytes 786440 | tf_op jit(solution)/shard_map/ppermute | solution.py:47
  107.2 10.1 %collective-permute-start.7 = (bf16[1024,128]{1,0:T(8,128)(2,1)S(1)}, bf16[1024,128]{1,0:T(8,128)(2,1)S(1)}, u32[]{:S(2)}, u32[]{:S(2)}) collective-permute-start(bf16[1024,128]{1,0:T(8,128)(2,1)S(1)} %get-tuple-element.41), channel_id=1, source_target_pairs={{0,5},{1,4},{2,7},{3,6},{4,1},{5,0},{6,3},{7,2},{8,13},{9,12},{10,... | collective-permute-start | bytes 786440 | tf_op jit(solution)/shard_map/ppermute | solution.py:47
  107.2 16.6 %collective-permute-start.8 = (bf16[1024,128]{1,0:T(8,128)(2,1)S(1)}, bf16[1024,128]{1,0:T(8,128)(2,1)S(1)}, u32[]{:S(2)}, u32[]{:S(2)}) collective-permute-start(bf16[1024,128]{1,0:T(8,128)(2,1)S(1)} %get-tuple-element.40), channel_id=1, source_target_pairs={{0,6},{1,7},{2,4},{3,5},{4,2},{5,3},{6,0},{7,1},{8,14},{9,15},{10,... | collective-permute-start | bytes 786440 | tf_op jit(solution)/shard_map/ppermute | solution.py:47
  110.2 16.8 %collective-permute-start.9 = (bf16[1024,128]{1,0:T(8,128)(2,1)S(1)}, bf16[1024,128]{1,0:T(8,128)(2,1)S(1)}, u32[]{:S(2)}, u32[]{:S(2)}) collective-permute-start(bf16[1024,128]{1,0:T(8,128)(2,1)S(1)} %get-tuple-element.39), channel_id=1, source_target_pairs={{0,7},{1,6},{2,5},{3,4},{4,3},{5,2},{6,1},{7,0},{8,15},{9,14},{10,... | collective-permute-start | bytes 786440 | tf_op jit(solution)/shard_map/ppermute | solution.py:47

commit v3 on v2

v3 whole, which is shorter than its diff:
```python
import math

import jax
import jax.numpy as jnp
from jax import lax
from jax.experimental import pallas as pl
from jax.experimental.pallas import tpu as pltpu
from jax.sharding import PartitionSpec as P

logit_scale = 2.0
log2e = math.log2(math.e)
BLK = 256
ORDER = (2, 1, 3, 0)
VMEM = 8 * 1024 * 1024


def img_perm(f):
    pairs = []
    for y in range(2):
        for x in range(4):
            for c in range(2):
                y2, x2, c2 = f(y, x, c)
                pairs.append(((y * 4 + x) * 2 + c, (y2 * 4 + x2) * 2 + c2))
    return pairs


def phr_perm(f):
    pairs = []
    for y in range(2):
        for z in range(4):
            y2, z2 = f(y, z)
            pairs.append((y * 4 + z, y2 * 4 + z2))
    return pairs


CORE = img_perm(lambda y, x, c: (y, x, 1 - c))
X1 = img_perm(lambda y, x, c: (y, x ^ 1, c))
X3 = img_perm(lambda y, x, c: (y, x ^ 3, c))
YH = img_perm(lambda y, x, c: (1 - y, x, c))


def over_img(a, perm):
    return lax.ppermute(a, "img", perm)


def over_phr(a, dy, dz):
    return lax.ppermute(a, "phr", phr_perm(lambda y, z: (y ^ dy, z ^ dz)))


def vmem(a):
    return pltpu.with_memory_space_constraint(a, pltpu.VMEM)


WHOLE = pl.BlockSpec(memory_space=pltpu.VMEM)
SCALAR = pl.BlockSpec(memory_space=pltpu.SMEM)
HBM = pl.BlockSpec(memory_space=pltpu.HBM)


def call(body, in_specs, outs, name, **kwargs):
    return pl.pallas_call(
        body,
        in_specs=in_specs,
        out_specs=[WHOLE] * len(outs),
        out_shape=[pltpu.VMEM(*out) for out in outs],
        compiler_params=pltpu.CompilerParams(vmem_limit_bytes=VMEM),
        cost_estimate=pl.CostEstimate(flops=1, bytes_accessed=1, transcendentals=0),
        name=name,
        **kwargs,
    )


def score_block(j, phrases, regions, e, m, l):
    part = pl.ds(j * BLK, BLK)
    s = lax.dot_general(
        phrases[part], regions[...], (((1,), (1,)), ((), ())), preferred_element_type=jnp.float32
    )
    s = s * (logit_scale * log2e)
    top = jnp.max(s, axis=0, keepdims=True)
    value = jnp.exp2(s - top)
    e[part] = value
    m[j] = top
    l[j] = jnp.sum(value, axis=0, keepdims=True)


def block_state(m, l, state):
    tiles = m.shape[0]
    top = m[0]
    for j in range(1, tiles):
        top = jnp.maximum(top, m[j])
    total = l[0] * jnp.exp2(m[0] - top)
    for j in range(1, tiles):
        total += l[j] * jnp.exp2(m[j] - top)
    state[0:1] = top
    state[1:2] = total


def flat_positive(valid, positive):
    boxes = valid.shape[1]
    shape = (boxes, positive.shape[1])
    row = lax.broadcasted_iota(jnp.int32, shape, 0)
    spread = (row == lax.broadcasted_iota(jnp.int32, shape, 1) % boxes).astype(jnp.float32)
    wide = jnp.dot(
        valid[...].astype(jnp.float32), spread, preferred_element_type=jnp.float32
    )
    shape = wide.shape
    row = lax.broadcasted_iota(jnp.int32, shape, 0)
    image = lax.broadcasted_iota(jnp.int32, shape, 1) // boxes
    weight = jnp.sum(jnp.where(row == image, wide, 0.0), axis=0, keepdims=True)
    return jnp.where(weight > 0.5, positive[...], -1)


def first_scores_kernel(
    blk, p_hbm, r_hbm, pos_hbm, valid_hbm, e, m, state, phrases, regions, pos, l, pos_in, valid, sem
):
    tiles = m.shape[0]
    copies = [pltpu.make_async_copy(r_hbm, regions, sem.at[tiles])]
    for j in range(tiles):
        rows = pl.ds(pl.multiple_of(blk[j] * BLK, BLK), BLK)
        copies.append(
            pltpu.make_async_copy(p_hbm.at[rows], phrases.at[pl.ds(j * BLK, BLK)], sem.at[j])
        )
    small = [
        pltpu.make_async_copy(pos_hbm, pos_in, sem.at[tiles + 1]),
        pltpu.make_async_copy(valid_hbm, valid, sem.at[tiles + 2]),
    ]
    for copy in small + copies:
        copy.start()
    for copy in small:
        copy.wait()
    pos[...] = flat_positive(valid, pos_in)
    for copy in copies[:3]:
        copy.wait()
    for j in range(2):
        score_block(j, phrases, regions, e, m, l)
    for copy in copies[3:]:
        copy.wait()
    for j in range(2, tiles):
        score_block(j, phrases, regions, e, m, l)
    block_state(m, l, state)


def first_scores_call(blk, phrases, regions, positive, valid):
    rows, dim = regions.shape
    half = phrases.shape[0] // 2
    tiles = half // BLK
    arrays = (phrases, regions, positive[None], valid)
    return call(
        first_scores_kernel,
        [SCALAR] + [HBM] * 4,
        [
            ((half, rows), jnp.float32),
            ((tiles, 1, rows), jnp.float32),
            ((2, rows), jnp.float32),
            ((half, dim), phrases.dtype),
            ((rows, dim), regions.dtype),
            ((1, rows), jnp.int32),
        ],
        "first_scores",
        scratch_shapes=[
            pltpu.VMEM((tiles, 1, rows), jnp.float32),
            pltpu.VMEM((1, rows), jnp.int32),
            pltpu.VMEM(valid.shape, jnp.int32),
            pltpu.SemaphoreType.DMA((tiles + 3,)),
        ],
    )(blk, *[pltpu.with_memory_space_constraint(a, pltpu.HBM) for a in arrays])


def scores_kernel(phrases, regions, e, m, state, l):
    for j in range(m.shape[0]):
        score_block(j, phrases, regions, e, m, l)
    block_state(m, l, state)


def scores_call(phrases, regions):
    rows, dim = regions.shape
    half = phrases.shape[0]
    tiles = half // BLK
    return call(
        scores_kernel,
        [WHOLE] * 2,
        [
            ((half, rows), jnp.float32),
            ((tiles, 1, rows), jnp.float32),
            ((2, rows), jnp.float32),
        ],
        "scores",
        scratch_shapes=[pltpu.VMEM((tiles, 1, rows), jnp.float32)],
    )(vmem(phrases), vmem(regions))


def coefficients(e, scale, pos, first):
    column = first + lax.broadcasted_iota(jnp.int32, e.shape, 0)
    return (e * scale - (column == pos).astype(jnp.float32)).astype(jnp.bfloat16)


def phrase_kernel(base, off, eo, ep, so, sp, po, pp, ro, rp, send_a, send_b, keep_a, keep_b):
    half = ro.shape[1] // 2
    places = (
        (send_a, 1, send_b, 1),
        (send_a, 0, keep_b, 1),
        (keep_a, 1, send_b, 0),
        (keep_a, 0, keep_b, 0),
    )
    for step, (a, ia, b, ib) in enumerate(places):
        j = base + step
        part = pl.ds(j * BLK, BLK)
        co = coefficients(eo[part], so[j], po[...], off[j])
        cp = coefficients(ep[part], sp[j], pp[...], off[j])
        acc = jnp.dot(co, ro[...], preferred_element_type=jnp.float32)
        acc += jnp.dot(cp, rp[...], preferred_element_type=jnp.float32)
        acc = logit_scale * acc
        a[ia] = acc[:, :half].astype(a.dtype)
        b[ib] = acc[:, half:].astype(b.dtype)


def phrase_call(base, off, *arrays):
    rows, dim = arrays[-1].shape
    shape = (2, BLK, dim // 2)
    return call(
        lambda *refs: phrase_kernel(base, *refs),
        [SCALAR] + [WHOLE] * len(arrays),
        [(shape, jnp.bfloat16)] * 2 + [(shape, jnp.float32)] * 2,
        "phrase_part",
    )(off, *[vmem(a) for a in arrays])


def region_rows(i, off, e, s, pos, phrases):
    lanes = pl.ds(i, BLK)
    coeff = jnp.concatenate(
        [
            coefficients(e[pl.ds(j * BLK, BLK), lanes], s[j, :, lanes], pos[:, lanes], off[j])
            for j in range(s.shape[0])
        ],
        axis=0,
    )
    return logit_scale * lax.dot_general(
        coeff, phrases[...], (((0,), (0,)), ((), ())), preferred_element_type=jnp.float32
    )


def pair_region_kernel(phr, off, e, s, pos, phrases, out):
    for i in range(0, s.shape[2], BLK):
        acc = region_rows(i, off, e, s, pos, phrases)
        for q in range(8):
            out[phr[0] ^ q, pl.ds(i, BLK)] = acc[:, q * 128 : (q + 1) * 128]


def pair_region_call(phr, off, e, s, pos, phrases):
    arrays = (e, s, pos, phrases)
    return call(
        pair_region_kernel,
        [SCALAR] * 2 + [WHOLE] * len(arrays),
        [((8, s.shape[2], 128), jnp.float32)],
        "pair_region_part",
    )(phr, off, *[vmem(a) for a in arrays])[0]


def own_region_kernel(
    phr, off, e, s, pos, phrases, from_pair, send_a, send_b, next_a, next_b, keep, acc
):
    rows = s.shape[2]
    half = rows // 2
    for i in range(0, rows, BLK):
        acc[...] = region_rows(i, off, e, s, pos, phrases)
        here, there = pl.ds(i, BLK), pl.ds(i % half, BLK)
        for k in range(8):
            dy, dz = k // 4, k % 4
            cols = pl.ds(pl.multiple_of((phr[0] ^ k) * 128, 128), 128)
            value = acc[:, cols] + from_pair[k, here]
            if dz == 0:
                keep[dy, here] = value
            elif i < half and dz == 3:
                next_a[dy, there] = value
            elif i < half:
                send_a[dz - 1, dy, there] = value.astype(send_a.dtype)
            elif dz == 1:
                next_b[dy, there] = value
            else:
                send_b[3 - dz, dy, there] = value.astype(send_b.dtype)


def own_region_call(phr, off, e, s, pos, phrases, from_pair):
    rows = s.shape[2]
    half = rows // 2
    arrays = (e, s, pos, phrases, from_pair)
    return call(
        own_region_kernel,
        [SCALAR] * 2 + [WHOLE] * len(arrays),
        [((2, 2, half, 128), jnp.bfloat16)] * 2
        + [((2, half, 128), jnp.float32)] * 2
        + [((2, rows, 128), jnp.float32)],
        "own_region_part",
        scratch_shapes=[pltpu.VMEM((BLK, phrases.shape[1]), jnp.float32)],
    )(phr, off, *[vmem(a) for a in arrays])


def combine(first, second):
    top = jnp.maximum(first[0], second[0])
    total = first[1] * jnp.exp2(first[0] - top) + second[1] * jnp.exp2(second[0] - top)
    return jnp.stack([top, total])


def after(value, *others):
    return lax.optimization_barrier((value, *others))


def region_sum(send_a, send_b, next_a, next_b, keep):
    half = keep.shape[1] // 2
    got_a = over_phr(send_a, 0, 1).astype(jnp.float32)
    got_b = over_phr(send_b, 0, 3).astype(jnp.float32)
    last_a = over_phr((next_a + got_a[1]).astype(jnp.bfloat16), 0, 3).astype(jnp.float32)
    last_b = over_phr((next_b + got_b[1]).astype(jnp.bfloat16), 0, 1).astype(jnp.float32)
    total = jnp.concatenate(
        [keep[:, :half] + got_a[0] + last_a, keep[:, half:] + got_b[0] + last_b], axis=1
    )
    other = over_phr(total[1].astype(jnp.bfloat16), 1, 0).astype(jnp.float32)
    return (total[0] + other).astype(jnp.bfloat16)


def per_device(regions, phrases, positive, valid):
    img, phr = lax.axis_index("img"), lax.axis_index("phr")
    blk = jnp.stack([img ^ (e * 8 + d * 2) for e in (1, 0) for d in ORDER]).astype(jnp.int32)
    off = (phr * phrases.shape[0] + blk * BLK).astype(jnp.int32)
    blk, off, phr_id = after(blk, off, phr.astype(jnp.int32)[None])

    regions_pair = over_img(regions, CORE)
    e_own, m_own, own, phrases, regions, po = first_scores_call(
        blk, phrases, regions, positive, valid
    )
    pp = over_img(po, CORE)
    e_pair, m_pair, pair = scores_call(phrases, regions_pair)

    state = jnp.stack([own, pair], axis=1)
    state = combine(state, over_img(jnp.stack([pair, own], axis=1), CORE))
    for dy, dz in ((1, 0), (0, 1), (0, 3)):
        state = combine(state, over_phr(state, dy, dz))
    lse = state[0] + jnp.log2(state[1])
    s_own = jnp.where(po >= 0, jnp.exp2(m_own - lse[0]), 0.0)
    s_pair = jnp.where(pp >= 0, jnp.exp2(m_pair - lse[1]), 0.0)

    def phrase_half(base, off):
        return phrase_call(
            base, off, e_own, e_pair, s_own, s_pair, po, pp, regions, regions_pair
        )

    def first_step(send_a, send_b, keep_a, keep_b):
        sum_a = keep_a + over_img(send_a, X1).astype(jnp.float32)
        sum_b = keep_b + over_img(send_b, X3).astype(jnp.float32)
        return sum_a[0], sum_b[0], sum_a[1].astype(jnp.bfloat16), sum_b[1].astype(jnp.bfloat16)

    def second_step(sum_a, sum_b, send_a, send_b):
        last_a = over_img(send_a, X3).astype(jnp.float32)
        last_b = over_img(send_b, X1).astype(jnp.float32)
        return jnp.concatenate([sum_a + last_a, sum_b + last_b], axis=1)

    for_pair = pair_region_call(phr_id, off, e_pair, s_pair, pp, phrases)
    for_pair, off = after(for_pair, off)
    from_pair = over_img(for_pair, CORE)
    far = phrase_half(0, off)
    send_a, send_b, off = after(far[0], far[1], off)
    far = first_step(send_a, send_b, *far[2:])
    kept = own_region_call(phr_id, off, e_own, s_own, po, phrases, from_pair)
    send_a, send_b, off = after(kept[0], kept[1], off)
    grad_regions = region_sum(send_a, send_b, *kept[2:])
    near = phrase_half(4, off)
    near = first_step(*near)
    far = second_step(*far)
    near = second_step(*near)
    grad_phrases = near + over_img(far.astype(jnp.bfloat16), YH).astype(jnp.float32)
    return grad_regions, grad_phrases.astype(jnp.bfloat16)


def solution(mesh):
    in_specs = (P("img", None), P("phr", None), P("img"), P("img", None))
    out_specs = (P("img", "phr"), P(("phr", "img"), None))
    return jax.shard_map(
        per_device, mesh=mesh, in_specs=in_specs, out_specs=out_specs, check_vma=False
    )
```

time: 128 us -> 104 us (0.81)
  local copies, waits for them, and re-layouts: 17.7 us -> 0.26 us
  waiting for transfers between devices: 35.7 us -> 33.1 us
  other arithmetic: 5.71 us -> 3.62 us
    unnamed x24 -> x0, local copies, waits for them, and re-layouts: 16.2 us -> none
    ppermute x12 -> x13, waiting for transfers between devices: 14.1 us -> 27.5 us  [over_img(): return lax.ppermute(a, 'img', perm)]
    ppermute x7 -> x8, waiting for transfers between devices: 13.7 us -> 5.52 us  [over_phr(): return lax.ppermute(a, 'phr', phr_perm(lambda y, z: (y ^ dy, z ^ dz)))]
    all_to_all x1 -> x0, waiting for transfers between devices: 7.82 us -> none  [per_device(): lax.all_to_all(sends, ('img', 'phr'), 0, 0, tiled=True, axis_index_groups...]
    all_to_all x1 -> x0, starting transfers between devices: 6.69 us -> none  [per_device(): lax.all_to_all(sends, ('img', 'phr'), 0, 0, tiled=True, axis_index_groups...]
    ppermute x7 -> x8, starting transfers between devices: 9.91 us -> 13.9 us  [over_phr(): return lax.ppermute(a, 'phr', phr_perm(lambda y, z: (y ^ dy, z ^ dz)))]
    ppermute x12 -> x13, starting transfers between devices: 14.7 us -> 16.3 us  [over_img(): return lax.ppermute(a, 'img', perm)]
  transfers between devices with their start and end apart: 20 -> 21, of which waited for: 8 -> 9; matrix products, arithmetic and copies ran while one was open for 5% -> 3% of each run, Pallas kernels for 25% -> 24%
where the time goes in v3:
time: 104 us
  Pallas kernels  35.6 us (34%)
  waiting for transfers between devices  33.1 us (32%)
  starting transfers between devices  30.2 us (29%)
  other arithmetic  3.62 us (3%)
    ppermute x13, waiting for transfers between devices, over_img(): return lax.ppermute(a, 'img', perm)  27.5 us
    ppermute x13, starting transfers between devices, over_img(): return lax.ppermute(a, 'img', perm)  16.3 us
    ppermute x8, starting transfers between devices, over_phr(): return lax.ppermute(a, 'phr', phr_perm(lambda y, z: (y ^ dy, z ^ dz)))  13.9 us
    pallas_call x2, Pallas kernels, phrase_call(): call(lambda *refs: phrase_kernel(base, *refs), [SCALAR] + [WHOLE] * len(a...  10.3 us
    pallas_call x1, Pallas kernels, first_scores_call(): call(first_scores_kernel, [SCALAR] + [HBM] * 4, [((half, rows), jnp.float...  8.32 us
    pallas_call x1, Pallas kernels, own_region_call(): call(own_region_kernel, [SCALAR] * 2 + [WHOLE] * len(arrays), [((2, 2, ha...  6.06 us
    pallas_call x1, Pallas kernels, pair_region_call(): call(pair_region_kernel, [SCALAR] * 2 + [WHOLE] * len(arrays), [((8, s.sh...  5.54 us
    ppermute x8, waiting for transfers between devices, over_phr(): return lax.ppermute(a, 'phr', phr_perm(lambda y, z: (y ^ dy, z ^ dz)))  5.52 us
  transfers between devices with their start and end apart: 21, of which 9 were waited for; matrix products, arithmetic and copies ran while one was open for 3% of the time, Pallas kernels for 24%

profile of v3, /device:TPU:0, one launch (start us, length us, event | category | flops | bytes accessed | tf_op | source)
XLA Modules:
  0.0 103.7 jit_solution(13299394832830020175)
XLA Ops:
  0.6 0.1 collective-permute-start
  0.7 0.1 stack.64.blk
  0.8 8.3 %first_scores.1 = (f32[2048,1024]{1,0:T(8,128)S(1)}, f32[8,1,1024]{2,1,0:T(1,128)S(1)}, f32[2,1024]{1,0:T(2,128)S(1)}, bf16[2048,1024]{1,0:T(8,128)(2,1)S(1)}, b...) custom-call(s32[8]{0:T(128)S(1)} %stack.64.blk, bf16[4096,1024]{1,0:T(8,128)(2,1)} %p_hbm.1, ...), custom_call_target="tpu_custom_call" | custom-call | flops 1 | bytes 1 | tf_op jit(solution)/shard_map/first_scores/pallas_call | solution.py:147
  9.2 5.4 %scores.1 = (f32[2048,1024]{1,0:T(8,128)S(1)}, f32[8,1,1024]{2,1,0:T(1,128)S(1)}, f32[2,1024]{1,0:T(2,128)S(1)}) custom-call(bf16[2048,1024]{1,0:T(8,128)(2,1)S(1)} %get-tuple-element.38.phrases, bf16[1024,1024]{1,0:T(8,128)(2,1)S(1)} %collective-permute-done.regions.refs_8_), custom_call_target="tpu_custom_call" | custom-call | flops 1 | bytes 1 | tf_op jit(solution)/shard_map/scores/pallas_call | solution.py:178
  14.6 0.6 collective-permute-start.2
  15.1 0.8 collective-permute-done.2
  16.0 1.7 %collective-permute-start.3 = (f32[2,2,1024]{2,1,0:T(2,128)S(1)}, f32[2,2,1024]{2,1,0:T(2,128)S(1)}, u32[]{:S(2)}, u32[]{:S(2)}) collective-permute-start(f32[2,2,1024]{2,1,0:T(2,128)S(1)} %pad_maximum_fusion.3), channel_id=1, source_target_pairs={{0,4},{1,5},{2,6},{3,7},{4,0},{5,1},{6,2},{7,3},{8,12},{9,13},{10,... | collective-permute-start | bytes 49160 | tf_op jit(solution)/shard_map/ppermute | solution.py:47
  17.8 2.1 %collective-permute-done.3 = f32[2,2,1024]{2,1,0:T(2,128)S(1)} collective-permute-done((f32[2,2,1024]{2,1,0:T(2,128)S(1)}, f32[2,2,1024]{2,1,0:T(2,128)S(1)}, u32[]{:S(2)}, u32[]{:S(2)}) %collective-permute-start.3) | collective-permute-done | bytes 16416 | tf_op jit(solution)/shard_map/ppermute | solution.py:47
  19.9 2.1 %collective-permute-start.4 = (f32[2,2,1024]{2,1,0:T(2,128)S(1)}, f32[2,2,1024]{2,1,0:T(2,128)S(1)}, u32[]{:S(2)}, u32[]{:S(2)}) collective-permute-start(f32[2,2,1024]{2,1,0:T(2,128)S(1)} %pad_maximum_fusion.4), channel_id=1, source_target_pairs={{0,1},{1,0},{2,3},{3,2},{4,5},{5,4},{6,7},{7,6},{8,9},{9,8},{10,11... | collective-permute-start | bytes 49160 | tf_op jit(solution)/shard_map/ppermute | solution.py:47
  22.0 1.7 %collective-permute-done.4 = f32[2,2,1024]{2,1,0:T(2,128)S(1)} collective-permute-done((f32[2,2,1024]{2,1,0:T(2,128)S(1)}, f32[2,2,1024]{2,1,0:T(2,128)S(1)}, u32[]{:S(2)}, u32[]{:S(2)}) %collective-permute-start.4) | collective-permute-done | bytes 16416 | tf_op jit(solution)/shard_map/ppermute | solution.py:47
  23.8 4.4 %collective-permute-start.5 = (f32[2,2,1024]{2,1,0:T(2,128)S(1)}, f32[2,2,1024]{2,1,0:T(2,128)S(1)}, u32[]{:S(2)}, u32[]{:S(2)}) collective-permute-start(f32[2,2,1024]{2,1,0:T(2,128)S(1)} %pad_maximum_fusion.5), channel_id=1, source_target_pairs={{0,3},{1,2},{2,1},{3,0},{4,7},{5,6},{6,5},{7,4},{8,11},{9,10},{10,... | collective-permute-start | bytes 49160 | tf_op jit(solution)/shard_map/ppermute | solution.py:47
  28.2 1.7 %collective-permute-done.5 = f32[2,2,1024]{2,1,0:T(2,128)S(1)} collective-permute-done((f32[2,2,1024]{2,1,0:T(2,128)S(1)}, f32[2,2,1024]{2,1,0:T(2,128)S(1)}, u32[]{:S(2)}, u32[]{:S(2)}) %collective-permute-start.5) | collective-permute-done | bytes 16416 | tf_op jit(solution)/shard_map/ppermute | solution.py:47
  29.9 0.1 fusion.30
  30.1 5.5 %pair_region_part.1 = f32[8,1024,128]{2,1,0:T(8,128)S(1)} custom-call(s32[1]{0:T(128)} %bitcast.8.phr, s32[8]{0:T(128)S(1)} %multiply_add_fusion.3.off.refs_0_, f32[2048,1024]{1,0:T(8,128)S(1)} %get-tuple-element.39.e.refs_2_, f32[8,1,1024]{2,1,0:T(1,128)S(1)} %broadcast_select_fusion.1.s.refs_4_, s32[1,1024]{1,0:T(1,128)S(1)} %collective-permute-done.1.pos.refs_6_, ...), custom_call_target="tpu_custom_call" | custom-call | flops 1 | bytes 1 | tf_op jit(solution)/shard_map/pair_region_part/pallas_call | solution.py:250
  35.6 0.1 collective-permute-start.6
  35.8 5.2 %phrase_part.2 = (bf16[2,256,512]{2,1,0:T(8,128)(2,1)S(1)}, bf16[2,256,512]{2,1,0:T(8,128)(2,1)S(1)}, f32[2,256,512]{2,1,0:T(8,128)S(1)}, f32[2,256,512]{2,1,0:T(8,128)S(1)}) custom-call(s32[8]{0:T(128)S(1)} %multiply_add_fusion.3.off.refs_0_, f32[2048,1024]{1,0:T(8,128)S(1)} %get-tuple-element.45.refs_1_.e, f32[2048,1024]{1,0:T(8,128)S(1)} %get-tuple-element.39.e.refs_2_, ...), custom_call_target="tpu_custom_call" | custom-call | flops 1 | bytes 1 | tf_op jit(solution)/shard_map/phrase_part/pallas_call | solution.py:219
  41.0 1.6 %collective-permute-start.16 = (bf16[2,256,512]{2,1,0:T(8,128)(2,1)S(1)}, bf16[2,256,512]{2,1,0:T(8,128)(2,1)S(1)}, u32[]{:S(2)}, u32[]{:S(2)}) collective-permute-start(bf16[2,256,512]{2,1,0:T(8,128)(2,1)S(1)} %get-tuple-element.65), channel_id=1, source_target_pairs={{0,16},{8,24},{16,0},{24,8},{32,48},{40,56},{48,32},{56,40},{64,80... | collective-permute-start | bytes 1572872 | tf_op jit(solution)/shard_map/ppermute | solution.py:43
  42.5 2.1 %collective-permute-start.18 = (bf16[2,256,512]{2,1,0:T(8,128)(2,1)S(1)}, bf16[2,256,512]{2,1,0:T(8,128)(2,1)S(1)}, u32[]{:S(2)}, u32[]{:S(2)}) collective-permute-start(bf16[2,256,512]{2,1,0:T(8,128)(2,1)S(1)} %get-tuple-element.67), channel_id=1, source_target_pairs={{0,48},{8,56},{16,32},{24,40},{32,16},{40,24},{48,0},{56,8},{64,11... | collective-permute-start | bytes 1572872 | tf_op jit(solution)/shard_map/ppermute | solution.py:43
  44.6 10.7 %collective-permute-done.16 = bf16[2,256,512]{2,1,0:T(8,128)(2,1)S(1)} collective-permute-done((bf16[2,256,512]{2,1,0:T(8,128)(2,1)S(1)}, bf16[2,256,512]{2,1,0:T(8,128)(2,1)S(1)}, u32[]{:S(2)}, u32[]{:S(2)}) %collective-permute-start.16) | collective-permute-done | bytes 524320 | tf_op jit(solution)/shard_map/ppermute | solution.py:43
  55.4 0.2 convert_add_fusion.1
  55.6 2.8 %collective-permute-start.17 = (bf16[256,512]{1,0:T(8,128)(2,1)S(1)}, bf16[256,512]{1,0:T(8,128)(2,1)S(1)}, u32[]{:S(2)}, u32[]{:S(2)}) collective-permute-start(bf16[256,512]{1,0:T(8,128)(2,1)S(1)} %fusion.23), channel_id=1, source_target_pairs={{0,48},{8,56},{16,32},{24,40},{32,16},{40,24},{48,0},{56,8},{64,11... | collective-permute-start | bytes 786440 | tf_op jit(solution)/shard_map/ppermute | solution.py:43
  58.4 0.2 convert_add_fusion
  58.6 0.5 collective-permute-start.19
  59.2 6.1 %own_region_part.1 = (bf16[2,2,512,128]{3,2,1,0:T(8,128)(2,1)S(1)}, bf16[2,2,512,128]{3,2,1,0:T(8,128)(2,1)S(1)}, f32[2,512,128]{2,1,0:T(8,128)S(1)}, f32[2,512,128]{2,1,0:T(8,128)S(1)}, f32[2,1024,128]{2,1,0:T(8,128)S(1)}) custom-call(s32[1]{0:T(128)} %bitcast.8.phr, s32[8]{0:T(128)S(1)} %multiply_add_fusion.3.off.refs_0_, ...), custom_call_target="tpu_custom_call" | custom-call | flops 1 | bytes 1 | tf_op jit(solution)/shard_map/own_region_part/pallas_call | solution.py:286
  65.2 0.1 collective-permute-start.7
  65.3 0.1 fusion.8
  65.4 3.3 %collective-permute-start.9 = (bf16[2,2,512,128]{3,2,1,0:T(8,128)(2,1)S(1)}, bf16[2,2,512,128]{3,2,1,0:T(8,128)(2,1)S(1)}, u32[]{:S(2)}, u32[]{:S(2)}) collective-permute-start(bf16[2,2,512,128]{3,2,1,0:T(8,128)(2,1)S(1)} %get-tuple-element.57), channel_id=1, source_target_pairs={{0,3},{1,2},{2,1},{3,0},{4,7},{5,6},{6,5},{7,4},{8,11},{9,10},{10,... | collective-permute-start | bytes 1572872 | tf_op jit(solution)/shard_map/ppermute | solution.py:47
  68.7 0.1 fusion.6
  68.8 5.2 %phrase_part.3 = (bf16[2,256,512]{2,1,0:T(8,128)(2,1)S(1)}, bf16[2,256,512]{2,1,0:T(8,128)(2,1)S(1)}, f32[2,256,512]{2,1,0:T(8,128)S(1)}, f32[2,256,512]{2,1,0:T(8,128)S(1)}) custom-call(s32[8]{0:T(128)S(1)} %multiply_add_fusion.3.off.refs_0_, f32[2048,1024]{1,0:T(8,128)S(1)} %get-tuple-element.45.refs_1_.e, f32[2048,1024]{1,0:T(8,128)S(1)} %get-tuple-element.39.e.refs_2_, ...), custom_call_target="tpu_custom_call" | custom-call | flops 1 | bytes 1 | tf_op jit(solution)/shard_map/phrase_part/pallas_call | solution.py:219
  74.0 1.9 %collective-permute-start.12 = (bf16[2,256,512]{2,1,0:T(8,128)(2,1)S(1)}, bf16[2,256,512]{2,1,0:T(8,128)(2,1)S(1)}, u32[]{:S(2)}, u32[]{:S(2)}) collective-permute-start(bf16[2,256,512]{2,1,0:T(8,128)(2,1)S(1)} %get-tuple-element.61), channel_id=1, source_target_pairs={{0,16},{8,24},{16,0},{24,8},{32,48},{40,56},{48,32},{56,40},{64,80... | collective-permute-start | bytes 1572872 | tf_op jit(solution)/shard_map/ppermute | solution.py:43
  75.9 3.3 %collective-permute-start.20 = (bf16[256,1024]{1,0:T(8,128)(2,1)S(1)}, bf16[256,1024]{1,0:T(8,128)(2,1)S(1)}, u32[]{:S(2)}, u32[]{:S(2)}) collective-permute-start(bf16[256,1024]{1,0:T(8,128)(2,1)S(1)} %pad_maximum_fusion.1), channel_id=1, source_target_pairs={{0,64},{8,72},{16,80},{24,88},{32,96},{40,104},{48,112},{56,120},{... | collective-permute-start | bytes 1572872 | tf_op jit(solution)/shard_map/ppermute | solution.py:43
  79.2 1.5 %collective-permute-start.14 = (bf16[2,256,512]{2,1,0:T(8,128)(2,1)S(1)}, bf16[2,256,512]{2,1,0:T(8,128)(2,1)S(1)}, u32[]{:S(2)}, u32[]{:S(2)}) collective-permute-start(bf16[2,256,512]{2,1,0:T(8,128)(2,1)S(1)} %get-tuple-element.63), channel_id=1, source_target_pairs={{0,48},{8,56},{16,32},{24,40},{32,16},{40,24},{48,0},{56,8},{64,11... | collective-permute-start | bytes 1572872 | tf_op jit(solution)/shard_map/ppermute | solution.py:43
  80.8 1.0 collective-permute-start.8
  81.9 0.6 collective-permute-start.10
  82.5 4.3 %collective-permute-done.12 = bf16[2,256,512]{2,1,0:T(8,128)(2,1)S(1)} collective-permute-done((bf16[2,256,512]{2,1,0:T(8,128)(2,1)S(1)}, bf16[2,256,512]{2,1,0:T(8,128)(2,1)S(1)}, u32[]{:S(2)}, u32[]{:S(2)}) %collective-permute-start.12) | collective-permute-done | bytes 524320 | tf_op jit(solution)/shard_map/ppermute | solution.py:43
  86.8 0.2 convert_add_fusion.3
  87.0 1.9 %collective-permute-start.13 = (bf16[256,512]{1,0:T(8,128)(2,1)S(1)}, bf16[256,512]{1,0:T(8,128)(2,1)S(1)}, u32[]{:S(2)}, u32[]{:S(2)}) collective-permute-start(bf16[256,512]{1,0:T(8,128)(2,1)S(1)} %fusion.21), channel_id=1, source_target_pairs={{0,48},{8,56},{16,32},{24,40},{32,16},{40,24},{48,0},{56,8},{64,11... | collective-permute-start | bytes 786440 | tf_op jit(solution)/shard_map/ppermute | solution.py:43
  88.9 6.3 %collective-permute-done.14 = bf16[2,256,512]{2,1,0:T(8,128)(2,1)S(1)} collective-permute-done((bf16[2,256,512]{2,1,0:T(8,128)(2,1)S(1)}, bf16[2,256,512]{2,1,0:T(8,128)(2,1)S(1)}, u32[]{:S(2)}, u32[]{:S(2)}) %collective-permute-start.14) | collective-permute-done | bytes 524320 | tf_op jit(solution)/shard_map/ppermute | solution.py:43
  95.2 0.2 convert_add_fusion.2
  95.5 0.1 collective-permute-start.15
  95.6 0.2 fusion.15
  95.8 0.7 collective-permute-start.11
  96.5 1.7 %collective-permute-done.13 = bf16[256,512]{1,0:T(8,128)(2,1)S(1)} collective-permute-done((bf16[256,512]{1,0:T(8,128)(2,1)S(1)}, bf16[256,512]{1,0:T(8,128)(2,1)S(1)}, u32[]{:S(2)}, u32[]{:S(2)}) %collective-permute-start.13) | collective-permute-done | bytes 262176 | tf_op jit(solution)/shard_map/ppermute | solution.py:43
  98.2 0.1 fusion.10
  98.2 3.7 %collective-permute-done.15 = bf16[256,512]{1,0:T(8,128)(2,1)S(1)} collective-permute-done((bf16[256,512]{1,0:T(8,128)(2,1)S(1)}, bf16[256,512]{1,0:T(8,128)(2,1)S(1)}, u32[]{:S(2)}, u32[]{:S(2)}) %collective-permute-start.15) | collective-permute-done | bytes 262176 | tf_op jit(solution)/shard_map/ppermute | solution.py:43
  101.9 0.1 fusion.9
  102.0 1.0 fusion
  103.0 0.8 fusion.4
  (39 shorter events, 0.9 us)
Async XLA Ops:
  0.6 8.5 %collective-permute-start = (bf16[1024,1024]{1,0:T(8,128)(2,1)}, bf16[1024,1024]{1,0:T(8,128)(2,1)S(1)}, u32[]{:S(2)}, u32[]{:S(2)}) collective-permute-start(bf16[1024,1024]{1,0:T(8,128)(2,1)} %r_hbm.1), channel_id=1, source_target_pairs={{0,8},{8,0},{16,24},{24,16},{32,40},{40,32},{48,56},{56,48},{64,72... | collective-permute-start | bytes 6291464 | tf_op jit(solution)/shard_map/ppermute | solution.py:43
  14.6 1.4 %collective-permute-start.2 = (f32[2,2,1024]{2,0,1:T(2,128)S(1)}, f32[2,2,1024]{2,0,1:T(2,128)S(1)}, u32[]{:S(2)}, u32[]{:S(2)}) collective-permute-start(f32[2,2,1024]{2,0,1:T(2,128)S(1)} %pad_maximum_fusion.2), channel_id=1, source_target_pairs={{0,8},{8,0},{16,24},{24,16},{32,40},{40,32},{48,56},{56,48},{64,72... | collective-permute-start | bytes 49160 | tf_op jit(solution)/shard_map/ppermute | solution.py:43
  16.0 3.8 %collective-permute-start.3 = (f32[2,2,1024]{2,1,0:T(2,128)S(1)}, f32[2,2,1024]{2,1,0:T(2,128)S(1)}, u32[]{:S(2)}, u32[]{:S(2)}) collective-permute-start(f32[2,2,1024]{2,1,0:T(2,128)S(1)} %pad_maximum_fusion.3), channel_id=1, source_target_pairs={{0,4},{1,5},{2,6},{3,7},{4,0},{5,1},{6,2},{7,3},{8,12},{9,13},{10,... | collective-permute-start | bytes 49160 | tf_op jit(solution)/shard_map/ppermute | solution.py:47
  19.9 3.8 %collective-permute-start.4 = (f32[2,2,1024]{2,1,0:T(2,128)S(1)}, f32[2,2,1024]{2,1,0:T(2,128)S(1)}, u32[]{:S(2)}, u32[]{:S(2)}) collective-permute-start(f32[2,2,1024]{2,1,0:T(2,128)S(1)} %pad_maximum_fusion.4), channel_id=1, source_target_pairs={{0,1},{1,0},{2,3},{3,2},{4,5},{5,4},{6,7},{7,6},{8,9},{9,8},{10,11... | collective-permute-start | bytes 49160 | tf_op jit(solution)/shard_map/ppermute | solution.py:47
  22.0 6.2 %collective-permute-start.1 = (s32[1,1024]{1,0:T(1,128)S(1)}, s32[1,1024]{1,0:T(1,128)S(1)}, u32[]{:S(2)}, u32[]{:S(2)}) collective-permute-start(s32[1,1024]{1,0:T(1,128)S(1)} %get-tuple-element.40.refs_5_.pos), channel_id=1, source_target_pairs={{0,8},{8,0},{16,24},{24,16},{32,40},{40,32},{48,56},{56,48},{64,72... | collective-permute-start | bytes 12296 | tf_op jit(solution)/shard_map/ppermute | solution.py:43
  23.8 6.1 %collective-permute-start.5 = (f32[2,2,1024]{2,1,0:T(2,128)S(1)}, f32[2,2,1024]{2,1,0:T(2,128)S(1)}, u32[]{:S(2)}, u32[]{:S(2)}) collective-permute-start(f32[2,2,1024]{2,1,0:T(2,128)S(1)} %pad_maximum_fusion.5), channel_id=1, source_target_pairs={{0,3},{1,2},{2,1},{3,0},{4,7},{5,6},{6,5},{7,4},{8,11},{9,10},{10,... | collective-permute-start | bytes 49160 | tf_op jit(solution)/shard_map/ppermute | solution.py:47
  35.6 23.6 %collective-permute-start.6 = (f32[8,1024,128]{2,1,0:T(8,128)S(1)}, f32[8,1024,128]{2,1,0:T(8,128)S(1)}, u32[]{:S(2)}, u32[]{:S(2)}) collective-permute-start(f32[8,1024,128]{2,1,0:T(8,128)S(1)} %pair_region_part.1), channel_id=1, source_target_pairs={{0,8},{8,0},{16,24},{24,16},{32,40},{40,32},{48,56},{56,48},{64,72... | collective-permute-start | bytes 12582920 | tf_op jit(solution)/shard_map/ppermute | solution.py:43
  41.0 14.4 %collective-permute-start.16 = (bf16[2,256,512]{2,1,0:T(8,128)(2,1)S(1)}, bf16[2,256,512]{2,1,0:T(8,128)(2,1)S(1)}, u32[]{:S(2)}, u32[]{:S(2)}) collective-permute-start(bf16[2,256,512]{2,1,0:T(8,128)(2,1)S(1)} %get-tuple-element.65), channel_id=1, source_target_pairs={{0,16},{8,24},{16,0},{24,8},{32,48},{40,56},{48,32},{56,40},{64,80... | collective-permute-start | bytes 1572872 | tf_op jit(solution)/shard_map/ppermute | solution.py:43
  42.5 15.9 %collective-permute-start.18 = (bf16[2,256,512]{2,1,0:T(8,128)(2,1)S(1)}, bf16[2,256,512]{2,1,0:T(8,128)(2,1)S(1)}, u32[]{:S(2)}, u32[]{:S(2)}) collective-permute-start(bf16[2,256,512]{2,1,0:T(8,128)(2,1)S(1)} %get-tuple-element.67), channel_id=1, source_target_pairs={{0,48},{8,56},{16,32},{24,40},{32,16},{40,24},{48,0},{56,8},{64,11... | collective-permute-start | bytes 1572872 | tf_op jit(solution)/shard_map/ppermute | solution.py:43
  55.6 9.7 %collective-permute-start.17 = (bf16[256,512]{1,0:T(8,128)(2,1)S(1)}, bf16[256,512]{1,0:T(8,128)(2,1)S(1)}, u32[]{:S(2)}, u32[]{:S(2)}) collective-permute-start(bf16[256,512]{1,0:T(8,128)(2,1)S(1)} %fusion.23), channel_id=1, source_target_pairs={{0,48},{8,56},{16,32},{24,40},{32,16},{40,24},{48,0},{56,8},{64,11... | collective-permute-start | bytes 786440 | tf_op jit(solution)/shard_map/ppermute | solution.py:43
  58.6 10.1 %collective-permute-start.19 = (bf16[256,512]{1,0:T(8,128)(2,1)S(1)}, bf16[256,512]{1,0:T(8,128)(2,1)S(1)}, u32[]{:S(2)}, u32[]{:S(2)}) collective-permute-start(bf16[256,512]{1,0:T(8,128)(2,1)S(1)} %fusion.24), channel_id=1, source_target_pairs={{0,16},{8,24},{16,0},{24,8},{32,48},{40,56},{48,32},{56,40},{64,80... | collective-permute-start | bytes 786440 | tf_op jit(solution)/shard_map/ppermute | solution.py:43
  65.2 15.4 %collective-permute-start.7 = (bf16[2,2,512,128]{3,2,1,0:T(8,128)(2,1)S(1)}, bf16[2,2,512,128]{3,2,1,0:T(8,128)(2,1)S(1)}, u32[]{:S(2)}, u32[]{:S(2)}) collective-permute-start(bf16[2,2,512,128]{3,2,1,0:T(8,128)(2,1)S(1)} %get-tuple-element.55), channel_id=1, source_target_pairs={{0,1},{1,0},{2,3},{3,2},{4,5},{5,4},{6,7},{7,6},{8,9},{9,8},{10,11... | collective-permute-start | bytes 1572872 | tf_op jit(solution)/shard_map/ppermute | solution.py:47
  65.4 16.4 %collective-permute-start.9 = (bf16[2,2,512,128]{3,2,1,0:T(8,128)(2,1)S(1)}, bf16[2,2,512,128]{3,2,1,0:T(8,128)(2,1)S(1)}, u32[]{:S(2)}, u32[]{:S(2)}) collective-permute-start(bf16[2,2,512,128]{3,2,1,0:T(8,128)(2,1)S(1)} %get-tuple-element.57), channel_id=1, source_target_pairs={{0,3},{1,2},{2,1},{3,0},{4,7},{5,6},{6,5},{7,4},{8,11},{9,10},{10,... | collective-permute-start | bytes 1572872 | tf_op jit(solution)/shard_map/ppermute | solution.py:47
  74.0 12.9 %collective-permute-start.12 = (bf16[2,256,512]{2,1,0:T(8,128)(2,1)S(1)}, bf16[2,256,512]{2,1,0:T(8,128)(2,1)S(1)}, u32[]{:S(2)}, u32[]{:S(2)}) collective-permute-start(bf16[2,256,512]{2,1,0:T(8,128)(2,1)S(1)} %get-tuple-element.61), channel_id=1, source_target_pairs={{0,16},{8,24},{16,0},{24,8},{32,48},{40,56},{48,32},{56,40},{64,80... | collective-permute-start | bytes 1572872 | tf_op jit(solution)/shard_map/ppermute | solution.py:43
  75.9 26.1 %collective-permute-start.20 = (bf16[256,1024]{1,0:T(8,128)(2,1)S(1)}, bf16[256,1024]{1,0:T(8,128)(2,1)S(1)}, u32[]{:S(2)}, u32[]{:S(2)}) collective-permute-start(bf16[256,1024]{1,0:T(8,128)(2,1)S(1)} %pad_maximum_fusion.1), channel_id=1, source_target_pairs={{0,64},{8,72},{16,80},{24,88},{32,96},{40,104},{48,112},{56,120},{... | collective-permute-start | bytes 1572872 | tf_op jit(solution)/shard_map/ppermute | solution.py:43
  79.2 16.1 %collective-permute-start.14 = (bf16[2,256,512]{2,1,0:T(8,128)(2,1)S(1)}, bf16[2,256,512]{2,1,0:T(8,128)(2,1)S(1)}, u32[]{:S(2)}, u32[]{:S(2)}) collective-permute-start(bf16[2,256,512]{2,1,0:T(8,128)(2,1)S(1)} %get-tuple-element.63), channel_id=1, source_target_pairs={{0,48},{8,56},{16,32},{24,40},{32,16},{40,24},{48,0},{56,8},{64,11... | collective-permute-start | bytes 1572872 | tf_op jit(solution)/shard_map/ppermute | solution.py:43
  80.8 14.8 %collective-permute-start.8 = (bf16[2,512,128]{2,1,0:T(8,128)(2,1)S(1)}, bf16[2,512,128]{2,1,0:T(8,128)(2,1)S(1)}, u32[]{:S(2)}, u32[]{:S(2)}) collective-permute-start(bf16[2,512,128]{2,1,0:T(8,128)(2,1)S(1)} %fusion.17), channel_id=1, source_target_pairs={{0,3},{1,2},{2,1},{3,0},{4,7},{5,6},{6,5},{7,4},{8,11},{9,10},{10,... | collective-permute-start | bytes 786440 | tf_op jit(solution)/shard_map/ppermute | solution.py:47
  81.9 13.6 %collective-permute-start.10 = (bf16[2,512,128]{2,1,0:T(8,128)(2,1)S(1)}, bf16[2,512,128]{2,1,0:T(8,128)(2,1)S(1)}, u32[]{:S(2)}, u32[]{:S(2)}) collective-permute-start(bf16[2,512,128]{2,1,0:T(8,128)(2,1)S(1)} %fusion.13), channel_id=1, source_target_pairs={{0,1},{1,0},{2,3},{3,2},{4,5},{5,4},{6,7},{7,6},{8,9},{9,8},{10,11... | collective-permute-start | bytes 786440 | tf_op jit(solution)/shard_map/ppermute | solution.py:47
  87.0 11.1 %collective-permute-start.13 = (bf16[256,512]{1,0:T(8,128)(2,1)S(1)}, bf16[256,512]{1,0:T(8,128)(2,1)S(1)}, u32[]{:S(2)}, u32[]{:S(2)}) collective-permute-start(bf16[256,512]{1,0:T(8,128)(2,1)S(1)} %fusion.21), channel_id=1, source_target_pairs={{0,48},{8,56},{16,32},{24,40},{32,16},{40,24},{48,0},{56,8},{64,11... | collective-permute-start | bytes 786440 | tf_op jit(solution)/shard_map/ppermute | solution.py:43
  95.5 6.5 %collective-permute-start.15 = (bf16[256,512]{1,0:T(8,128)(2,1)S(1)}, bf16[256,512]{1,0:T(8,128)(2,1)S(1)}, u32[]{:S(2)}, u32[]{:S(2)}) collective-permute-start(bf16[256,512]{1,0:T(8,128)(2,1)S(1)} %fusion.22), channel_id=1, source_target_pairs={{0,16},{8,24},{16,0},{24,8},{32,48},{40,56},{48,32},{56,40},{64,80... | collective-permute-start | bytes 786440 | tf_op jit(solution)/shard_map/ppermute | solution.py:43
  95.8 7.2 %collective-permute-start.11 = (bf16[1024,128]{1,0:T(8,128)(2,1)S(1)}, bf16[1024,128]{1,0:T(8,128)(2,1)S(1)}, u32[]{:S(2)}, u32[]{:S(2)}) collective-permute-start(bf16[1024,128]{1,0:T(8,128)(2,1)S(1)} %fusion.20), channel_id=1, source_target_pairs={{0,4},{1,5},{2,6},{3,7},{4,0},{5,1},{6,2},{7,3},{8,12},{9,13},{10,... | collective-permute-start | bytes 786440 | tf_op jit(solution)/shard_map/ppermute | solution.py:47

commit v4 on v3

v4 whole, which is shorter than its diff:
```python
import math

import jax
import jax.numpy as jnp
from jax import lax
from jax.experimental import pallas as pl
from jax.experimental.pallas import tpu as pltpu
from jax.sharding import PartitionSpec as P

logit_scale = 2.0
log2e = math.log2(math.e)
BLK = 256
VMEM = 8 * 1024 * 1024


def img_perm(f):
    pairs = []
    for y in range(2):
        for x in range(4):
            for c in range(2):
                y2, x2, c2 = f(y, x, c)
                pairs.append(((y * 4 + x) * 2 + c, (y2 * 4 + x2) * 2 + c2))
    return pairs


def phr_perm(f):
    pairs = []
    for y in range(2):
        for z in range(4):
            y2, z2 = f(y, z)
            pairs.append((y * 4 + z, y2 * 4 + z2))
    return pairs


CORE = img_perm(lambda y, x, c: (y, x, 1 - c))
YH = img_perm(lambda y, x, c: (1 - y, x, c))
YL = phr_perm(lambda y, z: (1 - y, z))
NEAR = ((1, 3), (3, 1))
X = [img_perm(lambda y, x, c: (y, x ^ NEAR[step][c], c)) for step in range(2)]
Z = [
    [
        (i * 8 + p, i * 8 + q)
        for i in range(16)
        for p, q in phr_perm(lambda y, z: (y, z ^ NEAR[step][i % 2]))
    ]
    for step in range(2)
]


def over_img(a, perm):
    return lax.ppermute(a, "img", perm)


def over_phr(a, dy, dz):
    return lax.ppermute(a, "phr", phr_perm(lambda y, z: (y ^ dy, z ^ dz)))


def over_z(a, step):
    return lax.ppermute(a, ("img", "phr"), Z[step])


def vmem(a):
    return pltpu.with_memory_space_constraint(a, pltpu.VMEM)


WHOLE = pl.BlockSpec(memory_space=pltpu.VMEM)
SCALAR = pl.BlockSpec(memory_space=pltpu.SMEM)
HBM = pl.BlockSpec(memory_space=pltpu.HBM)


def call(body, in_specs, outs, name, waits=0, **kwargs):
    def kernel(*refs):
        body(*refs[: len(in_specs)], *refs[len(in_specs) + waits :])

    return pl.pallas_call(
        kernel,
        in_specs=in_specs + [pl.BlockSpec(memory_space=pl.ANY)] * waits,
        out_specs=[WHOLE] * len(outs),
        out_shape=[pltpu.VMEM(*out) for out in outs],
        compiler_params=pltpu.CompilerParams(vmem_limit_bytes=VMEM),
        cost_estimate=pl.CostEstimate(flops=1, bytes_accessed=1, transcendentals=0),
        name=name,
        **kwargs,
    )


def score_block(j, phrases, regions, e, m, l):
    part = pl.ds(j * BLK, BLK)
    s = lax.dot_general(
        phrases[part], regions[...], (((1,), (1,)), ((), ())), preferred_element_type=jnp.float32
    )
    s = s * (logit_scale * log2e)
    top = jnp.max(s, axis=0, keepdims=True)
    value = jnp.exp2(s - top)
    e[part] = value.astype(e.dtype)
    m[j] = top
    l[j] = jnp.sum(value, axis=0, keepdims=True)


def block_state(m, l, state, before=None):
    tiles = m.shape[0]
    top = m[0]
    for j in range(1, tiles):
        top = jnp.maximum(top, m[j])
    if before is not None:
        top = jnp.maximum(top, before[0:1])
    total = l[0] * jnp.exp2(m[0] - top)
    for j in range(1, tiles):
        total += l[j] * jnp.exp2(m[j] - top)
    if before is not None:
        total += before[1:2] * jnp.exp2(before[0:1] - top)
    state[0:1] = top
    state[1:2] = total


def flat_positive(valid, positive):
    boxes = valid.shape[1]
    shape = (boxes, positive.shape[1])
    row = lax.broadcasted_iota(jnp.int32, shape, 0)
    spread = (row == lax.broadcasted_iota(jnp.int32, shape, 1) % boxes).astype(jnp.float32)
    wide = jnp.dot(
        valid[...].astype(jnp.float32), spread, preferred_element_type=jnp.float32
    )
    shape = wide.shape
    row = lax.broadcasted_iota(jnp.int32, shape, 0)
    image = lax.broadcasted_iota(jnp.int32, shape, 1) // boxes
    weight = jnp.sum(jnp.where(row == image, wide, 0.0), axis=0, keepdims=True)
    return jnp.where(weight > 0.5, positive[...], -1)


def first_scores_kernel(blk, p_hbm, r_hbm, pos_hbm, valid_hbm, *refs):
    e, m, state, phrases, own, regions, pos, l, pos_in, valid, sem = refs
    tiles = m.shape[0]
    copies = [pltpu.make_async_copy(r_hbm, regions, sem.at[2 * tiles])]
    for out, start in ((phrases, tiles), (own, 0)):
        for j in range(tiles):
            rows = pl.ds(pl.multiple_of(blk[start + j] * BLK, BLK), BLK)
            copies.append(
                pltpu.make_async_copy(
                    p_hbm.at[rows], out.at[pl.ds(j * BLK, BLK)], sem.at[start + j]
                )
            )
    small = [
        pltpu.make_async_copy(pos_hbm, pos_in, sem.at[2 * tiles + 1]),
        pltpu.make_async_copy(valid_hbm, valid, sem.at[2 * tiles + 2]),
    ]
    for copy in small + copies[:3]:
        copy.start()
    for copy in small:
        copy.wait()
    pos[...] = flat_positive(valid, pos_in)
    for copy in copies[:3]:
        copy.wait()
    for copy in copies[3:]:
        copy.start()
    for j in range(2):
        score_block(j, phrases, regions, e, m, l)
    for copy in copies[3 : tiles + 1]:
        copy.wait()
    for j in range(2, tiles):
        score_block(j, phrases, regions, e, m, l)
    block_state(m, l, state)
    for copy in copies[tiles + 1 :]:
        copy.wait()


def first_scores_call(blk, phrases, regions, positive, valid):
    rows, dim = regions.shape
    half = phrases.shape[0] // 2
    tiles = half // BLK
    arrays = (phrases, regions, positive[None], valid)
    return call(
        first_scores_kernel,
        [SCALAR] + [HBM] * 4,
        [
            ((half, rows), jnp.bfloat16),
            ((tiles, 1, rows), jnp.float32),
            ((2, rows), jnp.float32),
            ((half, dim), phrases.dtype),
            ((half, dim), phrases.dtype),
            ((rows, dim), regions.dtype),
            ((1, rows), jnp.int32),
        ],
        "first_scores",
        scratch_shapes=[
            pltpu.VMEM((tiles, 1, rows), jnp.float32),
            pltpu.VMEM((1, rows), jnp.int32),
            pltpu.VMEM(valid.shape, jnp.int32),
            pltpu.SemaphoreType.DMA((2 * tiles + 3,)),
        ],
    )(blk, *[pltpu.with_memory_space_constraint(a, pltpu.HBM) for a in arrays])


def scores_kernel(phrases, regions, before, e, m, state, l):
    for j in range(m.shape[0]):
        score_block(j, phrases, regions, e, m, l)
    block_state(m, l, state, before)


def scores_call(phrases, regions, before):
    rows, dim = regions.shape
    half = phrases.shape[0]
    tiles = half // BLK
    arrays = (phrases, regions, before)
    return call(
        scores_kernel,
        [WHOLE] * len(arrays),
        [
            ((half, rows), jnp.float32),
            ((tiles, 1, rows), jnp.float32),
            ((2, rows), jnp.float32),
        ],
        "scores",
        scratch_shapes=[pltpu.VMEM((tiles, 1, rows), jnp.float32)],
    )(*[vmem(a) for a in arrays])


def coefficients(e, scale, pos, first):
    column = first + lax.broadcasted_iota(jnp.int32, e.shape, 0)
    return (e.astype(jnp.float32) * scale - (column == pos).astype(jnp.float32)).astype(jnp.bfloat16)


def phrase_kernel(base, off, eo, ep, so, sp, po, pp, ro, rp, send, keep):
    for step, (out, place) in enumerate(((send, 1), (send, 0), (keep, 1), (keep, 0))):
        j = base + step
        part = pl.ds(j * BLK, BLK)
        co = coefficients(eo[part], so[j], po[...], off[j])
        cp = coefficients(ep[part], sp[j], pp[...], off[j])
        acc = jnp.dot(co, ro[...], preferred_element_type=jnp.float32)
        acc += jnp.dot(cp, rp[...], preferred_element_type=jnp.float32)
        out[place] = (logit_scale * acc).astype(out.dtype)


def phrase_call(base, off, *arrays, wait):
    rows, dim = arrays[-1].shape
    shape = (2, BLK, dim)
    return call(
        lambda *refs: phrase_kernel(base, *refs),
        [SCALAR] + [WHOLE] * len(arrays),
        [(shape, jnp.bfloat16), (shape, jnp.float32)],
        "phrase_part",
        waits=len(wait),
    )(off, *[vmem(a) for a in arrays], *wait)


def add_kernel(got, keep, total, send):
    total[...] = keep[0] + got[0].astype(jnp.float32)
    send[...] = (keep[1] + got[1].astype(jnp.float32)).astype(send.dtype)


def add_call(got, keep, wait):
    shape = got.shape[1:]
    return call(
        add_kernel,
        [WHOLE] * 2,
        [(shape, jnp.float32), (shape, jnp.bfloat16)],
        "add_part",
        waits=len(wait),
    )(vmem(got), vmem(keep), *wait)


def region_rows(lanes, off, e, s, pos, phrases):
    coeff = jnp.concatenate(
        [
            coefficients(e[pl.ds(j * BLK, BLK), lanes], s[j, :, lanes], pos[:, lanes], off(j))
            for j in range(s.shape[0])
        ],
        axis=0,
    )
    return lax.dot_general(
        coeff, phrases[...], (((0,), (0,)), ((), ())), preferred_element_type=jnp.float32
    )


def region_kernel(phr, rel, off, e, s, phrases, e_far, s_far, p_far, pos, send, keep, acc):
    tiles = s.shape[0]
    for i in range(0, s.shape[2], BLK):
        here = pl.ds(i, BLK)
        value = region_rows(here, lambda j: off[j], e, s, pos, phrases)
        value += region_rows(here, lambda j: off[tiles + j], e_far, s_far, pos, p_far)
        acc[...] = logit_scale * value
        for dy in range(2):
            for place, (out, slot) in enumerate(((keep, 0), (send, 0), (send, 1), (keep, 1))):
                k = dy * 4 + rel[place]
                cols = pl.ds(pl.multiple_of((phr[0] ^ k) * 128, 128), 128)
                out[slot, dy, here] = acc[:, cols].astype(out.dtype)


def region_call(phr, rel, off, *arrays, wait):
    rows, dim = arrays[1].shape[2], arrays[2].shape[1]
    shape = (2, 2, rows, 128)
    return call(
        region_kernel,
        [SCALAR] * 3 + [WHOLE] * len(arrays),
        [(shape, jnp.bfloat16), (shape, jnp.float32)],
        "region_part",
        waits=len(wait),
        scratch_shapes=[pltpu.VMEM((BLK, dim), jnp.float32)],
    )(phr, rel, off, *[vmem(a) for a in arrays], *wait)


def combine(first, second):
    top = jnp.maximum(first[0], second[0])
    total = first[1] * jnp.exp2(first[0] - top) + second[1] * jnp.exp2(second[0] - top)
    return jnp.stack([top, total])


def per_device(regions, phrases, positive, valid):
    img, phr = lax.axis_index("img"), lax.axis_index("phr")
    core = img % 2
    first, second = 1 + 2 * core, 3 - 2 * core
    blk = jnp.stack(
        [img ^ (e * 8 + d * 2) for e in (1, 0) for d in (2, first, second, 0)]
        + [img ^ (e * 8 + d * 2 + 1) for e in (1, 0) for d in (2, second, first, 0)]
    )
    rel = jnp.stack([0 * core, first, 2 + 0 * core, second])
    off = phr * phrases.shape[0] + blk * BLK
    scalars = [a.astype(jnp.int32) for a in (blk, rel, off, phr[None])]
    blk, rel, off, phr = lax.optimization_barrier(scalars)

    regions_pair = over_img(regions, CORE)
    e_far, m_far, state, p_far, phrases, regions, po = first_scores_call(
        blk, phrases, regions, positive, valid
    )
    pp = over_img(po, CORE)
    e_pair = over_img(e_far, CORE)
    e_own, m_own, state = scores_call(phrases, regions, state)

    for dy, dz in ((1, 0), (0, 1), (0, 3)):
        state = combine(state, over_phr(state, dy, dz))
    lse = state[0] + jnp.log2(state[1])
    s_far = jnp.where(po >= 0, jnp.exp2(m_far - lse), 0.0)
    s_own = jnp.where(po >= 0, jnp.exp2(m_own - lse), 0.0)
    s_pair = over_img(s_far, CORE)

    def phrase_half(base, wait):
        return phrase_call(
            base, off, e_own, e_pair, s_own, s_pair, po, pp, regions, regions_pair, wait=wait
        )

    far_send, far_keep = phrase_half(0, [])
    far_got = over_img(far_send, X[0])
    send, keep = region_call(
        phr, rel, off, e_own, s_own, phrases, e_far, s_far, p_far, po, wait=[far_send]
    )
    got = over_z(send, 0)
    far_sum, far_send = add_call(far_got, far_keep, [send])
    near_send, near_keep = phrase_half(4, [far_send])
    near_got = over_img(near_send, X[0])
    far = far_sum + over_img(far_send, X[1]).astype(jnp.float32)
    far = far.astype(jnp.bfloat16)
    from_yh = over_img(far, YH)
    region_sum, send = add_call(got, keep, [far])
    region = region_sum + over_z(send, 1).astype(jnp.float32)
    send, from_yh = lax.optimization_barrier((region[1].astype(jnp.bfloat16), from_yh))
    from_yl = lax.ppermute(send, "phr", YL)
    near_sum, near_send = add_call(near_got, near_keep, [])
    near = near_sum + over_img(near_send, X[1]).astype(jnp.float32)
    grad_phrases = (near + from_yh.astype(jnp.float32)).astype(jnp.bfloat16)
    grad_regions = (region[0] + from_yl.astype(jnp.float32)).astype(jnp.bfloat16)
    return grad_regions, grad_phrases.astype(jnp.bfloat16)


def solution(mesh):
    in_specs = (P("img", None), P("phr", None), P("img"), P("img", None))
    out_specs = (P("img", "phr"), P(("phr", "img"), None))
    return jax.shard_map(
        per_device, mesh=mesh, in_specs=in_specs, out_specs=out_specs, check_vma=False
    )
```

time: 104 us -> 89.7 us (0.86); the launches traced: 104 us -> 88.2 us
  waiting for transfers between devices: 33.1 us -> 24.7 us
  starting transfers between devices: 30.2 us -> 25.2 us
  other arithmetic: 3.62 us -> 2.4 us
    ppermute x13 -> x9, waiting for transfers between devices: 27.5 us -> 10.2 us  [over_img(): return lax.ppermute(a, 'img', perm)]
    ppermute x0 -> x3, waiting for transfers between devices: none -> 9.28 us  [the longest x1 4.79 us: per_device(): from_yl = lax.ppermute(send, 'phr', YL)]
    ppermute x8 -> x3, starting transfers between devices: 13.9 us -> 8.03 us  [over_phr(): return lax.ppermute(a, 'phr', phr_perm(lambda y, z: (y ^ dy, z ^ dz)))]
    ppermute x0 -> x3, starting transfers between devices: none -> 5.01 us  [the longest x2 3.43 us: over_z(): return lax.ppermute(a, ('img', 'phr'), Z[step])]
    ppermute x13 -> x9, starting transfers between devices: 16.3 us -> 12.1 us  [over_img(): return lax.ppermute(a, 'img', perm)]
    pallas_call x4 -> x6, Pallas kernels: 25.3 us -> 24.9 us  [the longest x1 10.1 us: region_call(): call(region_kernel, [SCALAR] * 3 + [WHOLE] * len(arrays), [(shape, jnp.bf...]
    ppermute x8 -> x3, waiting for transfers between devices: 5.52 us -> 5.24 us  [over_phr(): return lax.ppermute(a, 'phr', phr_perm(lambda y, z: (y ^ dy, z ^ dz)))]
  transfers between devices with their start and end apart: 21 -> 15, of which waited for: 9 -> 11; matrix products, arithmetic and copies ran while one was open for 3% -> 1% of each run, Pallas kernels for 24% -> 24%
where the time goes in v4:
time: 89.7 us; the launch traced here: 88.2 us
  Pallas kernels  35 us (39%)
  starting transfers between devices  25.2 us (28%)
  waiting for transfers between devices  24.7 us (28%)
  other arithmetic  2.4 us (3%)
    ppermute x9, starting transfers between devices, over_img(): return lax.ppermute(a, 'img', perm)  12.1 us
    ppermute x9, waiting for transfers between devices, over_img(): return lax.ppermute(a, 'img', perm)  10.2 us
    pallas_call x1, Pallas kernels, region_call(): call(region_kernel, [SCALAR] * 3 + [WHOLE] * len(arrays), [(shape, jnp.bf...  10.1 us
    pallas_call x2, Pallas kernels, phrase_call(): call(lambda *refs: phrase_kernel(base, *refs), [SCALAR] + [WHOLE] * len(a...  10.1 us
    pallas_call x1, Pallas kernels, first_scores_call(): call(first_scores_kernel, [SCALAR] + [HBM] * 4, [((half, rows), jnp.bfloa...  8.7 us
    ppermute x3, starting transfers between devices, over_phr(): return lax.ppermute(a, 'phr', phr_perm(lambda y, z: (y ^ dy, z ^ dz)))  8.03 us
    pallas_call x1, Pallas kernels, scores_call(): call(scores_kernel, [WHOLE] * len(arrays), [((half, rows), jnp.float32),...  5.37 us
    ppermute x3, waiting for transfers between devices, over_phr(): return lax.ppermute(a, 'phr', phr_perm(lambda y, z: (y ^ dy, z ^ dz)))  5.24 us
  transfers between devices with their start and end apart: 15, of which 11 were waited for; matrix products, arithmetic and copies ran while one was open for 1% of the time, Pallas kernels for 24%

profile of v4, /device:TPU:0, one launch (start us, length us, event | category | flops | bytes accessed | tf_op | source)
XLA Modules:
  0.0 88.2 jit_solution(630817822269535621)
XLA Ops:
  0.7 0.1 stack.86.refs_0_
  0.8 0.1 pad_add_fusion.refs_1_
  0.8 0.0 copy-start
  0.8 8.7 %first_scores.1 = (bf16[2048,1024]{1,0:T(8,128)(2,1)S(1)}, f32[8,1,1024]{2,1,0:T(1,128)S(1)}, f32[2,1024]{1,0:T(2,128)S(1)}, bf16[2048,1024]{1,0:T(8,128)(2,1)S(...) custom-call(s32[16]{0:T(128)S(1)} %stack.86.refs_0_, ...), custom_call_target="tpu_custom_call" | custom-call | flops 1 | bytes 1 | tf_op jit(solution)/shard_map/first_scores/pallas_call | solution.py:172
  9.6 0.1 collective-permute-start.3
  9.7 0.0 copy-done
  9.7 0.5 collective-permute-start.6
  10.2 5.4 %scores.1 = (f32[2048,1024]{1,0:T(8,128)S(1)}, f32[8,1,1024]{2,1,0:T(1,128)S(1)}, f32[2,1024]{1,0:T(2,128)S(1)}) custom-call(bf16[2048,1024]{1,0:T(8,128)(2,1)S(1)} %get-tuple-element.34.refs_0_.refs_5_, bf16[1024,1024]{1,0:T(8,128)(2,1)S(1)} %get-tuple-element.35.refs_1_.refs_7_, f32[2,1024]{1,0:T(2,128)S(1)} %get-tuple-element.36.refs_2_), custom_call_target="tpu_custom_call" | custom-call | flops 1 | bytes 1 | tf_op jit(solution)/shard_map/scores/pallas_call | solution.py:205
  15.5 1.7 %collective-permute-start = (f32[2,1024]{1,0:T(2,128)S(1)}, f32[2,1024]{1,0:T(2,128)S(1)}, u32[]{:S(2)}, u32[]{:S(2)}) collective-permute-start(f32[2,1024]{1,0:T(2,128)S(1)} %get-tuple-element.40), channel_id=1, source_target_pairs={{0,4},{1,5},{2,6},{3,7},{4,0},{5,1},{6,2},{7,3},{8,12},{9,13},{10,... | collective-permute-start | bytes 24584 | tf_op jit(solution)/shard_map/ppermute | solution.py:55
  17.3 2.0 %collective-permute-done = f32[2,1024]{1,0:T(2,128)S(1)} collective-permute-done((f32[2,1024]{1,0:T(2,128)S(1)}, f32[2,1024]{1,0:T(2,128)S(1)}, u32[]{:S(2)}, u32[]{:S(2)}) %collective-permute-start) | collective-permute-done | bytes 8224 | tf_op jit(solution)/shard_map/ppermute | solution.py:55
  19.3 2.1 %collective-permute-start.1 = (f32[2,1024]{1,0:T(2,128)S(1)}, f32[2,1024]{1,0:T(2,128)S(1)}, u32[]{:S(2)}, u32[]{:S(2)}) collective-permute-start(f32[2,1024]{1,0:T(2,128)S(1)} %pad_maximum_fusion), channel_id=1, source_target_pairs={{0,1},{1,0},{2,3},{3,2},{4,5},{5,4},{6,7},{7,6},{8,9},{9,8},{10,11... | collective-permute-start | bytes 24584 | tf_op jit(solution)/shard_map/ppermute | solution.py:55
  21.4 1.6 %collective-permute-done.1 = f32[2,1024]{1,0:T(2,128)S(1)} collective-permute-done((f32[2,1024]{1,0:T(2,128)S(1)}, f32[2,1024]{1,0:T(2,128)S(1)}, u32[]{:S(2)}, u32[]{:S(2)}) %collective-permute-start.1) | collective-permute-done | bytes 8224 | tf_op jit(solution)/shard_map/ppermute | solution.py:55
  23.1 4.2 %collective-permute-start.2 = (f32[2,1024]{1,0:T(2,128)S(1)}, f32[2,1024]{1,0:T(2,128)S(1)}, u32[]{:S(2)}, u32[]{:S(2)}) collective-permute-start(f32[2,1024]{1,0:T(2,128)S(1)} %pad_maximum_fusion.1), channel_id=1, source_target_pairs={{0,3},{1,2},{2,1},{3,0},{4,7},{5,6},{6,5},{7,4},{8,11},{9,10},{10,... | collective-permute-start | bytes 24584 | tf_op jit(solution)/shard_map/ppermute | solution.py:55
  27.3 1.6 %collective-permute-done.2 = f32[2,1024]{1,0:T(2,128)S(1)} collective-permute-done((f32[2,1024]{1,0:T(2,128)S(1)}, f32[2,1024]{1,0:T(2,128)S(1)}, u32[]{:S(2)}, u32[]{:S(2)}) %collective-permute-start.2) | collective-permute-done | bytes 8224 | tf_op jit(solution)/shard_map/ppermute | solution.py:55
  29.0 0.1 broadcast_select_fusion
  29.1 0.3 collective-permute-start.4
  29.4 0.5 collective-permute-start.5
  29.9 0.8 collective-permute-done.5.refs_6_
  30.7 0.0 collective-permute-done.4.refs_4_
  30.7 0.0 collective-permute-done.6.refs_8_
  30.7 0.0 collective-permute-done.3.refs_2_
  30.7 5.1 %phrase_part.2 = (bf16[2,256,1024]{2,1,0:T(8,128)(2,1)S(1)}, f32[2,256,1024]{2,1,0:T(8,128)S(1)}) custom-call(s32[16]{0:T(128)S(1)} %multiply_add_fusion.3.refs_0_.refs_2_, f32[2048,1024]{1,0:T(8,128)S(1)} %get-tuple-element.37.refs_1_.refs_3_, bf16[2048,1024]{1,0:T(8,128)(2,1)S(1)} %collective-permute-done.3.refs_2_, ...), custom_call_target="tpu_custom_call" | custom-call | flops 1 | bytes 1 | tf_op jit(solution)/shard_map/phrase_part/pallas_call | solution.py:237
  35.8 1.8 %collective-permute-start.8 = (bf16[2,256,1024]{2,1,0:T(8,128)(2,1)S(1)}, bf16[2,256,1024]{2,1,0:T(8,128)(2,1)S(1)}, u32[]{:S(2)}, u32[]{:S(2)}) collective-permute-start(bf16[2,256,1024]{2,1,0:T(8,128)(2,1)S(1)} %get-tuple-element.44.refs_10_), channel_id=1, source_target_pairs={{0,16},{8,56},{16,0},{24,40},{32,48},{40,24},{48,32},{56,8},{64,80... | collective-permute-start | bytes 3145736 | tf_op jit(solution)/shard_map/ppermute | solution.py:51
  37.6 10.1 %region_part.1 = (bf16[2,2,1024,128]{3,2,1,0:T(8,128)(2,1)S(1)}, f32[2,2,1024,128]{3,2,1,0:T(8,128)S(1)}) custom-call(s32[1]{0:T(128)} %bitcast.18.refs_0_, s32[4]{0:T(128)S(1)} %pad_add_fusion.refs_1_, s32[16]{0:T(128)S(1)} %multiply_add_fusion.3.refs_0_.refs_2_, f32[2048,1024]{1,0:T(8,128)S(1)} %get-tuple-element.37.refs_1_.refs_3_, ...), custom_call_target="tpu_custom_call" | custom-call | flops 1 | bytes 1 | tf_op jit(solution)/shard_map/region_part/pallas_call | solution.py:292
  47.7 0.1 collective-permute-start.7
  47.8 3.1 %collective-permute-done.8.refs_0_ = bf16[2,256,1024]{2,1,0:T(8,128)(2,1)S(1)} collective-permute-done((bf16[2,256,1024]{2,1,0:T(8,128)(2,1)S(1)}, bf16[2,256,1024]{2,1,0:T(8,128)(2,1)S(1)}, u32[]{:S(2)}, u32[]{:S(2)}) %collective-permute-start.8) | collective-permute-done | bytes 1048608 | tf_op jit(solution)/shard_map/ppermute | solution.py:51
  50.9 0.2 add_part.3
  51.0 3.1 %collective-permute-start.9 = (bf16[256,1024]{1,0:T(8,128)(2,1)S(1)}, bf16[256,1024]{1,0:T(8,128)(2,1)S(1)}, u32[]{:S(2)}, u32[]{:S(2)}) collective-permute-start(bf16[256,1024]{1,0:T(8,128)(2,1)S(1)} %get-tuple-element.49.refs_9_), channel_id=1, source_target_pairs={{0,48},{8,24},{16,32},{24,8},{32,16},{40,56},{48,0},{56,40},{64,11... | collective-permute-start | bytes 1572872 | tf_op jit(solution)/shard_map/ppermute | solution.py:51
  54.1 5.1 %phrase_part.3 = (bf16[2,256,1024]{2,1,0:T(8,128)(2,1)S(1)}, f32[2,256,1024]{2,1,0:T(8,128)S(1)}) custom-call(s32[16]{0:T(128)S(1)} %multiply_add_fusion.3.refs_0_.refs_2_, f32[2048,1024]{1,0:T(8,128)S(1)} %get-tuple-element.37.refs_1_.refs_3_, bf16[2048,1024]{1,0:T(8,128)(2,1)S(1)} %collective-permute-done.3.refs_2_, ...), custom_call_target="tpu_custom_call" | custom-call | flops 1 | bytes 1 | tf_op jit(solution)/shard_map/phrase_part/pallas_call | solution.py:237
  59.2 0.3 collective-permute-start.13
  59.5 2.4 %collective-permute-done.9 = bf16[256,1024]{1,0:T(8,128)(2,1)S(1)} collective-permute-done((bf16[256,1024]{1,0:T(8,128)(2,1)S(1)}, bf16[256,1024]{1,0:T(8,128)(2,1)S(1)}, u32[]{:S(2)}, u32[]{:S(2)}) %collective-permute-start.9) | collective-permute-done | bytes 524320 | tf_op jit(solution)/shard_map/ppermute | solution.py:51
  61.9 0.2 add_convert_fusion.1.refs_2_
  62.1 0.5 collective-permute-done.7.refs_0_
  62.6 0.2 add_part.4
  62.8 3.3 %collective-permute-start.10 = (bf16[2,1024,128]{2,1,0:T(8,128)(2,1)S(1)}, bf16[2,1024,128]{2,1,0:T(8,128)(2,1)S(1)}, u32[]{:S(2)}, u32[]{:S(2)}) collective-permute-start(bf16[2,1024,128]{2,1,0:T(8,128)(2,1)S(1)} %get-tuple-element.51), channel_id=1, source_target_pairs={{0,3},{1,2},{2,1},{3,0},{4,7},{5,6},{6,5},{7,4},{8,9},{9,8},{10,11... | collective-permute-start | bytes 1572872 | tf_op jit(solution)/shard_map/ppermute | solution.py:59
  66.2 3.2 %collective-permute-start.11 = (bf16[256,1024]{1,0:T(8,128)(2,1)S(1)}, bf16[256,1024]{1,0:T(8,128)(2,1)S(1)}, u32[]{:S(2)}, u32[]{:S(2)}) collective-permute-start(bf16[256,1024]{1,0:T(8,128)(2,1)S(1)} %add_convert_fusion.1.refs_2_), channel_id=1, source_target_pairs={{0,64},{8,72},{16,80},{24,88},{32,96},{40,104},{48,112},{56,120},{... | collective-permute-start | bytes 1572872 | tf_op jit(solution)/shard_map/ppermute | solution.py:51
  69.3 4.0 %collective-permute-done.10 = bf16[2,1024,128]{2,1,0:T(8,128)(2,1)S(1)} collective-permute-done((bf16[2,1024,128]{2,1,0:T(8,128)(2,1)S(1)}, bf16[2,1024,128]{2,1,0:T(8,128)(2,1)S(1)}, u32[]{:S(2)}, u32[]{:S(2)}) %collective-permute-start.10) | collective-permute-done | bytes 524320 | tf_op jit(solution)/shard_map/ppermute | solution.py:59
  73.3 0.1 convert_add_fusion
  73.4 0.7 collective-permute-done.13.refs_0_
  74.1 0.2 add_part.5
  74.3 2.4 %collective-permute-start.14 = (bf16[256,1024]{1,0:T(8,128)(2,1)S(1)}, bf16[256,1024]{1,0:T(8,128)(2,1)S(1)}, u32[]{:S(2)}, u32[]{:S(2)}) collective-permute-start(bf16[256,1024]{1,0:T(8,128)(2,1)S(1)} %get-tuple-element.56), channel_id=1, source_target_pairs={{0,48},{8,24},{16,32},{24,8},{32,16},{40,56},{48,0},{56,40},{64,11... | collective-permute-start | bytes 1572872 | tf_op jit(solution)/shard_map/ppermute | solution.py:51
  76.8 3.2 %collective-permute-done.11 = bf16[256,1024]{1,0:T(8,128)(2,1)S(1)} collective-permute-done((bf16[256,1024]{1,0:T(8,128)(2,1)S(1)}, bf16[256,1024]{1,0:T(8,128)(2,1)S(1)}, u32[]{:S(2)}, u32[]{:S(2)}) %collective-permute-start.11) | collective-permute-done | bytes 524320 | tf_op jit(solution)/shard_map/ppermute | solution.py:51
  80.0 1.6 %collective-permute-start.12 = (bf16[1024,128]{1,0:T(8,128)(2,1)S(1)}, bf16[1024,128]{1,0:T(8,128)(2,1)S(1)}, u32[]{:S(2)}, u32[]{:S(2)}) collective-permute-start(bf16[1024,128]{1,0:T(8,128)(2,1)S(1)} %fusion.2), channel_id=1, source_target_pairs={{0,4},{1,5},{2,6},{3,7},{4,0},{5,1},{6,2},{7,3},{8,12},{9,13},{10,... | collective-permute-start | bytes 786440 | tf_op jit(solution)/shard_map/ppermute | solution.py:356
  81.6 4.8 %collective-permute-done.12 = bf16[1024,128]{1,0:T(8,128)(2,1)S(1)} collective-permute-done((bf16[1024,128]{1,0:T(8,128)(2,1)S(1)}, bf16[1024,128]{1,0:T(8,128)(2,1)S(1)}, u32[]{:S(2)}, u32[]{:S(2)}) %collective-permute-start.12) | collective-permute-done | bytes 262176 | tf_op jit(solution)/shard_map/ppermute | solution.py:356
  86.4 0.8 fusion.1
  87.1 0.0 collective-permute-done.14
  87.1 1.1 %add_convert_fusion = bf16[256,1024]{1,0:T(8,128)(2,1)} fusion(bf16[256,1024]{1,0:T(8,128)(2,1)S(1)} %collective-permute-done.11, f32[256,1024]{1,0:T(8,128)S(1)} %get-tuple-element.55, bf16[256,1024]{1,0:T(8,128)(2,1)S(1)} %collective-permute-done.14), kind=kLoop, calls=%fused_computation | loop fusion | flops 1310720 | bytes 2621440 | tf_op jit(solution)/shard_map/convert_element_type | solution.py:359
  (9 shorter events, 0.2 us)
Async XLA Ops:
  0.8 8.8 %copy-start = (bf16[1024,1024]{1,0:T(8,128)(2,1)S(1)}, bf16[1024,1024]{1,0:T(8,128)(2,1)}, u32[]{:S(2)}) copy-start(bf16[1024,1024]{1,0:T(8,128)(2,1)} %refs_2_.1) | copy-start | bytes 6291460
  9.6 21.1 %collective-permute-start.3 = (bf16[2048,1024]{1,0:T(8,128)(2,1)S(1)}, bf16[2048,1024]{1,0:T(8,128)(2,1)S(1)}, u32[]{:S(2)}, u32[]{:S(2)}) collective-permute-start(bf16[2048,1024]{1,0:T(8,128)(2,1)S(1)} %get-tuple-element.41.refs_6_), channel_id=1, source_target_pairs={{0,8},{8,0},{16,24},{24,16},{32,40},{40,32},{48,56},{56,48},{64,72... | collective-permute-start | bytes 12582920 | tf_op jit(solution)/shard_map/ppermute | solution.py:51
  9.7 21.0 %collective-permute-start.6 = (bf16[1024,1024]{1,0:T(8,128)(2,1)S(1)}, bf16[1024,1024]{1,0:T(8,128)(2,1)S(1)}, u32[]{:S(2)}, u32[]{:S(2)}) collective-permute-start(bf16[1024,1024]{1,0:T(8,128)(2,1)S(1)} %copy-done), channel_id=1, source_target_pairs={{0,8},{8,0},{16,24},{24,16},{32,40},{40,32},{48,56},{56,48},{64,72... | collective-permute-start | bytes 6291464 | tf_op jit(solution)/shard_map/ppermute | solution.py:51
  15.5 3.7 %collective-permute-start = (f32[2,1024]{1,0:T(2,128)S(1)}, f32[2,1024]{1,0:T(2,128)S(1)}, u32[]{:S(2)}, u32[]{:S(2)}) collective-permute-start(f32[2,1024]{1,0:T(2,128)S(1)} %get-tuple-element.40), channel_id=1, source_target_pairs={{0,4},{1,5},{2,6},{3,7},{4,0},{5,1},{6,2},{7,3},{8,12},{9,13},{10,... | collective-permute-start | bytes 24584 | tf_op jit(solution)/shard_map/ppermute | solution.py:55
  19.3 3.7 %collective-permute-start.1 = (f32[2,1024]{1,0:T(2,128)S(1)}, f32[2,1024]{1,0:T(2,128)S(1)}, u32[]{:S(2)}, u32[]{:S(2)}) collective-permute-start(f32[2,1024]{1,0:T(2,128)S(1)} %pad_maximum_fusion), channel_id=1, source_target_pairs={{0,1},{1,0},{2,3},{3,2},{4,5},{5,4},{6,7},{7,6},{8,9},{9,8},{10,11... | collective-permute-start | bytes 24584 | tf_op jit(solution)/shard_map/ppermute | solution.py:55
  23.1 5.8 %collective-permute-start.2 = (f32[2,1024]{1,0:T(2,128)S(1)}, f32[2,1024]{1,0:T(2,128)S(1)}, u32[]{:S(2)}, u32[]{:S(2)}) collective-permute-start(f32[2,1024]{1,0:T(2,128)S(1)} %pad_maximum_fusion.1), channel_id=1, source_target_pairs={{0,3},{1,2},{2,1},{3,0},{4,7},{5,6},{6,5},{7,4},{8,11},{9,10},{10,... | collective-permute-start | bytes 24584 | tf_op jit(solution)/shard_map/ppermute | solution.py:55
  29.1 1.6 %collective-permute-start.4 = (f32[8,1,1024]{2,1,0:T(1,128)S(1)}, f32[8,1,1024]{2,1,0:T(1,128)S(1)}, u32[]{:S(2)}, u32[]{:S(2)}) collective-permute-start(f32[8,1,1024]{2,1,0:T(1,128)S(1)} %get-tuple-element.70.refs_7_), channel_id=1, source_target_pairs={{0,8},{8,0},{16,24},{24,16},{32,40},{40,32},{48,56},{56,48},{64,72... | collective-permute-start | bytes 98312 | tf_op jit(solution)/shard_map/ppermute | solution.py:51
  29.4 1.3 %collective-permute-start.5 = (s32[1,1024]{1,0:T(1,128)S(1)}, s32[1,1024]{1,0:T(1,128)S(1)}, u32[]{:S(2)}, u32[]{:S(2)}) collective-permute-start(s32[1,1024]{1,0:T(1,128)S(1)} %get-tuple-element.38.refs_5_.refs_9_), channel_id=1, source_target_pairs={{0,8},{8,0},{16,24},{24,16},{32,40},{40,32},{48,56},{56,48},{64,72... | collective-permute-start | bytes 12296 | tf_op jit(solution)/shard_map/ppermute | solution.py:51
  35.8 15.1 %collective-permute-start.8 = (bf16[2,256,1024]{2,1,0:T(8,128)(2,1)S(1)}, bf16[2,256,1024]{2,1,0:T(8,128)(2,1)S(1)}, u32[]{:S(2)}, u32[]{:S(2)}) collective-permute-start(bf16[2,256,1024]{2,1,0:T(8,128)(2,1)S(1)} %get-tuple-element.44.refs_10_), channel_id=1, source_target_pairs={{0,16},{8,56},{16,0},{24,40},{32,48},{40,24},{48,32},{56,8},{64,80... | collective-permute-start | bytes 3145736 | tf_op jit(solution)/shard_map/ppermute | solution.py:51
  47.7 14.9 %collective-permute-start.7 = (bf16[2,2,1024,128]{3,2,1,0:T(8,128)(2,1)S(1)}, bf16[2,2,1024,128]{3,2,1,0:T(8,128)(2,1)S(1)}, u32[]{:S(2)}, u32[]{:S(2)}) collective-permute-start(bf16[2,2,1024,128]{3,2,1,0:T(8,128)(2,1)S(1)} %get-tuple-element.45.refs_2_), channel_id=1, source_target_pairs={{0,1},{1,0},{2,3},{3,2},{4,5},{5,4},{6,7},{7,6},{8,11},{9,10},{10,... | collective-permute-start | bytes 3145736 | tf_op jit(solution)/shard_map/ppermute | solution.py:59
  51.0 10.9 %collective-permute-start.9 = (bf16[256,1024]{1,0:T(8,128)(2,1)S(1)}, bf16[256,1024]{1,0:T(8,128)(2,1)S(1)}, u32[]{:S(2)}, u32[]{:S(2)}) collective-permute-start(bf16[256,1024]{1,0:T(8,128)(2,1)S(1)} %get-tuple-element.49.refs_9_), channel_id=1, source_target_pairs={{0,48},{8,24},{16,32},{24,8},{32,16},{40,56},{48,0},{56,40},{64,11... | collective-permute-start | bytes 1572872 | tf_op jit(solution)/shard_map/ppermute | solution.py:51
  59.2 14.9 %collective-permute-start.13 = (bf16[2,256,1024]{2,1,0:T(8,128)(2,1)S(1)}, bf16[2,256,1024]{2,1,0:T(8,128)(2,1)S(1)}, u32[]{:S(2)}, u32[]{:S(2)}) collective-permute-start(bf16[2,256,1024]{2,1,0:T(8,128)(2,1)S(1)} %get-tuple-element.53), channel_id=1, source_target_pairs={{0,16},{8,56},{16,0},{24,40},{32,48},{40,24},{48,32},{56,8},{64,80... | collective-permute-start | bytes 3145736 | tf_op jit(solution)/shard_map/ppermute | solution.py:51
  62.8 10.5 %collective-permute-start.10 = (bf16[2,1024,128]{2,1,0:T(8,128)(2,1)S(1)}, bf16[2,1024,128]{2,1,0:T(8,128)(2,1)S(1)}, u32[]{:S(2)}, u32[]{:S(2)}) collective-permute-start(bf16[2,1024,128]{2,1,0:T(8,128)(2,1)S(1)} %get-tuple-element.51), channel_id=1, source_target_pairs={{0,3},{1,2},{2,1},{3,0},{4,7},{5,6},{6,5},{7,4},{8,9},{9,8},{10,11... | collective-permute-start | bytes 1572872 | tf_op jit(solution)/shard_map/ppermute | solution.py:59
  66.2 13.8 %collective-permute-start.11 = (bf16[256,1024]{1,0:T(8,128)(2,1)S(1)}, bf16[256,1024]{1,0:T(8,128)(2,1)S(1)}, u32[]{:S(2)}, u32[]{:S(2)}) collective-permute-start(bf16[256,1024]{1,0:T(8,128)(2,1)S(1)} %add_convert_fusion.1.refs_2_), channel_id=1, source_target_pairs={{0,64},{8,72},{16,80},{24,88},{32,96},{40,104},{48,112},{56,120},{... | collective-permute-start | bytes 1572872 | tf_op jit(solution)/shard_map/ppermute | solution.py:51
  74.3 12.8 %collective-permute-start.14 = (bf16[256,1024]{1,0:T(8,128)(2,1)S(1)}, bf16[256,1024]{1,0:T(8,128)(2,1)S(1)}, u32[]{:S(2)}, u32[]{:S(2)}) collective-permute-start(bf16[256,1024]{1,0:T(8,128)(2,1)S(1)} %get-tuple-element.56), channel_id=1, source_target_pairs={{0,48},{8,24},{16,32},{24,8},{32,16},{40,56},{48,0},{56,40},{64,11... | collective-permute-start | bytes 1572872 | tf_op jit(solution)/shard_map/ppermute | solution.py:51
  80.0 6.4 %collective-permute-start.12 = (bf16[1024,128]{1,0:T(8,128)(2,1)S(1)}, bf16[1024,128]{1,0:T(8,128)(2,1)S(1)}, u32[]{:S(2)}, u32[]{:S(2)}) collective-permute-start(bf16[1024,128]{1,0:T(8,128)(2,1)S(1)} %fusion.2), channel_id=1, source_target_pairs={{0,4},{1,5},{2,6},{3,7},{4,0},{5,1},{6,2},{7,3},{8,12},{9,13},{10,... | collective-permute-start | bytes 786440 | tf_op jit(solution)/shard_map/ppermute | solution.py:356

commit v5 on v4

--- a/solution.py
+++ b/solution.py
@@ -220,27 +220,26 @@
     return (e.astype(jnp.float32) * scale - (column == pos).astype(jnp.float32)).astype(jnp.bfloat16)
 
 
-def phrase_kernel(base, off, eo, ep, so, sp, po, pp, ro, rp, send, keep):
-    for step, (out, place) in enumerate(((send, 1), (send, 0), (keep, 1), (keep, 0))):
+def phrase_kernel(base, off, eo, ep, so, sp, po, pp, ro, rp, out):
+    for step in range(2):
         j = base + step
         part = pl.ds(j * BLK, BLK)
         co = coefficients(eo[part], so[j], po[...], off[j])
         cp = coefficients(ep[part], sp[j], pp[...], off[j])
         acc = jnp.dot(co, ro[...], preferred_element_type=jnp.float32)
         acc += jnp.dot(cp, rp[...], preferred_element_type=jnp.float32)
-        out[place] = (logit_scale * acc).astype(out.dtype)
-
-
-def phrase_call(base, off, *arrays, wait):
+        out[1 - step] = (logit_scale * acc).astype(out.dtype)
+
+
+def phrase_call(base, dtype, off, *arrays, wait):
     rows, dim = arrays[-1].shape
-    shape = (2, BLK, dim)
     return call(
         lambda *refs: phrase_kernel(base, *refs),
         [SCALAR] + [WHOLE] * len(arrays),
-        [(shape, jnp.bfloat16), (shape, jnp.float32)],
+        [((2, BLK, dim), dtype)],
         "phrase_part",
         waits=len(wait),
-    )(off, *[vmem(a) for a in arrays], *wait)
+    )(off, *[vmem(a) for a in arrays], *wait)[0]
 
 
 def add_kernel(got, keep, total, send):
@@ -333,30 +332,32 @@
     s_own = jnp.where(po >= 0, jnp.exp2(m_own - lse), 0.0)
     s_pair = over_img(s_far, CORE)
 
-    def phrase_half(base, wait):
-        return phrase_call(
-            base, off, e_own, e_pair, s_own, s_pair, po, pp, regions, regions_pair, wait=wait
-        )
-
-    far_send, far_keep = phrase_half(0, [])
+    def phrases_of(base, dtype, wait):
+        arrays = (e_own, e_pair, s_own, s_pair, po, pp, regions, regions_pair)
+        return phrase_call(base, dtype, off, *arrays, wait=wait)
+
+    far_send = phrases_of(0, jnp.bfloat16, [])
     far_got = over_img(far_send, X[0])
+    far_keep = phrases_of(2, jnp.float32, [far_send])
     send, keep = region_call(
-        phr, rel, off, e_own, s_own, phrases, e_far, s_far, p_far, po, wait=[far_send]
+        phr, rel, off, e_own, s_own, phrases, e_far, s_far, p_far, po, wait=[far_keep]
     )
     got = over_z(send, 0)
     far_sum, far_send = add_call(far_got, far_keep, [send])
-    near_send, near_keep = phrase_half(4, [far_send])
+    near_send = phrases_of(4, jnp.bfloat16, [far_send])
     near_got = over_img(near_send, X[0])
+    near_keep = phrases_of(6, jnp.float32, [near_send])
     far = far_sum + over_img(far_send, X[1]).astype(jnp.float32)
     far = far.astype(jnp.bfloat16)
     from_yh = over_img(far, YH)
-    region_sum, send = add_call(got, keep, [far])
-    region = region_sum + over_z(send, 1).astype(jnp.float32)
-    send, from_yh = lax.optimization_barrier((region[1].astype(jnp.bfloat16), from_yh))
-    from_yl = lax.ppermute(send, "phr", YL)
+    region_sum, send = add_call(got, keep, [far, near_keep])
     near_sum, near_send = add_call(near_got, near_keep, [])
+    from_z, from_yh, near_sum = lax.optimization_barrier((over_z(send, 1), from_yh, near_sum))
+    region = region_sum + from_z.astype(jnp.float32)
+    from_yl = lax.ppermute(region[1].astype(jnp.bfloat16), "phr", YL)
     near = near_sum + over_img(near_send, X[1]).astype(jnp.float32)
     grad_phrases = (near + from_yh.astype(jnp.float32)).astype(jnp.bfloat16)
+    from_yl, grad_phrases = lax.optimization_barrier((from_yl, grad_phrases))
     grad_regions = (region[0] + from_yl.astype(jnp.float32)).astype(jnp.bfloat16)
     return grad_regions, grad_phrases.astype(jnp.bfloat16)
 

time: 89.7 us -> 86.5 us (0.964)
  waiting for transfers between devices: 24.7 us -> 21.5 us
  Pallas kernels: 35 us -> 36.7 us
  starting transfers between devices: 25.2 us -> 24.2 us
    ppermute x1, waiting for transfers between devices: 4.79 us -> 0.11 us  [per_device(): from_yl = lax.ppermute(region[1].astype(jnp.bfloat16), 'phr', YL)]
    ppermute x9, waiting for transfers between devices: 10.2 us -> 13.5 us  [over_img(): return lax.ppermute(a, 'img', perm)]
    ppermute x2, waiting for transfers between devices: 4.49 us -> 2.55 us  [over_z(): return lax.ppermute(a, ('img', 'phr'), Z[step])]
    ppermute x9, starting transfers between devices: 12.1 us -> 10.3 us  [over_img(): return lax.ppermute(a, 'img', perm)]
    ppermute x2, starting transfers between devices: 3.43 us -> 5.15 us  [over_z(): return lax.ppermute(a, ('img', 'phr'), Z[step])]
    pallas_call x2 -> x4, Pallas kernels: 10.1 us -> 11.7 us  [phrase_call(): call(lambda *refs: phrase_kernel(base, *refs), [SCALAR] + [WHOLE] * len(a...]
  transfers between devices with their start and end apart: 15 -> 15, of which waited for: 11 -> 10; matrix products, arithmetic and copies ran while one was open for 1% -> 2% of each run, Pallas kernels for 24% -> 29%
where the time goes in v5:
time: 86.5 us; the launch traced here: 85.7 us
  Pallas kernels  36.7 us (42%)
  starting transfers between devices  24.2 us (28%)
  waiting for transfers between devices  21.5 us (25%)
  other arithmetic  2.38 us (3%)
    ppermute x9, waiting for transfers between devices, over_img(): return lax.ppermute(a, 'img', perm)  13.5 us
    pallas_call x4, Pallas kernels, phrase_call(): call(lambda *refs: phrase_kernel(base, *refs), [SCALAR] + [WHOLE] * len(a...  11.7 us
    pallas_call x1, Pallas kernels, region_call(): call(region_kernel, [SCALAR] * 3 + [WHOLE] * len(arrays), [(shape, jnp.bf...  10.3 us
    ppermute x9, starting transfers between devices, over_img(): return lax.ppermute(a, 'img', perm)  10.3 us
    pallas_call x1, Pallas kernels, first_scores_call(): call(first_scores_kernel, [SCALAR] + [HBM] * 4, [((half, rows), jnp.bfloa...  8.72 us
    ppermute x3, starting transfers between devices, over_phr(): return lax.ppermute(a, 'phr', phr_perm(lambda y, z: (y ^ dy, z ^ dz)))  7.97 us
    pallas_call x1, Pallas kernels, scores_call(): call(scores_kernel, [WHOLE] * len(arrays), [((half, rows), jnp.float32),...  5.4 us
    ppermute x3, waiting for transfers between devices, over_phr(): return lax.ppermute(a, 'phr', phr_perm(lambda y, z: (y ^ dy, z ^ dz)))  5.26 us
  transfers between devices with their start and end apart: 15, of which 10 were waited for; matrix products, arithmetic and copies ran while one was open for 2% of the time, Pallas kernels for 29%

profile of v5, /device:TPU:0, one launch (start us, length us, event | category | flops | bytes accessed | tf_op | source)
XLA Modules:
  0.0 85.7 jit_solution(5945840287976793583)
XLA Ops:
  0.7 0.1 stack.86.refs_0_
  0.8 0.1 pad_add_fusion.refs_1_
  0.8 8.7 %first_scores.1 = (bf16[2048,1024]{1,0:T(8,128)(2,1)S(1)}, f32[8,1,1024]{2,1,0:T(1,128)S(1)}, f32[2,1024]{1,0:T(2,128)S(1)}, bf16[2048,1024]{1,0:T(8,128)(2,1)S(...) custom-call(s32[16]{0:T(128)S(1)} %stack.86.refs_0_, ...), custom_call_target="tpu_custom_call" | custom-call | flops 1 | bytes 1 | tf_op jit(solution)/shard_map/first_scores/pallas_call | solution.py:172
  9.6 0.1 collective-permute-start.3
  9.7 0.0 copy-done
  9.7 0.5 collective-permute-start.6
  10.2 5.4 %scores.1 = (f32[2048,1024]{1,0:T(8,128)S(1)}, f32[8,1,1024]{2,1,0:T(1,128)S(1)}, f32[2,1024]{1,0:T(2,128)S(1)}) custom-call(bf16[2048,1024]{1,0:T(8,128)(2,1)S(1)} %get-tuple-element.33.refs_0_.refs_5_, bf16[1024,1024]{1,0:T(8,128)(2,1)S(1)} %get-tuple-element.34.refs_1_.refs_7_, f32[2,1024]{1,0:T(2,128)S(1)} %get-tuple-element.35.refs_2_), custom_call_target="tpu_custom_call" | custom-call | flops 1 | bytes 1 | tf_op jit(solution)/shard_map/scores/pallas_call | solution.py:205
  15.6 1.7 %collective-permute-start = (f32[2,1024]{1,0:T(2,128)S(1)}, f32[2,1024]{1,0:T(2,128)S(1)}, u32[]{:S(2)}, u32[]{:S(2)}) collective-permute-start(f32[2,1024]{1,0:T(2,128)S(1)} %get-tuple-element.39), channel_id=1, source_target_pairs={{0,4},{1,5},{2,6},{3,7},{4,0},{5,1},{6,2},{7,3},{8,12},{9,13},{10,... | collective-permute-start | bytes 24584 | tf_op jit(solution)/shard_map/ppermute | solution.py:55
  17.3 2.0 %collective-permute-done = f32[2,1024]{1,0:T(2,128)S(1)} collective-permute-done((f32[2,1024]{1,0:T(2,128)S(1)}, f32[2,1024]{1,0:T(2,128)S(1)}, u32[]{:S(2)}, u32[]{:S(2)}) %collective-permute-start) | collective-permute-done | bytes 8224 | tf_op jit(solution)/shard_map/ppermute | solution.py:55
  19.4 2.1 %collective-permute-start.1 = (f32[2,1024]{1,0:T(2,128)S(1)}, f32[2,1024]{1,0:T(2,128)S(1)}, u32[]{:S(2)}, u32[]{:S(2)}) collective-permute-start(f32[2,1024]{1,0:T(2,128)S(1)} %pad_maximum_fusion), channel_id=1, source_target_pairs={{0,1},{1,0},{2,3},{3,2},{4,5},{5,4},{6,7},{7,6},{8,9},{9,8},{10,11... | collective-permute-start | bytes 24584 | tf_op jit(solution)/shard_map/ppermute | solution.py:55
  21.4 1.7 %collective-permute-done.1 = f32[2,1024]{1,0:T(2,128)S(1)} collective-permute-done((f32[2,1024]{1,0:T(2,128)S(1)}, f32[2,1024]{1,0:T(2,128)S(1)}, u32[]{:S(2)}, u32[]{:S(2)}) %collective-permute-start.1) | collective-permute-done | bytes 8224 | tf_op jit(solution)/shard_map/ppermute | solution.py:55
  23.1 4.2 %collective-permute-start.2 = (f32[2,1024]{1,0:T(2,128)S(1)}, f32[2,1024]{1,0:T(2,128)S(1)}, u32[]{:S(2)}, u32[]{:S(2)}) collective-permute-start(f32[2,1024]{1,0:T(2,128)S(1)} %pad_maximum_fusion.1), channel_id=1, source_target_pairs={{0,3},{1,2},{2,1},{3,0},{4,7},{5,6},{6,5},{7,4},{8,11},{9,10},{10,... | collective-permute-start | bytes 24584 | tf_op jit(solution)/shard_map/ppermute | solution.py:55
  27.3 1.6 %collective-permute-done.2 = f32[2,1024]{1,0:T(2,128)S(1)} collective-permute-done((f32[2,1024]{1,0:T(2,128)S(1)}, f32[2,1024]{1,0:T(2,128)S(1)}, u32[]{:S(2)}, u32[]{:S(2)}) %collective-permute-start.2) | collective-permute-done | bytes 8224 | tf_op jit(solution)/shard_map/ppermute | solution.py:55
  29.0 0.1 broadcast_select_fusion
  29.1 0.3 collective-permute-start.4
  29.4 0.5 collective-permute-start.5
  29.9 0.8 collective-permute-done.5.refs_6_
  30.7 0.0 collective-permute-done.4.refs_4_
  30.7 0.0 collective-permute-done.6.refs_8_
  30.7 0.0 collective-permute-done.3.refs_2_
  30.7 2.9 %phrase_part.4.refs_9_ = bf16[2,256,1024]{2,1,0:T(8,128)(2,1)S(1)} custom-call(s32[16]{0:T(128)S(1)} %multiply_add_fusion.3.refs_0_.refs_2_, f32[2048,1024]{1,0:T(8,128)S(1)} %get-tuple-element.36.refs_1_.refs_3_, bf16[2048,1024]{1,0:T(8,128)(2,1)S(1)} %collective-permute-done.3.refs_2_, f32[8,1,1024]{2,1,0:T(1,128)S(1)} %get-tuple-element.69.refs_3_.refs_4_, ...), custom_call_target="tpu_custom_call" | custom-call | flops 1 | bytes 1 | tf_op jit(solution)/shard_map/phrase_part/pallas_call | solution.py:236
  33.6 1.8 %collective-permute-start.8 = (bf16[2,256,1024]{2,1,0:T(8,128)(2,1)S(1)}, bf16[2,256,1024]{2,1,0:T(8,128)(2,1)S(1)}, u32[]{:S(2)}, u32[]{:S(2)}) collective-permute-start(bf16[2,256,1024]{2,1,0:T(8,128)(2,1)S(1)} %phrase_part.4.refs_9_), channel_id=1, source_target_pairs={{0,16},{8,56},{16,0},{24,40},{32,48},{40,24},{48,32},{56,8},{64,80... | collective-permute-start | bytes 3145736 | tf_op jit(solution)/shard_map/ppermute | solution.py:51
  35.5 2.9 %phrase_part.5.refs_10_.refs_1_ = f32[2,256,1024]{2,1,0:T(8,128)S(1)} custom-call(s32[16]{0:T(128)S(1)} %multiply_add_fusion.3.refs_0_.refs_2_, f32[2048,1024]{1,0:T(8,128)S(1)} %get-tuple-element.36.refs_1_.refs_3_, bf16[2048,1024]{1,0:T(8,128)(2,1)S(1)} %collective-permute-done.3.refs_2_, f32[8,1,1024]{2,1,0:T(1,128)S(1)} %get-tuple-element.69.refs_3_.refs_4_, ...), custom_call_target="tpu_custom_call" | custom-call | flops 1 | bytes 1 | tf_op jit(solution)/shard_map/phrase_part/pallas_call | solution.py:236
  38.4 10.3 %region_part.1 = (bf16[2,2,1024,128]{3,2,1,0:T(8,128)(2,1)S(1)}, f32[2,2,1024,128]{3,2,1,0:T(8,128)S(1)}) custom-call(s32[1]{0:T(128)} %bitcast.18.refs_0_, s32[4]{0:T(128)S(1)} %pad_add_fusion.refs_1_, s32[16]{0:T(128)S(1)} %multiply_add_fusion.3.refs_0_.refs_2_, f32[2048,1024]{1,0:T(8,128)S(1)} %get-tuple-element.36.refs_1_.refs_3_, ...), custom_call_target="tpu_custom_call" | custom-call | flops 1 | bytes 1 | tf_op jit(solution)/shard_map/region_part/pallas_call | solution.py:291
  48.7 0.1 collective-permute-start.7
  48.8 0.0 collective-permute-done.8.refs_0_
  48.8 0.2 add_part.3
  49.0 3.1 %collective-permute-start.9 = (bf16[256,1024]{1,0:T(8,128)(2,1)S(1)}, bf16[256,1024]{1,0:T(8,128)(2,1)S(1)}, u32[]{:S(2)}, u32[]{:S(2)}) collective-permute-start(bf16[256,1024]{1,0:T(8,128)(2,1)S(1)} %get-tuple-element.46.refs_9_), channel_id=1, source_target_pairs={{0,48},{8,24},{16,32},{24,8},{32,16},{40,56},{48,0},{56,40},{64,11... | collective-permute-start | bytes 1572872 | tf_op jit(solution)/shard_map/ppermute | solution.py:51
  52.1 2.9 %phrase_part.6.refs_9_ = bf16[2,256,1024]{2,1,0:T(8,128)(2,1)S(1)} custom-call(s32[16]{0:T(128)S(1)} %multiply_add_fusion.3.refs_0_.refs_2_, f32[2048,1024]{1,0:T(8,128)S(1)} %get-tuple-element.36.refs_1_.refs_3_, bf16[2048,1024]{1,0:T(8,128)(2,1)S(1)} %collective-permute-done.3.refs_2_, f32[8,1,1024]{2,1,0:T(1,128)S(1)} %get-tuple-element.69.refs_3_.refs_4_, ...), custom_call_target="tpu_custom_call" | custom-call | flops 1 | bytes 1 | tf_op jit(solution)/shard_map/phrase_part/pallas_call | solution.py:236
  55.0 0.3 collective-permute-start.12
  55.3 2.9 %phrase_part.7.refs_3_.refs_1_ = f32[2,256,1024]{2,1,0:T(8,128)S(1)} custom-call(s32[16]{0:T(128)S(1)} %multiply_add_fusion.3.refs_0_.refs_2_, f32[2048,1024]{1,0:T(8,128)S(1)} %get-tuple-element.36.refs_1_.refs_3_, bf16[2048,1024]{1,0:T(8,128)(2,1)S(1)} %collective-permute-done.3.refs_2_, f32[8,1,1024]{2,1,0:T(1,128)S(1)} %get-tuple-element.69.refs_3_.refs_4_, ...), custom_call_target="tpu_custom_call" | custom-call | flops 1 | bytes 1 | tf_op jit(solution)/shard_map/phrase_part/pallas_call | solution.py:236
  58.3 1.5 %collective-permute-done.9 = bf16[256,1024]{1,0:T(8,128)(2,1)S(1)} collective-permute-done((bf16[256,1024]{1,0:T(8,128)(2,1)S(1)}, bf16[256,1024]{1,0:T(8,128)(2,1)S(1)}, u32[]{:S(2)}, u32[]{:S(2)}) %collective-permute-start.9) | collective-permute-done | bytes 524320 | tf_op jit(solution)/shard_map/ppermute | solution.py:51
  59.8 0.1 add_convert_fusion.1.refs_2_
  59.9 3.2 %collective-permute-start.11 = (bf16[256,1024]{1,0:T(8,128)(2,1)S(1)}, bf16[256,1024]{1,0:T(8,128)(2,1)S(1)}, u32[]{:S(2)}, u32[]{:S(2)}) collective-permute-start(bf16[256,1024]{1,0:T(8,128)(2,1)S(1)} %add_convert_fusion.1.refs_2_), channel_id=1, source_target_pairs={{0,64},{8,72},{16,80},{24,88},{32,96},{40,104},{48,112},{56,120},{... | collective-permute-start | bytes 1572872 | tf_op jit(solution)/shard_map/ppermute | solution.py:51
  63.2 0.4 collective-permute-done.7.refs_0_
  63.6 0.2 add_part.4
  63.8 5.1 %collective-permute-start.10 = (bf16[2,1024,128]{2,1,0:T(8,128)(2,1)S(1)}, bf16[2,1024,128]{2,1,0:T(8,128)(2,1)S(1)}, u32[]{:S(2)}, u32[]{:S(2)}) collective-permute-start(bf16[2,1024,128]{2,1,0:T(8,128)(2,1)S(1)} %get-tuple-element.48), channel_id=1, source_target_pairs={{0,3},{1,2},{2,1},{3,0},{4,7},{5,6},{6,5},{7,4},{8,9},{9,8},{10,11... | collective-permute-start | bytes 1572872 | tf_op jit(solution)/shard_map/ppermute | solution.py:59
  68.8 4.3 %collective-permute-done.12.refs_0_ = bf16[2,256,1024]{2,1,0:T(8,128)(2,1)S(1)} collective-permute-done((bf16[2,256,1024]{2,1,0:T(8,128)(2,1)S(1)}, bf16[2,256,1024]{2,1,0:T(8,128)(2,1)S(1)}, u32[]{:S(2)}, u32[]{:S(2)}) %collective-permute-start.12) | collective-permute-done | bytes 1048608 | tf_op jit(solution)/shard_map/ppermute | solution.py:51
  73.1 0.2 add_part.5
  73.3 0.5 collective-permute-start.14
  73.8 0.0 collective-permute-done.11
  73.8 2.1 %collective-permute-done.10 = bf16[2,1024,128]{2,1,0:T(8,128)(2,1)S(1)} collective-permute-done((bf16[2,1024,128]{2,1,0:T(8,128)(2,1)S(1)}, bf16[2,1024,128]{2,1,0:T(8,128)(2,1)S(1)}, u32[]{:S(2)}, u32[]{:S(2)}) %collective-permute-start.10) | collective-permute-done | bytes 524320 | tf_op jit(solution)/shard_map/ppermute | solution.py:59
  76.0 0.1 convert_add_fusion
  76.1 0.8 collective-permute-start.13
  76.9 6.9 %collective-permute-done.14 = bf16[256,1024]{1,0:T(8,128)(2,1)S(1)} collective-permute-done((bf16[256,1024]{1,0:T(8,128)(2,1)S(1)}, bf16[256,1024]{1,0:T(8,128)(2,1)S(1)}, u32[]{:S(2)}, u32[]{:S(2)}) %collective-permute-start.14) | collective-permute-done | bytes 524320 | tf_op jit(solution)/shard_map/ppermute | solution.py:51
  83.8 1.0 %add_convert_fusion = bf16[256,1024]{1,0:T(8,128)(2,1)} fusion(bf16[256,1024]{1,0:T(8,128)(2,1)S(1)} %collective-permute-done.11, f32[256,1024]{1,0:T(8,128)S(1)} %get-tuple-element.51, bf16[256,1024]{1,0:T(8,128)(2,1)S(1)} %collective-permute-done.14), kind=kLoop, calls=%fused_computation | loop fusion | flops 1310720 | bytes 2621440 | tf_op jit(solution)/shard_map/convert_element_type | solution.py:359
  84.8 0.1 collective-permute-done.13
  84.9 0.8 fusion.1
  (10 shorter events, 0.2 us)
Async XLA Ops:
  0.8 8.8 %copy-start = (bf16[1024,1024]{1,0:T(8,128)(2,1)S(1)}, bf16[1024,1024]{1,0:T(8,128)(2,1)}, u32[]{:S(2)}) copy-start(bf16[1024,1024]{1,0:T(8,128)(2,1)} %refs_2_.1) | copy-start | bytes 6291460
  9.6 21.1 %collective-permute-start.3 = (bf16[2048,1024]{1,0:T(8,128)(2,1)S(1)}, bf16[2048,1024]{1,0:T(8,128)(2,1)S(1)}, u32[]{:S(2)}, u32[]{:S(2)}) collective-permute-start(bf16[2048,1024]{1,0:T(8,128)(2,1)S(1)} %get-tuple-element.40.refs_6_), channel_id=1, source_target_pairs={{0,8},{8,0},{16,24},{24,16},{32,40},{40,32},{48,56},{56,48},{64,72... | collective-permute-start | bytes 12582920 | tf_op jit(solution)/shard_map/ppermute | solution.py:51
  9.7 21.0 %collective-permute-start.6 = (bf16[1024,1024]{1,0:T(8,128)(2,1)S(1)}, bf16[1024,1024]{1,0:T(8,128)(2,1)S(1)}, u32[]{:S(2)}, u32[]{:S(2)}) collective-permute-start(bf16[1024,1024]{1,0:T(8,128)(2,1)S(1)} %copy-done), channel_id=1, source_target_pairs={{0,8},{8,0},{16,24},{24,16},{32,40},{40,32},{48,56},{56,48},{64,72... | collective-permute-start | bytes 6291464 | tf_op jit(solution)/shard_map/ppermute | solution.py:51
  15.6 3.7 %collective-permute-start = (f32[2,1024]{1,0:T(2,128)S(1)}, f32[2,1024]{1,0:T(2,128)S(1)}, u32[]{:S(2)}, u32[]{:S(2)}) collective-permute-start(f32[2,1024]{1,0:T(2,128)S(1)} %get-tuple-element.39), channel_id=1, source_target_pairs={{0,4},{1,5},{2,6},{3,7},{4,0},{5,1},{6,2},{7,3},{8,12},{9,13},{10,... | collective-permute-start | bytes 24584 | tf_op jit(solution)/shard_map/ppermute | solution.py:55
  19.4 3.7 %collective-permute-start.1 = (f32[2,1024]{1,0:T(2,128)S(1)}, f32[2,1024]{1,0:T(2,128)S(1)}, u32[]{:S(2)}, u32[]{:S(2)}) collective-permute-start(f32[2,1024]{1,0:T(2,128)S(1)} %pad_maximum_fusion), channel_id=1, source_target_pairs={{0,1},{1,0},{2,3},{3,2},{4,5},{5,4},{6,7},{7,6},{8,9},{9,8},{10,11... | collective-permute-start | bytes 24584 | tf_op jit(solution)/shard_map/ppermute | solution.py:55
  23.1 5.8 %collective-permute-start.2 = (f32[2,1024]{1,0:T(2,128)S(1)}, f32[2,1024]{1,0:T(2,128)S(1)}, u32[]{:S(2)}, u32[]{:S(2)}) collective-permute-start(f32[2,1024]{1,0:T(2,128)S(1)} %pad_maximum_fusion.1), channel_id=1, source_target_pairs={{0,3},{1,2},{2,1},{3,0},{4,7},{5,6},{6,5},{7,4},{8,11},{9,10},{10,... | collective-permute-start | bytes 24584 | tf_op jit(solution)/shard_map/ppermute | solution.py:55
  29.1 1.6 %collective-permute-start.4 = (f32[8,1,1024]{2,1,0:T(1,128)S(1)}, f32[8,1,1024]{2,1,0:T(1,128)S(1)}, u32[]{:S(2)}, u32[]{:S(2)}) collective-permute-start(f32[8,1,1024]{2,1,0:T(1,128)S(1)} %get-tuple-element.68.refs_7_), channel_id=1, source_target_pairs={{0,8},{8,0},{16,24},{24,16},{32,40},{40,32},{48,56},{56,48},{64,72... | collective-permute-start | bytes 98312 | tf_op jit(solution)/shard_map/ppermute | solution.py:51
  29.4 1.3 %collective-permute-start.5 = (s32[1,1024]{1,0:T(1,128)S(1)}, s32[1,1024]{1,0:T(1,128)S(1)}, u32[]{:S(2)}, u32[]{:S(2)}) collective-permute-start(s32[1,1024]{1,0:T(1,128)S(1)} %get-tuple-element.37.refs_5_.refs_9_), channel_id=1, source_target_pairs={{0,8},{8,0},{16,24},{24,16},{32,40},{40,32},{48,56},{56,48},{64,72... | collective-permute-start | bytes 12296 | tf_op jit(solution)/shard_map/ppermute | solution.py:51
  33.6 15.2 %collective-permute-start.8 = (bf16[2,256,1024]{2,1,0:T(8,128)(2,1)S(1)}, bf16[2,256,1024]{2,1,0:T(8,128)(2,1)S(1)}, u32[]{:S(2)}, u32[]{:S(2)}) collective-permute-start(bf16[2,256,1024]{2,1,0:T(8,128)(2,1)S(1)} %phrase_part.4.refs_9_), channel_id=1, source_target_pairs={{0,16},{8,56},{16,0},{24,40},{32,48},{40,24},{48,32},{56,8},{64,80... | collective-permute-start | bytes 3145736 | tf_op jit(solution)/shard_map/ppermute | solution.py:51
  48.7 14.9 %collective-permute-start.7 = (bf16[2,2,1024,128]{3,2,1,0:T(8,128)(2,1)S(1)}, bf16[2,2,1024,128]{3,2,1,0:T(8,128)(2,1)S(1)}, u32[]{:S(2)}, u32[]{:S(2)}) collective-permute-start(bf16[2,2,1024,128]{3,2,1,0:T(8,128)(2,1)S(1)} %get-tuple-element.43.refs_2_), channel_id=1, source_target_pairs={{0,1},{1,0},{2,3},{3,2},{4,5},{5,4},{6,7},{7,6},{8,11},{9,10},{10,... | collective-permute-start | bytes 3145736 | tf_op jit(solution)/shard_map/ppermute | solution.py:59
  49.0 10.7 %collective-permute-start.9 = (bf16[256,1024]{1,0:T(8,128)(2,1)S(1)}, bf16[256,1024]{1,0:T(8,128)(2,1)S(1)}, u32[]{:S(2)}, u32[]{:S(2)}) collective-permute-start(bf16[256,1024]{1,0:T(8,128)(2,1)S(1)} %get-tuple-element.46.refs_9_), channel_id=1, source_target_pairs={{0,48},{8,24},{16,32},{24,8},{32,16},{40,56},{48,0},{56,40},{64,11... | collective-permute-start | bytes 1572872 | tf_op jit(solution)/shard_map/ppermute | solution.py:51
  55.0 18.1 %collective-permute-start.12 = (bf16[2,256,1024]{2,1,0:T(8,128)(2,1)S(1)}, bf16[2,256,1024]{2,1,0:T(8,128)(2,1)S(1)}, u32[]{:S(2)}, u32[]{:S(2)}) collective-permute-start(bf16[2,256,1024]{2,1,0:T(8,128)(2,1)S(1)} %phrase_part.6.refs_9_), channel_id=1, source_target_pairs={{0,16},{8,56},{16,0},{24,40},{32,48},{40,24},{48,32},{56,8},{64,80... | collective-permute-start | bytes 3145736 | tf_op jit(solution)/shard_map/ppermute | solution.py:51
  59.9 13.9 %collective-permute-start.11 = (bf16[256,1024]{1,0:T(8,128)(2,1)S(1)}, bf16[256,1024]{1,0:T(8,128)(2,1)S(1)}, u32[]{:S(2)}, u32[]{:S(2)}) collective-permute-start(bf16[256,1024]{1,0:T(8,128)(2,1)S(1)} %add_convert_fusion.1.refs_2_), channel_id=1, source_target_pairs={{0,64},{8,72},{16,80},{24,88},{32,96},{40,104},{48,112},{56,120},{... | collective-permute-start | bytes 1572872 | tf_op jit(solution)/shard_map/ppermute | solution.py:51
  63.8 12.2 %collective-permute-start.10 = (bf16[2,1024,128]{2,1,0:T(8,128)(2,1)S(1)}, bf16[2,1024,128]{2,1,0:T(8,128)(2,1)S(1)}, u32[]{:S(2)}, u32[]{:S(2)}) collective-permute-start(bf16[2,1024,128]{2,1,0:T(8,128)(2,1)S(1)} %get-tuple-element.48), channel_id=1, source_target_pairs={{0,3},{1,2},{2,1},{3,0},{4,7},{5,6},{6,5},{7,4},{8,9},{9,8},{10,11... | collective-permute-start | bytes 1572872 | tf_op jit(solution)/shard_map/ppermute | solution.py:59
  73.3 10.5 %collective-permute-start.14 = (bf16[256,1024]{1,0:T(8,128)(2,1)S(1)}, bf16[256,1024]{1,0:T(8,128)(2,1)S(1)}, u32[]{:S(2)}, u32[]{:S(2)}) collective-permute-start(bf16[256,1024]{1,0:T(8,128)(2,1)S(1)} %get-tuple-element.52), channel_id=1, source_target_pairs={{0,48},{8,24},{16,32},{24,8},{32,16},{40,56},{48,0},{56,40},{64,11... | collective-permute-start | bytes 1572872 | tf_op jit(solution)/shard_map/ppermute | solution.py:51
  76.1 8.8 %collective-permute-start.13 = (bf16[1024,128]{1,0:T(8,128)(2,1)S(1)}, bf16[1024,128]{1,0:T(8,128)(2,1)S(1)}, u32[]{:S(2)}, u32[]{:S(2)}) collective-permute-start(bf16[1024,128]{1,0:T(8,128)(2,1)S(1)} %fusion.2), channel_id=1, source_target_pairs={{0,4},{1,5},{2,6},{3,7},{4,0},{5,1},{6,2},{7,3},{8,12},{9,13},{10,... | collective-permute-start | bytes 786440 | tf_op jit(solution)/shard_map/ppermute | solution.py:357

commit v6 on v5

--- a/solution.py
+++ b/solution.py
@@ -273,8 +273,8 @@
 
 def region_kernel(phr, rel, off, e, s, phrases, e_far, s_far, p_far, pos, send, keep, acc):
     tiles = s.shape[0]
-    for i in range(0, s.shape[2], BLK):
-        here = pl.ds(i, BLK)
+    for i in range(0, s.shape[2], 2 * BLK):
+        here = pl.ds(i, 2 * BLK)
         value = region_rows(here, lambda j: off[j], e, s, pos, phrases)
         value += region_rows(here, lambda j: off[tiles + j], e_far, s_far, pos, p_far)
         acc[...] = logit_scale * value
@@ -294,7 +294,7 @@
         [(shape, jnp.bfloat16), (shape, jnp.float32)],
         "region_part",
         waits=len(wait),
-        scratch_shapes=[pltpu.VMEM((BLK, dim), jnp.float32)],
+        scratch_shapes=[pltpu.VMEM((2 * BLK, dim), jnp.float32)],
     )(phr, rel, off, *[vmem(a) for a in arrays], *wait)
 
 
@@ -325,8 +325,10 @@
     e_pair = over_img(e_far, CORE)
     e_own, m_own, state = scores_call(phrases, regions, state)
 
-    for dy, dz in ((1, 0), (0, 1), (0, 3)):
+    for dy, dz in ((1, 0), (0, 1)):
         state = combine(state, over_phr(state, dy, dz))
+    state, pp = lax.optimization_barrier((state, pp))
+    state = combine(state, over_phr(state, 0, 3))
     lse = state[0] + jnp.log2(state[1])
     s_far = jnp.where(po >= 0, jnp.exp2(m_far - lse), 0.0)
     s_own = jnp.where(po >= 0, jnp.exp2(m_own - lse), 0.0)

time: 86.5 us -> 86 us (level)
  starting transfers between devices: 24.2 us -> 23.1 us
    ppermute x9, starting transfers between devices: 10.3 us -> 8.98 us  [over_img(): return lax.ppermute(a, 'img', perm)]
where the time goes in v6:
time: 86 us; the launch traced here: 85 us
  Pallas kernels  36.7 us (43%)
  starting transfers between devices  23.1 us (27%)
  waiting for transfers between devices  21.9 us (25%)
  other arithmetic  2.36 us (3%)
    ppermute x9, waiting for transfers between devices, over_img(): return lax.ppermute(a, 'img', perm)  13.4 us
    pallas_call x4, Pallas kernels, phrase_call(): call(lambda *refs: phrase_kernel(base, *refs), [SCALAR] + [WHOLE] * len(a...  11.7 us
    pallas_call x1, Pallas kernels, region_call(): call(region_kernel, [SCALAR] * 3 + [WHOLE] * len(arrays), [(shape, jnp.bf...  10.2 us
    ppermute x9, starting transfers between devices, over_img(): return lax.ppermute(a, 'img', perm)  8.98 us
    pallas_call x1, Pallas kernels, first_scores_call(): call(first_scores_kernel, [SCALAR] + [HBM] * 4, [((half, rows), jnp.bfloa...  8.72 us
    ppermute x3, starting transfers between devices, over_phr(): return lax.ppermute(a, 'phr', phr_perm(lambda y, z: (y ^ dy, z ^ dz)))  8.15 us
    pallas_call x1, Pallas kernels, scores_call(): call(scores_kernel, [WHOLE] * len(arrays), [((half, rows), jnp.float32),...  5.4 us
    ppermute x3, waiting for transfers between devices, over_phr(): return lax.ppermute(a, 'phr', phr_perm(lambda y, z: (y ^ dy, z ^ dz)))  5.25 us
  transfers between devices with their start and end apart: 15, of which 10 were waited for; matrix products, arithmetic and copies ran while one was open for 2% of the time, Pallas kernels for 29%

profile of v6, /device:TPU:0, one launch (start us, length us, event | category | flops | bytes accessed | tf_op | source)
XLA Modules:
  0.0 85.0 jit_solution(7463058312066322105)
XLA Ops:
  0.7 0.1 stack.86.refs_0_
  0.8 0.1 pad_add_fusion.refs_1_
  0.8 8.7 %first_scores.1 = (bf16[2048,1024]{1,0:T(8,128)(2,1)S(1)}, f32[8,1,1024]{2,1,0:T(1,128)S(1)}, f32[2,1024]{1,0:T(2,128)S(1)}, bf16[2048,1024]{1,0:T(8,128)(2,1)S(...) custom-call(s32[16]{0:T(128)S(1)} %stack.86.refs_0_, ...), custom_call_target="tpu_custom_call" | custom-call | flops 1 | bytes 1 | tf_op jit(solution)/shard_map/first_scores/pallas_call | solution.py:172
  9.6 0.1 collective-permute-start.4
  9.7 0.0 copy-done
  9.7 0.5 collective-permute-start.6
  10.2 5.4 %scores.1 = (f32[2048,1024]{1,0:T(8,128)S(1)}, f32[8,1,1024]{2,1,0:T(1,128)S(1)}, f32[2,1024]{1,0:T(2,128)S(1)}) custom-call(bf16[2048,1024]{1,0:T(8,128)(2,1)S(1)} %get-tuple-element.35.refs_0_.refs_5_, bf16[1024,1024]{1,0:T(8,128)(2,1)S(1)} %get-tuple-element.36.refs_1_.refs_7_, f32[2,1024]{1,0:T(2,128)S(1)} %get-tuple-element.37.refs_2_), custom_call_target="tpu_custom_call" | custom-call | flops 1 | bytes 1 | tf_op jit(solution)/shard_map/scores/pallas_call | solution.py:205
  15.6 1.7 %collective-permute-start = (f32[2,1024]{1,0:T(2,128)S(1)}, f32[2,1024]{1,0:T(2,128)S(1)}, u32[]{:S(2)}, u32[]{:S(2)}) collective-permute-start(f32[2,1024]{1,0:T(2,128)S(1)} %get-tuple-element.41), channel_id=1, source_target_pairs={{0,4},{1,5},{2,6},{3,7},{4,0},{5,1},{6,2},{7,3},{8,12},{9,13},{10,... | collective-permute-start | bytes 24584 | tf_op jit(solution)/shard_map/ppermute | solution.py:55
  17.3 0.0 collective-permute-start.2
  17.3 2.0 %collective-permute-done = f32[2,1024]{1,0:T(2,128)S(1)} collective-permute-done((f32[2,1024]{1,0:T(2,128)S(1)}, f32[2,1024]{1,0:T(2,128)S(1)}, u32[]{:S(2)}, u32[]{:S(2)}) %collective-permute-start) | collective-permute-done | bytes 8224 | tf_op jit(solution)/shard_map/ppermute | solution.py:55
  19.3 2.1 %collective-permute-start.1 = (f32[2,1024]{1,0:T(2,128)S(1)}, f32[2,1024]{1,0:T(2,128)S(1)}, u32[]{:S(2)}, u32[]{:S(2)}) collective-permute-start(f32[2,1024]{1,0:T(2,128)S(1)} %pad_maximum_fusion), channel_id=1, source_target_pairs={{0,1},{1,0},{2,3},{3,2},{4,5},{5,4},{6,7},{7,6},{8,9},{9,8},{10,11... | collective-permute-start | bytes 24584 | tf_op jit(solution)/shard_map/ppermute | solution.py:55
  21.4 1.6 %collective-permute-done.1 = f32[2,1024]{1,0:T(2,128)S(1)} collective-permute-done((f32[2,1024]{1,0:T(2,128)S(1)}, f32[2,1024]{1,0:T(2,128)S(1)}, u32[]{:S(2)}, u32[]{:S(2)}) %collective-permute-start.1) | collective-permute-done | bytes 8224 | tf_op jit(solution)/shard_map/ppermute | solution.py:55
  23.1 0.0 collective-permute-done.2.refs_6_
  23.1 4.4 %collective-permute-start.3 = (f32[2,1024]{1,0:T(2,128)S(1)}, f32[2,1024]{1,0:T(2,128)S(1)}, u32[]{:S(2)}, u32[]{:S(2)}) collective-permute-start(f32[2,1024]{1,0:T(2,128)S(1)} %pad_maximum_fusion.1), channel_id=1, source_target_pairs={{0,3},{1,2},{2,1},{3,0},{4,7},{5,6},{6,5},{7,4},{8,11},{9,10},{10,... | collective-permute-start | bytes 24584 | tf_op jit(solution)/shard_map/ppermute | solution.py:55
  27.5 1.6 %collective-permute-done.3 = f32[2,1024]{1,0:T(2,128)S(1)} collective-permute-done((f32[2,1024]{1,0:T(2,128)S(1)}, f32[2,1024]{1,0:T(2,128)S(1)}, u32[]{:S(2)}, u32[]{:S(2)}) %collective-permute-start.3) | collective-permute-done | bytes 8224 | tf_op jit(solution)/shard_map/ppermute | solution.py:55
  29.2 0.1 broadcast_select_fusion
  29.3 0.1 collective-permute-start.5
  29.4 1.2 %collective-permute-done.5.refs_4_ = f32[8,1,1024]{2,1,0:T(1,128)S(1)} collective-permute-done((f32[8,1,1024]{2,1,0:T(1,128)S(1)}, f32[8,1,1024]{2,1,0:T(1,128)S(1)}, u32[]{:S(2)}, u32[]{:S(2)}) %collective-permute-start.5) | collective-permute-done | bytes 32800 | tf_op jit(solution)/shard_map/ppermute | solution.py:51
  30.6 0.0 collective-permute-done.6.refs_8_
  30.6 0.0 collective-permute-done.4.refs_2_
  30.6 2.9 %phrase_part.4.refs_9_ = bf16[2,256,1024]{2,1,0:T(8,128)(2,1)S(1)} custom-call(s32[16]{0:T(128)S(1)} %multiply_add_fusion.1.refs_0_.refs_2_, f32[2048,1024]{1,0:T(8,128)S(1)} %get-tuple-element.38.refs_1_.refs_3_, bf16[2048,1024]{1,0:T(8,128)(2,1)S(1)} %collective-permute-done.4.refs_2_, f32[8,1,1024]{2,1,0:T(1,128)S(1)} %get-tuple-element.69.refs_3_.refs_4_, ...), custom_call_target="tpu_custom_call" | custom-call | flops 1 | bytes 1 | tf_op jit(solution)/shard_map/phrase_part/pallas_call | solution.py:236
  33.5 1.6 %collective-permute-start.8 = (bf16[2,256,1024]{2,1,0:T(8,128)(2,1)S(1)}, bf16[2,256,1024]{2,1,0:T(8,128)(2,1)S(1)}, u32[]{:S(2)}, u32[]{:S(2)}) collective-permute-start(bf16[2,256,1024]{2,1,0:T(8,128)(2,1)S(1)} %phrase_part.4.refs_9_), channel_id=1, source_target_pairs={{0,16},{8,56},{16,0},{24,40},{32,48},{40,24},{48,32},{56,8},{64,80... | collective-permute-start | bytes 3145736 | tf_op jit(solution)/shard_map/ppermute | solution.py:51
  35.1 2.9 %phrase_part.5.refs_10_.refs_1_ = f32[2,256,1024]{2,1,0:T(8,128)S(1)} custom-call(s32[16]{0:T(128)S(1)} %multiply_add_fusion.1.refs_0_.refs_2_, f32[2048,1024]{1,0:T(8,128)S(1)} %get-tuple-element.38.refs_1_.refs_3_, bf16[2048,1024]{1,0:T(8,128)(2,1)S(1)} %collective-permute-done.4.refs_2_, f32[8,1,1024]{2,1,0:T(1,128)S(1)} %get-tuple-element.69.refs_3_.refs_4_, ...), custom_call_target="tpu_custom_call" | custom-call | flops 1 | bytes 1 | tf_op jit(solution)/shard_map/phrase_part/pallas_call | solution.py:236
  38.1 10.2 %region_part.1 = (bf16[2,2,1024,128]{3,2,1,0:T(8,128)(2,1)S(1)}, f32[2,2,1024,128]{3,2,1,0:T(8,128)S(1)}) custom-call(s32[1]{0:T(128)} %bitcast.18.refs_0_, s32[4]{0:T(128)S(1)} %pad_add_fusion.refs_1_, s32[16]{0:T(128)S(1)} %multiply_add_fusion.1.refs_0_.refs_2_, f32[2048,1024]{1,0:T(8,128)S(1)} %get-tuple-element.38.refs_1_.refs_3_, ...), custom_call_target="tpu_custom_call" | custom-call | flops 1 | bytes 1 | tf_op jit(solution)/shard_map/region_part/pallas_call | solution.py:291
  48.3 0.3 collective-permute-start.7
  48.6 0.0 collective-permute-done.8.refs_0_
  48.6 0.2 add_part.3
  48.9 2.6 %collective-permute-start.9 = (bf16[256,1024]{1,0:T(8,128)(2,1)S(1)}, bf16[256,1024]{1,0:T(8,128)(2,1)S(1)}, u32[]{:S(2)}, u32[]{:S(2)}) collective-permute-start(bf16[256,1024]{1,0:T(8,128)(2,1)S(1)} %get-tuple-element.50.refs_9_), channel_id=1, source_target_pairs={{0,48},{8,24},{16,32},{24,8},{32,16},{40,56},{48,0},{56,40},{64,11... | collective-permute-start | bytes 1572872 | tf_op jit(solution)/shard_map/ppermute | solution.py:51
  51.5 2.9 %phrase_part.6.refs_9_ = bf16[2,256,1024]{2,1,0:T(8,128)(2,1)S(1)} custom-call(s32[16]{0:T(128)S(1)} %multiply_add_fusion.1.refs_0_.refs_2_, f32[2048,1024]{1,0:T(8,128)S(1)} %get-tuple-element.38.refs_1_.refs_3_, bf16[2048,1024]{1,0:T(8,128)(2,1)S(1)} %collective-permute-done.4.refs_2_, f32[8,1,1024]{2,1,0:T(1,128)S(1)} %get-tuple-element.69.refs_3_.refs_4_, ...), custom_call_target="tpu_custom_call" | custom-call | flops 1 | bytes 1 | tf_op jit(solution)/shard_map/phrase_part/pallas_call | solution.py:236
  54.4 0.3 collective-permute-start.12
  54.7 2.9 %phrase_part.7.refs_3_.refs_1_ = f32[2,256,1024]{2,1,0:T(8,128)S(1)} custom-call(s32[16]{0:T(128)S(1)} %multiply_add_fusion.1.refs_0_.refs_2_, f32[2048,1024]{1,0:T(8,128)S(1)} %get-tuple-element.38.refs_1_.refs_3_, bf16[2048,1024]{1,0:T(8,128)(2,1)S(1)} %collective-permute-done.4.refs_2_, f32[8,1,1024]{2,1,0:T(1,128)S(1)} %get-tuple-element.69.refs_3_.refs_4_, ...), custom_call_target="tpu_custom_call" | custom-call | flops 1 | bytes 1 | tf_op jit(solution)/shard_map/phrase_part/pallas_call | solution.py:236
  57.7 1.7 %collective-permute-done.9 = bf16[256,1024]{1,0:T(8,128)(2,1)S(1)} collective-permute-done((bf16[256,1024]{1,0:T(8,128)(2,1)S(1)}, bf16[256,1024]{1,0:T(8,128)(2,1)S(1)}, u32[]{:S(2)}, u32[]{:S(2)}) %collective-permute-start.9) | collective-permute-done | bytes 524320 | tf_op jit(solution)/shard_map/ppermute | solution.py:51
  59.3 0.1 add_convert_fusion.1.refs_2_
  59.5 3.2 %collective-permute-start.11 = (bf16[256,1024]{1,0:T(8,128)(2,1)S(1)}, bf16[256,1024]{1,0:T(8,128)(2,1)S(1)}, u32[]{:S(2)}, u32[]{:S(2)}) collective-permute-start(bf16[256,1024]{1,0:T(8,128)(2,1)S(1)} %add_convert_fusion.1.refs_2_), channel_id=1, source_target_pairs={{0,64},{8,72},{16,80},{24,88},{32,96},{40,104},{48,112},{56,120},{... | collective-permute-start | bytes 1572872 | tf_op jit(solution)/shard_map/ppermute | solution.py:51
  62.7 0.7 collective-permute-done.7.refs_0_
  63.4 0.2 add_part.4
  63.6 4.9 %collective-permute-start.10 = (bf16[2,1024,128]{2,1,0:T(8,128)(2,1)S(1)}, bf16[2,1024,128]{2,1,0:T(8,128)(2,1)S(1)}, u32[]{:S(2)}, u32[]{:S(2)}) collective-permute-start(bf16[2,1024,128]{2,1,0:T(8,128)(2,1)S(1)} %get-tuple-element.52), channel_id=1, source_target_pairs={{0,3},{1,2},{2,1},{3,0},{4,7},{5,6},{6,5},{7,4},{8,9},{9,8},{10,11... | collective-permute-start | bytes 1572872 | tf_op jit(solution)/shard_map/ppermute | solution.py:59
  68.5 4.0 %collective-permute-done.12.refs_0_ = bf16[2,256,1024]{2,1,0:T(8,128)(2,1)S(1)} collective-permute-done((bf16[2,256,1024]{2,1,0:T(8,128)(2,1)S(1)}, bf16[2,256,1024]{2,1,0:T(8,128)(2,1)S(1)}, u32[]{:S(2)}, u32[]{:S(2)}) %collective-permute-start.12) | collective-permute-done | bytes 1048608 | tf_op jit(solution)/shard_map/ppermute | solution.py:51
  72.4 0.2 add_part.5
  72.7 0.5 collective-permute-start.14
  73.2 0.0 collective-permute-done.11
  73.2 2.4 %collective-permute-done.10 = bf16[2,1024,128]{2,1,0:T(8,128)(2,1)S(1)} collective-permute-done((bf16[2,1024,128]{2,1,0:T(8,128)(2,1)S(1)}, bf16[2,1024,128]{2,1,0:T(8,128)(2,1)S(1)}, u32[]{:S(2)}, u32[]{:S(2)}) %collective-permute-start.10) | collective-permute-done | bytes 524320 | tf_op jit(solution)/shard_map/ppermute | solution.py:59
  75.6 0.1 convert_add_fusion
  75.8 0.8 collective-permute-start.13
  76.5 6.6 %collective-permute-done.14 = bf16[256,1024]{1,0:T(8,128)(2,1)S(1)} collective-permute-done((bf16[256,1024]{1,0:T(8,128)(2,1)S(1)}, bf16[256,1024]{1,0:T(8,128)(2,1)S(1)}, u32[]{:S(2)}, u32[]{:S(2)}) %collective-permute-start.14) | collective-permute-done | bytes 524320 | tf_op jit(solution)/shard_map/ppermute | solution.py:51
  83.2 1.0 %add_convert_fusion = bf16[256,1024]{1,0:T(8,128)(2,1)} fusion(bf16[256,1024]{1,0:T(8,128)(2,1)S(1)} %collective-permute-done.11, f32[256,1024]{1,0:T(8,128)S(1)} %get-tuple-element.55, bf16[256,1024]{1,0:T(8,128)(2,1)S(1)} %collective-permute-done.14), kind=kLoop, calls=%fused_computation | loop fusion | flops 1310720 | bytes 2621440 | tf_op jit(solution)/shard_map/convert_element_type | solution.py:361
  84.2 0.1 collective-permute-done.13
  84.3 0.8 fusion.1
  (11 shorter events, 0.2 us)
Async XLA Ops:
  0.8 8.8 %copy-start = (bf16[1024,1024]{1,0:T(8,128)(2,1)S(1)}, bf16[1024,1024]{1,0:T(8,128)(2,1)}, u32[]{:S(2)}) copy-start(bf16[1024,1024]{1,0:T(8,128)(2,1)} %refs_2_.1) | copy-start | bytes 6291460
  9.6 21.0 %collective-permute-start.4 = (bf16[2048,1024]{1,0:T(8,128)(2,1)S(1)}, bf16[2048,1024]{1,0:T(8,128)(2,1)S(1)}, u32[]{:S(2)}, u32[]{:S(2)}) collective-permute-start(bf16[2048,1024]{1,0:T(8,128)(2,1)S(1)} %get-tuple-element.43.refs_6_), channel_id=1, source_target_pairs={{0,8},{8,0},{16,24},{24,16},{32,40},{40,32},{48,56},{56,48},{64,72... | collective-permute-start | bytes 12582920 | tf_op jit(solution)/shard_map/ppermute | solution.py:51
  9.7 20.9 %collective-permute-start.6 = (bf16[1024,1024]{1,0:T(8,128)(2,1)S(1)}, bf16[1024,1024]{1,0:T(8,128)(2,1)S(1)}, u32[]{:S(2)}, u32[]{:S(2)}) collective-permute-start(bf16[1024,1024]{1,0:T(8,128)(2,1)S(1)} %copy-done), channel_id=1, source_target_pairs={{0,8},{8,0},{16,24},{24,16},{32,40},{40,32},{48,56},{56,48},{64,72... | collective-permute-start | bytes 6291464 | tf_op jit(solution)/shard_map/ppermute | solution.py:51
  15.6 3.7 %collective-permute-start = (f32[2,1024]{1,0:T(2,128)S(1)}, f32[2,1024]{1,0:T(2,128)S(1)}, u32[]{:S(2)}, u32[]{:S(2)}) collective-permute-start(f32[2,1024]{1,0:T(2,128)S(1)} %get-tuple-element.41), channel_id=1, source_target_pairs={{0,4},{1,5},{2,6},{3,7},{4,0},{5,1},{6,2},{7,3},{8,12},{9,13},{10,... | collective-permute-start | bytes 24584 | tf_op jit(solution)/shard_map/ppermute | solution.py:55
  17.3 5.8 %collective-permute-start.2 = (s32[1,1024]{1,0:T(1,128)S(1)}, s32[1,1024]{1,0:T(1,128)S(1)}, u32[]{:S(2)}, u32[]{:S(2)}) collective-permute-start(s32[1,1024]{1,0:T(1,128)S(1)} %get-tuple-element.39.refs_5_.refs_9_), channel_id=1, source_target_pairs={{0,8},{8,0},{16,24},{24,16},{32,40},{40,32},{48,56},{56,48},{64,72... | collective-permute-start | bytes 12296 | tf_op jit(solution)/shard_map/ppermute | solution.py:51
  19.3 3.7 %collective-permute-start.1 = (f32[2,1024]{1,0:T(2,128)S(1)}, f32[2,1024]{1,0:T(2,128)S(1)}, u32[]{:S(2)}, u32[]{:S(2)}) collective-permute-start(f32[2,1024]{1,0:T(2,128)S(1)} %pad_maximum_fusion), channel_id=1, source_target_pairs={{0,1},{1,0},{2,3},{3,2},{4,5},{5,4},{6,7},{7,6},{8,9},{9,8},{10,11... | collective-permute-start | bytes 24584 | tf_op jit(solution)/shard_map/ppermute | solution.py:55
  23.1 6.0 %collective-permute-start.3 = (f32[2,1024]{1,0:T(2,128)S(1)}, f32[2,1024]{1,0:T(2,128)S(1)}, u32[]{:S(2)}, u32[]{:S(2)}) collective-permute-start(f32[2,1024]{1,0:T(2,128)S(1)} %pad_maximum_fusion.1), channel_id=1, source_target_pairs={{0,3},{1,2},{2,1},{3,0},{4,7},{5,6},{6,5},{7,4},{8,11},{9,10},{10,... | collective-permute-start | bytes 24584 | tf_op jit(solution)/shard_map/ppermute | solution.py:55
  29.3 1.3 %collective-permute-start.5 = (f32[8,1,1024]{2,1,0:T(1,128)S(1)}, f32[8,1,1024]{2,1,0:T(1,128)S(1)}, u32[]{:S(2)}, u32[]{:S(2)}) collective-permute-start(f32[8,1,1024]{2,1,0:T(1,128)S(1)} %get-tuple-element.68.refs_7_), channel_id=1, source_target_pairs={{0,8},{8,0},{16,24},{24,16},{32,40},{40,32},{48,56},{56,48},{64,72... | collective-permute-start | bytes 98312 | tf_op jit(solution)/shard_map/ppermute | solution.py:51
  33.5 15.1 %collective-permute-start.8 = (bf16[2,256,1024]{2,1,0:T(8,128)(2,1)S(1)}, bf16[2,256,1024]{2,1,0:T(8,128)(2,1)S(1)}, u32[]{:S(2)}, u32[]{:S(2)}) collective-permute-start(bf16[2,256,1024]{2,1,0:T(8,128)(2,1)S(1)} %phrase_part.4.refs_9_), channel_id=1, source_target_pairs={{0,16},{8,56},{16,0},{24,40},{32,48},{40,24},{48,32},{56,8},{64,80... | collective-permute-start | bytes 3145736 | tf_op jit(solution)/shard_map/ppermute | solution.py:51
  48.3 15.1 %collective-permute-start.7 = (bf16[2,2,1024,128]{3,2,1,0:T(8,128)(2,1)S(1)}, bf16[2,2,1024,128]{3,2,1,0:T(8,128)(2,1)S(1)}, u32[]{:S(2)}, u32[]{:S(2)}) collective-permute-start(bf16[2,2,1024,128]{3,2,1,0:T(8,128)(2,1)S(1)} %get-tuple-element.47.refs_2_), channel_id=1, source_target_pairs={{0,1},{1,0},{2,3},{3,2},{4,5},{5,4},{6,7},{7,6},{8,11},{9,10},{10,... | collective-permute-start | bytes 3145736 | tf_op jit(solution)/shard_map/ppermute | solution.py:59
  48.9 10.5 %collective-permute-start.9 = (bf16[256,1024]{1,0:T(8,128)(2,1)S(1)}, bf16[256,1024]{1,0:T(8,128)(2,1)S(1)}, u32[]{:S(2)}, u32[]{:S(2)}) collective-permute-start(bf16[256,1024]{1,0:T(8,128)(2,1)S(1)} %get-tuple-element.50.refs_9_), channel_id=1, source_target_pairs={{0,48},{8,24},{16,32},{24,8},{32,16},{40,56},{48,0},{56,40},{64,11... | collective-permute-start | bytes 1572872 | tf_op jit(solution)/shard_map/ppermute | solution.py:51
  54.4 18.0 %collective-permute-start.12 = (bf16[2,256,1024]{2,1,0:T(8,128)(2,1)S(1)}, bf16[2,256,1024]{2,1,0:T(8,128)(2,1)S(1)}, u32[]{:S(2)}, u32[]{:S(2)}) collective-permute-start(bf16[2,256,1024]{2,1,0:T(8,128)(2,1)S(1)} %phrase_part.6.refs_9_), channel_id=1, source_target_pairs={{0,16},{8,56},{16,0},{24,40},{32,48},{40,24},{48,32},{56,8},{64,80... | collective-permute-start | bytes 3145736 | tf_op jit(solution)/shard_map/ppermute | solution.py:51
  59.5 13.7 %collective-permute-start.11 = (bf16[256,1024]{1,0:T(8,128)(2,1)S(1)}, bf16[256,1024]{1,0:T(8,128)(2,1)S(1)}, u32[]{:S(2)}, u32[]{:S(2)}) collective-permute-start(bf16[256,1024]{1,0:T(8,128)(2,1)S(1)} %add_convert_fusion.1.refs_2_), channel_id=1, source_target_pairs={{0,64},{8,72},{16,80},{24,88},{32,96},{40,104},{48,112},{56,120},{... | collective-permute-start | bytes 1572872 | tf_op jit(solution)/shard_map/ppermute | solution.py:51
  63.6 12.1 %collective-permute-start.10 = (bf16[2,1024,128]{2,1,0:T(8,128)(2,1)S(1)}, bf16[2,1024,128]{2,1,0:T(8,128)(2,1)S(1)}, u32[]{:S(2)}, u32[]{:S(2)}) collective-permute-start(bf16[2,1024,128]{2,1,0:T(8,128)(2,1)S(1)} %get-tuple-element.52), channel_id=1, source_target_pairs={{0,3},{1,2},{2,1},{3,0},{4,7},{5,6},{6,5},{7,4},{8,9},{9,8},{10,11... | collective-permute-start | bytes 1572872 | tf_op jit(solution)/shard_map/ppermute | solution.py:59
  72.7 10.5 %collective-permute-start.14 = (bf16[256,1024]{1,0:T(8,128)(2,1)S(1)}, bf16[256,1024]{1,0:T(8,128)(2,1)S(1)}, u32[]{:S(2)}, u32[]{:S(2)}) collective-permute-start(bf16[256,1024]{1,0:T(8,128)(2,1)S(1)} %get-tuple-element.56), channel_id=1, source_target_pairs={{0,48},{8,24},{16,32},{24,8},{32,16},{40,56},{48,0},{56,40},{64,11... | collective-permute-start | bytes 1572872 | tf_op jit(solution)/shard_map/ppermute | solution.py:51
  75.8 8.5 %collective-permute-start.13 = (bf16[1024,128]{1,0:T(8,128)(2,1)S(1)}, bf16[1024,128]{1,0:T(8,128)(2,1)S(1)}, u32[]{:S(2)}, u32[]{:S(2)}) collective-permute-start(bf16[1024,128]{1,0:T(8,128)(2,1)S(1)} %fusion.2), channel_id=1, source_target_pairs={{0,4},{1,5},{2,6},{3,7},{4,0},{5,1},{6,2},{7,3},{8,12},{9,13},{10,... | collective-permute-start | bytes 786440 | tf_op jit(solution)/shard_map/ppermute | solution.py:359
